TPU v7x, 32 devices: a whole 2x2x4 slice. The times are simulated.
32 devices in a mesh: img: 8 (over z, x), lat: 4 (over y, core).
Axes of the slice: x: 2, y: 2, z: 4, core: 2. Of those that a mesh axis runs over, the one named last changes fastest.
Arguments:
- media: bfloat16 [64, 576, 1024], P('img', 'lat'), may hold values from -6 to 6
- latents: bfloat16 [64, 64, 1024], P('img', 'lat'), may hold values from -6 to 6
- bucket: int32 [64], P('img'), may hold values from 0 to 1, as said below
- gain_media: bfloat16 [1024], P(('img', 'lat')), may hold values from 0.099609375 to 1.8984375
- shift_media: bfloat16 [1024], P(('img', 'lat')), may hold values from -3 to 3
- gain_latent: bfloat16 [1024], P(('img', 'lat')), may hold values from 0.099609375 to 1.8984375
- shift_latent: bfloat16 [1024], P(('img', 'lat')), may hold values from -3 to 3
- gain_mlp: bfloat16 [1024], P(('img', 'lat')), may hold values from 0.099609375 to 1.8984375
- shift_mlp: bfloat16 [1024], P(('img', 'lat')), may hold values from -3 to 3
- w_query: bfloat16 [1024, 512], P(('img', 'lat')), may hold values from -0.1875 to 0.1875
- w_keyvalue: bfloat16 [1024, 1024], P(('img', 'lat')), may hold values from -0.1875 to 0.1875
- w_output: bfloat16 [512, 1024], P(('img', 'lat')), may hold values from -3 to 3
- w_up: bfloat16 [1024, 4096], P(('img', 'lat')), may hold values from -0.1875 to 0.1875
- w_down: bfloat16 [4096, 1024], P(('img', 'lat')), may hold values from -0.09375 to 0.09375
- cotangent: bfloat16 [64, 64, 1024], P('img', 'lat'), may hold values from -6 to 6
Outputs:
- latents_out: bfloat16 [64, 64, 1024], P('img', 'lat')
- grad_media: float32 [64, 576, 1024], P('img', 'lat')
- grad_latents: float32 [64, 64, 1024], P('img', 'lat')
- grad_gain_media: float32 [1024], P(('img', 'lat'))
- grad_shift_media: float32 [1024], P(('img', 'lat'))
- grad_gain_latent: float32 [1024], P(('img', 'lat'))
- grad_shift_latent: float32 [1024], P(('img', 'lat'))
- grad_gain_mlp: float32 [1024], P(('img', 'lat'))
- grad_shift_mlp: float32 [1024], P(('img', 'lat'))
- grad_w_query: float32 [1024, 512], P(('img', 'lat'))
- grad_w_keyvalue: float32 [1024, 1024], P(('img', 'lat'))
- grad_w_output: float32 [512, 1024], P(('img', 'lat'))
- grad_w_up: float32 [1024, 4096], P(('img', 'lat'))
- grad_w_down: float32 [4096, 1024], P(('img', 'lat'))
Inputs may be any that keep to these rules, and one draw needn't show every extreme that they name: `bucket`: 0 marks an image of 256 patches and 1 one of 576; among the 8 images of each index of img at least one has 576 patches.
All inputs are finite; a program needn't handle non-finite values.
Results may differ from a plain program's by a relative error of at most 0.014.
Values may be sent and summed in bfloat16 or wider, within the bound.
A program may use at most 192 MiB of HBM per device.

v0:
```python
import jax
import jax.numpy as jnp
from jax import lax
from jax.sharding import PartitionSpec as P

HEADS = 8
SHORT = 256
LONG = 576


EPS = 1e-05
SCALE = 0.125
NEG = -1e30


def layer_norm(values, norm_gain, norm_shift):
    row_mean = jnp.mean(values, axis=-1, keepdims=True)
    centred = values - row_mean
    spread = jnp.mean(centred * centred, axis=-1, keepdims=True)
    return centred * lax.rsqrt(spread + EPS) * norm_gain + norm_shift


def gelu_exact(values):
    return jax.nn.gelu(values, approximate=False)


def project(values, weight):
    return jnp.einsum("gtd,de->gte", values, weight, preferred_element_type=jnp.float32)


def project_back(gradient, weight):
    return jnp.einsum("gte,de->gtd", gradient, weight, preferred_element_type=jnp.float32)


def weight_grad(values, gradient):
    return jnp.einsum("gtd,gte->de", values, gradient, preferred_element_type=jnp.float32)


def split_heads(values):
    return values.reshape(values.shape[0], values.shape[1], HEADS, values.shape[2] // HEADS)


def join_heads(values):
    return values.reshape(values.shape[0], values.shape[1], -1)


def scores_of(query_set, key_set, valid):
    raw_scores = (
        jnp.einsum(
            "gqhd,gkhd->ghqk",
            split_heads(query_set),
            split_heads(key_set),
            preferred_element_type=jnp.float32,
        )
        * SCALE
    )
    return jnp.where(valid[:, None, None, :], raw_scores, NEG)


def heads_mix(prob_low, value_set):
    mixed_heads = jnp.einsum(
        "ghqk,gkhd->gqhd", prob_low, split_heads(value_set), preferred_element_type=jnp.float32
    )
    return join_heads(mixed_heads)


def attention_back(query_set, pair_set, valid, log_total, grad_set, finish_rows):
    inner = query_set.shape[2]
    key_set = pair_set[..., :inner]
    value_set = pair_set[..., inner:]
    probs = jnp.exp(scores_of(query_set, key_set, valid) - log_total[..., None])
    grad_probs = jnp.einsum(
        "gqhd,gkhd->ghqk",
        split_heads(grad_set),
        split_heads(value_set),
        preferred_element_type=jnp.float32,
    )
    row_sum = finish_rows(jnp.sum(probs * grad_probs, axis=-1))
    grad_scores = (probs * (grad_probs - row_sum[..., None])).astype(jnp.bfloat16)
    grad_query = (
        join_heads(
            jnp.einsum(
                "ghqk,gkhd->gqhd",
                grad_scores,
                split_heads(key_set),
                preferred_element_type=jnp.float32,
            )
        )
        * SCALE
    )
    grad_keys = (
        join_heads(
            jnp.einsum(
                "ghqk,gqhd->gkhd",
                grad_scores,
                split_heads(query_set),
                preferred_element_type=jnp.float32,
            )
        )
        * SCALE
    )
    grad_values = join_heads(
        jnp.einsum(
            "ghqk,gqhd->gkhd",
            probs.astype(jnp.bfloat16),
            split_heads(grad_set),
            preferred_element_type=jnp.float32,
        )
    )
    return (grad_query, jnp.concatenate([grad_keys, grad_values], axis=-1))


def keep_rows(row_part):
    return row_part


def on_device(
    media,
    latents,
    bucket,
    gain_media,
    shift_media,
    gain_latent,
    shift_latent,
    gain_mlp,
    shift_mlp,
    w_query,
    w_keyvalue,
    w_output,
    w_up,
    w_down,
    cotangent,
):
    (
        g_media,
        s_media,
        g_latent,
        s_latent,
        g_mlp,
        s_mlp,
        query_weight,
        pair_weight,
        out_weight,
        up_weight,
        down_weight,
    ) = (
        lax.all_gather(gain_media, ("img", "lat"), axis=0, tiled=True),
        lax.all_gather(shift_media, ("img", "lat"), axis=0, tiled=True),
        lax.all_gather(gain_latent, ("img", "lat"), axis=0, tiled=True),
        lax.all_gather(shift_latent, ("img", "lat"), axis=0, tiled=True),
        lax.all_gather(gain_mlp, ("img", "lat"), axis=0, tiled=True),
        lax.all_gather(shift_mlp, ("img", "lat"), axis=0, tiled=True),
        lax.all_gather(w_query, ("img", "lat"), axis=0, tiled=True),
        lax.all_gather(w_keyvalue, ("img", "lat"), axis=0, tiled=True),
        lax.all_gather(w_output, ("img", "lat"), axis=0, tiled=True),
        lax.all_gather(w_up, ("img", "lat"), axis=0, tiled=True),
        lax.all_gather(w_down, ("img", "lat"), axis=0, tiled=True),
    )
    patch_local = media.shape[1]
    lengths = SHORT + (LONG - SHORT) * bucket
    media_norm, media_norm_back = jax.vjp(
        layer_norm,
        media.astype(jnp.float32),
        g_media.astype(jnp.float32),
        s_media.astype(jnp.float32),
    )
    media_low = media_norm.astype(jnp.bfloat16)
    latent_norm, latent_norm_back = jax.vjp(
        layer_norm,
        latents.astype(jnp.float32),
        g_latent.astype(jnp.float32),
        s_latent.astype(jnp.float32),
    )
    latent_low = latent_norm.astype(jnp.bfloat16)
    pair_media = project(media_low, pair_weight).astype(jnp.bfloat16)
    pair_latent = project(latent_low, pair_weight).astype(jnp.bfloat16)
    query_low = project(latent_low, query_weight).astype(jnp.bfloat16)
    pair_local = jnp.concatenate([pair_media, pair_latent], axis=1)
    inner = query_low.shape[2]
    pair_all = lax.all_gather(pair_local, "lat", axis=1, tiled=True)
    per_device = pair_local.shape[1]
    positions = jnp.arange(pair_all.shape[1], dtype=jnp.int32)
    owner = positions // per_device
    offset = positions % per_device
    all_valid = (offset[None, :] >= patch_local) | (
        owner[None, :] * patch_local + offset[None, :] < lengths[:, None]
    )
    all_scores = scores_of(query_low, pair_all[..., :inner], all_valid)
    log_total = jax.nn.logsumexp(all_scores, axis=-1)
    prob_low = jnp.exp(all_scores - log_total[..., None]).astype(jnp.bfloat16)
    mixed = heads_mix(prob_low, pair_all[..., inner:])
    mixed_low = mixed.astype(jnp.bfloat16)
    resid = latents.astype(jnp.float32) + project(mixed_low, out_weight)
    mlp_norm, mlp_norm_back = jax.vjp(
        layer_norm, resid, g_mlp.astype(jnp.float32), s_mlp.astype(jnp.float32)
    )
    mlp_low = mlp_norm.astype(jnp.bfloat16)
    gate = project(mlp_low, up_weight)
    active, gelu_back = jax.vjp(gelu_exact, gate)
    active_low = active.astype(jnp.bfloat16)
    latents_out = (resid + project(active_low, down_weight)).astype(jnp.bfloat16)
    grad_down = weight_grad(active_low, cotangent)
    grad_active = project_back(cotangent, down_weight)
    grad_gate = gelu_back(grad_active)[0].astype(jnp.bfloat16)
    grad_up = weight_grad(mlp_low, grad_gate)
    grad_mlp_norm = project_back(grad_gate, up_weight)
    grad_resid_norm, grad_gain_mlp, grad_shift_mlp = mlp_norm_back(grad_mlp_norm)
    grad_resid = cotangent.astype(jnp.float32) + grad_resid_norm
    grad_attn = grad_resid.astype(jnp.bfloat16)
    grad_out_weight = weight_grad(mixed_low, grad_attn)
    grad_mixed = project_back(grad_attn, out_weight).astype(jnp.bfloat16)
    grad_query, grad_pair_all = attention_back(
        query_low, pair_all, all_valid, log_total, grad_mixed, keep_rows
    )
    grad_pair = lax.psum_scatter(
        grad_pair_all.astype(jnp.bfloat16), "lat", scatter_dimension=1, tiled=True
    )
    grad_query_low = grad_query.astype(jnp.bfloat16)
    grad_pair_media = grad_pair[:, :patch_local]
    grad_pair_latent = grad_pair[:, patch_local:]
    grad_pair_weight = weight_grad(media_low, grad_pair_media) + weight_grad(
        latent_low, grad_pair_latent
    )
    grad_query_weight = weight_grad(latent_low, grad_query_low)
    grad_media_norm = project_back(grad_pair_media, pair_weight)
    grad_latent_norm = project_back(grad_pair_latent, pair_weight) + project_back(
        grad_query_low, query_weight
    )
    grad_media, grad_gain_media, grad_shift_media = media_norm_back(grad_media_norm)
    grad_latent_in, grad_gain_latent, grad_shift_latent = latent_norm_back(grad_latent_norm)
    grad_latents = grad_resid + grad_latent_in
    summed = (
        lax.psum_scatter(grad_gain_media, ("img", "lat"), scatter_dimension=0, tiled=True),
        lax.psum_scatter(grad_shift_media, ("img", "lat"), scatter_dimension=0, tiled=True),
        lax.psum_scatter(grad_gain_latent, ("img", "lat"), scatter_dimension=0, tiled=True),
        lax.psum_scatter(grad_shift_latent, ("img", "lat"), scatter_dimension=0, tiled=True),
        lax.psum_scatter(grad_gain_mlp, ("img", "lat"), scatter_dimension=0, tiled=True),
        lax.psum_scatter(grad_shift_mlp, ("img", "lat"), scatter_dimension=0, tiled=True),
        lax.psum_scatter(grad_query_weight, ("img", "lat"), scatter_dimension=0, tiled=True),
        lax.psum_scatter(grad_pair_weight, ("img", "lat"), scatter_dimension=0, tiled=True),
        lax.psum_scatter(grad_out_weight, ("img", "lat"), scatter_dimension=0, tiled=True),
        lax.psum_scatter(grad_up, ("img", "lat"), scatter_dimension=0, tiled=True),
        lax.psum_scatter(grad_down, ("img", "lat"), scatter_dimension=0, tiled=True),
    )
    return (
        latents_out,
        grad_media,
        grad_latents,
        summed[0],
        summed[1],
        summed[2],
        summed[3],
        summed[4],
        summed[5],
        summed[6],
        summed[7],
        summed[8],
        summed[9],
        summed[10],
    )


def solution(mesh):
    return jax.shard_map(
        on_device,
        mesh=mesh,
        in_specs=(
            P("img", "lat", None),
            P("img", "lat", None),
            P("img"),
            P(("img", "lat")),
            P(("img", "lat")),
            P(("img", "lat")),
            P(("img", "lat")),
            P(("img", "lat")),
            P(("img", "lat")),
            P(("img", "lat"), None),
            P(("img", "lat"), None),
            P(("img", "lat"), None),
            P(("img", "lat"), None),
            P(("img", "lat"), None),
            P("img", "lat", None),
        ),
        out_specs=(
            P("img", "lat", None),
            P("img", "lat", None),
            P("img", "lat", None),
            P(("img", "lat")),
            P(("img", "lat")),
            P(("img", "lat")),
            P(("img", "lat")),
            P(("img", "lat")),
            P(("img", "lat")),
            P(("img", "lat"), None),
            P(("img", "lat"), None),
            P(("img", "lat"), None),
            P(("img", "lat"), None),
            P(("img", "lat"), None),
        ),
        check_vma=False,
    )
```

profile of v0, /device:TPU:0, one launch (start us, length us, event | category | flops | bytes accessed | tf_op | source)
XLA Modules:
  0.0 1348.7 jit_solution(15849844047199043418)
XLA Ops:
  11.0 2.1 convert_reduce_fusion
  14.6 42.3 %all-reduce.13 = (bf16[1024]{0:T(1024)(128)(2,1)S(1)}, bf16[1024]{0:T(1024)(128)(2,1)S(1)}, bf16[1024]{0:T(1024)(128)(2,1)S(1)}, bf16[1024]{0:T(1024)(128)(2,1)S...) all-reduce(bf16[1024]{0:T(1024)(128)(2,1)S(1)} %dynamic-update-slic, ...), channel_id=1, replica_groups=mesh['img'=8,'lat'=4] {'img','lat'}, use_global_device_ids=true, to_apply=%add.3 | all-reduce | flops 6144 | bytes 24576
  58.4 11.7 all-gather.7.cloned.1.call-done
  70.1 2.2 fusion.53
  72.4 3.0 fusion.39
  75.4 1.8 pad_maximum_fusion.1
  79.7 46.0 %all-gather.11.cloned.1.call-done = bf16[1024,512]{1,0:T(8,128)(2,1)} async-done(((bf16[32,512]{1,0:T(8,128)(2,1)}), bf16[1024,512]{1,0:T(8,128)(2,1)}) %all-gather.11.cloned.1.call-update) | async-done | bytes 1048592 | tf_op jit(solution)/shard_map/all_gather | solution.py:153
  125.7 1.6 convolution_convert_fusion.3
  127.5 69.4 %all-gather.9.cloned.1.call-done = bf16[8,640,1024]{2,1,0:T(8,128)(2,1)} async-done(((bf16[8,160,1024]{2,1,0:T(8,128)(2,1)}), bf16[8,640,1024]{2,1,0:T(8,128)(2,1)}) %all-gather.9.cloned.1.call-update) | async-done | bytes 10485776 | tf_op jit(solution)/shard_map/all_gather | solution.py:180
  196.9 8.9 fusion.109
  205.8 7.8 copy.49
  213.6 7.8 copy.50
  221.4 3.7 fusion.38
  225.9 1.8 fusion.56
  228.7 24.7 %all-gather.13.cloned.1.call-done = bf16[512,1024]{1,0:T(8,128)(2,1)} async-done(((bf16[16,1024]{1,0:T(8,128)(2,1)}), bf16[512,1024]{1,0:T(8,128)(2,1)}) %all-gather.13.cloned.1.call-update) | async-done | bytes 1048592 | tf_op jit(solution)/shard_map/all_gather | solution.py:155
  253.5 1.7 fusion.110
  255.4 77.2 %all-gather.15.cloned.1.call-done = bf16[1024,4096]{1,0:T(8,128)(2,1)} async-done(((bf16[32,4096]{1,0:T(8,128)(2,1)}), bf16[1024,4096]{1,0:T(8,128)(2,1)}) %all-gather.15.cloned.1.call-update) | async-done | bytes 8388624 | tf_op jit(solution)/shard_map/all_gather | solution.py:156
  332.6 7.3 fusion.74
  339.9 71.6 %all-gather.17.cloned.1.call-done = bf16[4096,1024]{1,0:T(8,128)(2,1)} async-done(((bf16[128,1024]{1,0:T(8,128)(2,1)}), bf16[4096,1024]{1,0:T(8,128)(2,1)}) %all-gather.17.cloned.1.call-update) | async-done | bytes 8388624 | tf_op jit(solution)/shard_map/all_gather | solution.py:157
  411.5 10.6 add_convert_fusion
  422.2 3.6 multiply_reduce_fusion.1
  428.8 1.8 reshape.232
  430.7 5.0 convolution_convert_fusion
  435.6 5.2 multiply_reduce_fusion
  440.8 7.8 copy.57
  448.6 2.6 multiply_convert_fusion.1
  451.2 3.9 multiply_convert_fusion
  455.1 7.9 copy.56
  463.0 10.0 pad_maximum_fusion
  474.3 4.2 fusion.57
  478.8 1.9 convolution_bitcast_fusion.3
  481.7 2.9 convolution_bitcast_fusion.2
  485.0 72.1 %reduce-scatter.7.cloned.1.call-done = bf16[8,160,1024]{2,1,0:T(8,128)(2,1)} async-done(((bf16[8,640,1024]{2,1,0:T(8,128)(2,1)}), bf16[8,160,1024]{2,1,0:T(8,128)(2,1)}) %reduce-scatter.7.cloned.1.call-update) | async-done | bytes 2621456 | tf_op jit(solution)/shard_map/reduce_scatter | solution.py:215
  557.1 4.9 fusion.35
  562.0 3.7 bitcast_add_fusion
  566.4 9.4 convolution_bitcast_fusion.1
  576.8 11.4 convolution_bitcast_fusion
  588.2 10.5 fusion.49
  602.2 3.2 fusion.106
  605.5 2.4 fusion.16
  607.9 39.9 %all-reduce.12 = (f32[1024]{0:T(1024)S(1)}, f32[1024]{0:T(1024)S(1)}, f32[1024]{0:T(1024)S(1)}, f32[1024]{0:T(1024)S(1)}, f32[1024]{0:T(1024)S(1)}, /*index=5*/f32[1024]{0:T(1024)S(1)}) all-reduce(f32[1024]{0:T(1024)S(1)} %get-tuple-element.14, ...), channel_id=3, replica_groups=mesh['img'=8,'lat'=4] {'img','lat'}, use_global_device_ids=true, to_apply=%region_17.18.clone | all-reduce | flops 6144 | bytes 49152
  651.3 2.1 add_add_fusion.3
  653.4 4.6 broadcast_add_fusion
  658.1 38.7 %reduce-scatter.9.cloned.1.call-done = f32[32,512]{1,0:T(8,128)} async-done(((f32[1024,512]{1,0:T(8,128)}), f32[32,512]{1,0:T(8,128)}) %reduce-scatter.9.cloned.1.call-update) | async-done | bytes 65552 | tf_op jit(solution)/shard_map/reduce_scatter | solution.py:239
  696.8 135.6 %reduce-scatter.13.cloned.1.call-done = f32[16,1024]{1,0:T(8,128)} async-done(((f32[512,1024]{1,0:T(8,128)}), f32[16,1024]{1,0:T(8,128)}) %reduce-scatter.13.cloned.1.call-update) | async-done | bytes 65552 | tf_op jit(solution)/shard_map/reduce_scatter | solution.py:241
  832.4 139.9 %reduce-scatter.11.cloned.1.call-done = f32[32,1024]{1,0:T(8,128)} async-done(((f32[1024,1024]{1,0:T(8,128)}), f32[32,1024]{1,0:T(8,128)}) %reduce-scatter.11.cloned.1.call-update) | async-done | bytes 131088 | tf_op jit(solution)/shard_map/reduce_scatter | solution.py:240
  972.3 181.8 %reduce-scatter.15.cloned.1.call-done = f32[32,4096]{1,0:T(8,128)} async-done(((f32[1024,4096]{1,0:T(8,128)}), f32[32,4096]{1,0:T(8,128)}) %reduce-scatter.15.cloned.1.call-update) | async-done | bytes 524304 | tf_op jit(solution)/shard_map/reduce_scatter | solution.py:242
  1154.1 187.3 %reduce-scatter.17.cloned.1.call-done = f32[128,1024]{1,0:T(8,128)} async-done(((f32[4096,1024]{1,0:T(8,128)}), f32[128,1024]{1,0:T(8,128)}) %reduce-scatter.17.cloned.1.call-update) | async-done | bytes 524304 | tf_op jit(solution)/shard_map/reduce_scatter | solution.py:243
  (217 shorter events, 25.6 us)
Async XLA Ops:
  7.2 49.8 %copy-start = (bf16[8,144,1024]{2,1,0:T(8,128)(2,1)S(1)}, bf16[8,144,1024]{2,1,0:T(8,128)(2,1)}, u32[]{:S(2)}) copy-start(bf16[8,144,1024]{2,1,0:T(8,128)(2,1)} %param.15) | copy-start | bytes 7077892
  7.2 6.0 copy-start.57
  7.2 6.2 copy-start.58
  7.2 6.5 copy-start.59
  7.2 6.7 copy-start.60
  7.2 6.9 copy-start.61
  7.2 7.1 copy-start.62
  7.3 62.9 %all-gather.7.cloned.1.call-start = ((), (), s32[]{:S(2)}) async-start(), calls=%async_computation.6 | async-start | bytes 2162688 | tf_op jit(solution)/shard_map/all_gather | solution.py:154
  8.0 117.7 %all-gather.11.cloned.1.call-start = ((), (), s32[]{:S(2)}) async-start(), calls=%async_computation.8 | async-start | bytes 1081344 | tf_op jit(solution)/shard_map/all_gather | solution.py:153
  8.7 188.2 %all-gather.9.cloned.1.call-start = ((), (), s32[]{:S(2)}) async-start(), calls=%async_computation.7 | async-start | bytes 13107200 | tf_op jit(solution)/shard_map/all_gather | solution.py:180
  11.0 45.9 %copy-start.44 = (f32[8,16]{1,0:T(8,128)}, f32[8,16]{1,0:T(8,128)S(1)}, u32[]{:S(2)}) copy-start(f32[8,16]{1,0:T(8,128)S(1)} %fusion.71) | copy-start | bytes 1540
  11.0 59.1 %copy-start.6 = (bf16[8,16,1024]{2,1,0:T(8,128)(2,1)S(1)}, bf16[8,16,1024]{2,1,0:T(8,128)(2,1)}, u32[]{:S(2)}) copy-start(bf16[8,16,1024]{2,1,0:T(8,128)(2,1)} %param.16) | copy-start | bytes 786436
  13.2 112.5 %copy-start.29 = (f32[8,16]{1,0:T(8,128)}, f32[8,16]{1,0:T(8,128)S(1)}, u32[]{:S(2)}) copy-start(f32[8,16]{1,0:T(8,128)S(1)} %fusion.96) | copy-start | bytes 1540
  56.9 68.8 %copy-start.50 = (f32[1024]{0:T(1024)}, f32[1024]{0:T(1024)S(1)}, u32[]{:S(2)}) copy-start(f32[1024]{0:T(1024)S(1)} %convert_element_type.94) | copy-start | bytes 12292
  56.9 15.4 %copy-start.53 = (f32[1024]{0:T(1024)}, f32[1024]{0:T(1024)S(1)}, u32[]{:S(2)}) copy-start(f32[1024]{0:T(1024)S(1)} %convert_element_type.90) | copy-start | bytes 12292
  57.0 15.4 %copy-start.34 = (f32[1024]{0:T(1024)}, f32[1024]{0:T(1024)S(1)}, u32[]{:S(2)}) copy-start(f32[1024]{0:T(1024)S(1)} %convert_element_type.89) | copy-start | bytes 12292
  58.4 17.0 %copy-start.24 = (f32[8,144]{1,0:T(8,128)}, f32[8,144]{1,0:T(8,128)S(1)}, u32[]{:S(2)}) copy-start(f32[8,144]{1,0:T(8,128)S(1)} %fusion.87) | copy-start | bytes 13828
  77.3 176.2 %all-gather.13.cloned.1.call-start = ((), (), s32[]{:S(2)}) async-start(), calls=%async_computation.9 | async-start | bytes 1081344 | tf_op jit(solution)/shard_map/all_gather | solution.py:155
  77.9 254.8 %all-gather.15.cloned.1.call-start = ((), (), s32[]{:S(2)}) async-start(), calls=%async_computation.10 | async-start | bytes 8650752 | tf_op jit(solution)/shard_map/all_gather | solution.py:156
  78.4 333.1 %all-gather.17.cloned.1.call-start = ((), (), s32[]{:S(2)}) async-start(), calls=%async_computation.11 | async-start | bytes 8650752 | tf_op jit(solution)/shard_map/all_gather | solution.py:157
  79.0 478.0 %reduce-scatter.7.cloned.1.call-start = ((), (), s32[]{:S(2)}) async-start(), calls=%async_computation.12 | async-start | bytes 13107200 | tf_op jit(solution)/shard_map/reduce_scatter | solution.py:215
  79.5 253.1 %copy-start.55 = (f32[1024]{0:T(1024)}, f32[1024]{0:T(1024)S(1)}, u32[]{:S(2)}) copy-start(f32[1024]{0:T(1024)S(1)} %convert_element_type.103) | copy-start | bytes 12292
  79.6 346.2 %copy-start.40 = (f32[1024]{0:T(1024)}, f32[1024]{0:T(1024)S(1)}, u32[]{:S(2)}) copy-start(f32[1024]{0:T(1024)S(1)} %convert_element_type.102) | copy-start | bytes 12292
  127.5 94.0 %copy-start.11 = (bf16[8,16,8,64]{3,2,1,0:T(8,128)(2,1)}, bf16[8,16,8,64]{3,2,1,0:T(8,128)(2,1)S(1)}, u32[]{:S(2)}) copy-start(bf16[8,16,8,64]{3,2,1,0:T(8,128)(2,1)S(1)} %reshape.230) | copy-start | bytes 393220
  255.2 170.6 %copy-start.27 = (f32[8,16]{1,0:T(8,128)}, f32[8,16]{1,0:T(8,128)S(1)}, u32[]{:S(2)}) copy-start(f32[8,16]{1,0:T(8,128)S(1)} %broadcast_multiply_fusion.1) | copy-start | bytes 1540
  255.4 170.4 %copy-start.42 = (f32[8,16]{1,0:T(8,128)}, f32[8,16]{1,0:T(8,128)S(1)}, u32[]{:S(2)}) copy-start(f32[8,16]{1,0:T(8,128)S(1)} %fusion.97) | copy-start | bytes 1540
  339.9 82.2 %copy-start.64 = (u8[16,4096]{1,0:T(8,128)(4,1)}, u8[16,4096]{1,0:T(8,128)(4,1)S(1)}, u32[]{:S(2)}) copy-start(u8[16,4096]{1,0:T(8,128)(4,1)S(1)} %get-tuple-element.18) | copy-start | bytes 196612
  411.5 10.6 copy-start.3
  430.7 5.0 copy-start.13
  473.0 5.8 copy-start.30
  473.0 5.8 copy-start.51
  473.0 223.8 %reduce-scatter.9.cloned.1.call-start = ((), (), s32[]{:S(2)}) async-start(), calls=%async_computation.13 | async-start | bytes 2162688 | tf_op jit(solution)/shard_map/reduce_scatter | solution.py:239
  480.8 351.6 %reduce-scatter.13.cloned.1.call-start = ((), (), s32[]{:S(2)}) async-start(), calls=%async_computation.15 | async-start | bytes 2162688 | tf_op jit(solution)/shard_map/reduce_scatter | solution.py:241
  481.7 75.3 %copy-start.1 = (bf16[8,144,1024]{2,1,0:T(8,128)(2,1)S(1)}, bf16[8,144,1024]{2,1,0:T(8,128)(2,1)}, u32[]{:S(2)}) copy-start(bf16[8,144,1024]{2,1,0:T(8,128)(2,1)} %param.15) | copy-start | bytes 7077892
  484.7 72.4 %copy-start.25 = (f32[8,144]{1,0:T(8,128)S(1)}, f32[8,144]{1,0:T(8,128)}, u32[]{:S(2)}) copy-start(f32[8,144]{1,0:T(8,128)} %copy-done.24) | copy-start | bytes 13828
  484.7 72.4 %copy-start.35 = (f32[1024]{0:T(1024)S(1)}, f32[1024]{0:T(1024)}, u32[]{:S(2)}) copy-start(f32[1024]{0:T(1024)} %copy-done.34) | copy-start | bytes 12292
  484.7 72.4 %copy-start.54 = (f32[1024]{0:T(1024)S(1)}, f32[1024]{0:T(1024)}, u32[]{:S(2)}) copy-start(f32[1024]{0:T(1024)} %copy-done.53) | copy-start | bytes 12292
  484.7 77.3 %copy-start.31 = (f32[8,16]{1,0:T(8,128)S(1)}, f32[8,16]{1,0:T(8,128)}, u32[]{:S(2)}) copy-start(f32[8,16]{1,0:T(8,128)} %copy-done.29) | copy-start | bytes 1540
  484.7 77.3 %copy-start.52 = (f32[1024]{0:T(1024)S(1)}, f32[1024]{0:T(1024)}, u32[]{:S(2)}) copy-start(f32[1024]{0:T(1024)} %copy-done.50) | copy-start | bytes 12292
  484.7 487.6 %reduce-scatter.11.cloned.1.call-start = ((), (), s32[]{:S(2)}) async-start(), calls=%async_computation.14 | async-start | bytes 4325376 | tf_op jit(solution)/shard_map/reduce_scatter | solution.py:240
  565.8 588.3 %reduce-scatter.15.cloned.1.call-start = ((), (), s32[]{:S(2)}) async-start(), calls=%async_computation.16 | async-start | bytes 17301504 | tf_op jit(solution)/shard_map/reduce_scatter | solution.py:242
  575.9 765.5 %reduce-scatter.17.cloned.1.call-start = ((), (), s32[]{:S(2)}) async-start(), calls=%async_computation.17 | async-start | bytes 17301504 | tf_op jit(solution)/shard_map/reduce_scatter | solution.py:243
  588.2 10.5 copy-start.15
  588.2 10.5 copy-start.46
  605.5 45.8 %copy-start.8 = (f32[8,16,1024]{2,1,0:T(8,128)S(1)}, f32[8,16,1024]{2,1,0:T(8,128)}, u32[]{:S(2)}) copy-start(f32[8,16,1024]{2,1,0:T(8,128)} %copy-done.7) | copy-start | bytes 1572868
  605.5 45.8 %copy-start.33 = (f32[8,16]{1,0:T(8,128)S(1)}, f32[8,16]{1,0:T(8,128)}, u32[]{:S(2)}) copy-start(f32[8,16]{1,0:T(8,128)} %copy-done.29) | copy-start | bytes 1540
  605.5 45.8 %copy-start.39 = (f32[8,16]{1,0:T(8,128)S(1)}, f32[8,16]{1,0:T(8,128)}, u32[]{:S(2)}) copy-start(f32[8,16]{1,0:T(8,128)} %copy-done.38) | copy-start | bytes 1540
  607.9 45.5 %copy-start.37 = (f32[1024]{0:T(1024)S(1)}, f32[1024]{0:T(1024)}, u32[]{:S(2)}) copy-start(f32[1024]{0:T(1024)} %copy-done.34) | copy-start | bytes 12292
  (31 other events, 69.0 us)
Sparse Core Ops, SparseCore 0:
  10.9 59.1 all-gather.6
  73.0 52.6 all-gather.10
  127.8 69.0 all-gather.8
  199.6 53.7 all-gather.12
  256.2 76.4 all-gather.14
  335.4 76.1 all-gather.16
  473.1 83.8 reduce-scatter.6
  559.9 136.8 reduce-scatter.8
  699.7 132.5 reduce-scatter.12
  835.1 137.2 reduce-scatter.10
  975.2 178.8 reduce-scatter.14
  1156.8 184.5 reduce-scatter.16
where the time goes:
time: 1360 us; the launch traced here: 1350 us
  waiting for transfers between devices  1060 us (78%)
  matrix products  105 us (8%)
  blocking collectives  82.2 us (6%)
  local copies, waits for them, and re-layouts  55.4 us (4%)
  other arithmetic  30.5 us (2%)
  between operations  15.5 us (1%)
    reduce_scatter x1, waiting for transfers between devices, on_device(): lax.psum_scatter(grad_down, ('img', 'lat'), scatter_dimension=0, tiled=True)  187 us
    reduce_scatter x1, waiting for transfers between devices, on_device(): lax.psum_scatter(grad_up, ('img', 'lat'), scatter_dimension=0, tiled=True)  182 us
    reduce_scatter x1, waiting for transfers between devices, on_device(): lax.psum_scatter(grad_pair_weight, ('img', 'lat'), scatter_dimension=0, t...  140 us
    reduce_scatter x1, waiting for transfers between devices, on_device(): lax.psum_scatter(grad_out_weight, ('img', 'lat'), scatter_dimension=0, ti...  136 us
    unnamed x2, blocking collectives  82.2 us
    all_gather x1, waiting for transfers between devices, on_device(): lax.all_gather(w_up, ('img', 'lat'), axis=0, tiled=True)  77.2 us
    reduce_scatter x1, waiting for transfers between devices, on_device(): lax.psum_scatter(grad_pair_all.astype(jnp.bfloat16), 'lat', scatter_dimen...  72.1 us
    all_gather x1, waiting for transfers between devices, on_device(): lax.all_gather(w_down, ('img', 'lat'), axis=0, tiled=True)  71.6 us
  transfers between devices with their start and end apart: 12, of which 12 were waited for; matrix products, arithmetic and copies ran while one was open for 9% of the time, Pallas kernels for 0%

commit v1 on v0

v1 whole, which is shorter than its diff:
```python
import jax
import jax.numpy as jnp
from jax import lax
from jax.experimental import pallas as pl
from jax.experimental.pallas import tpu as pltpu
from jax.sharding import PartitionSpec as P

MESH = pl.DeviceIdType.MESH
BF16 = jnp.bfloat16
F32 = jnp.float32

SHORT = 256
LONG = 576
HEADS = 8
EPS = 1e-05
SCALE = 0.125
NEG = -1e30

BLOCK = 8

KV = (0, 1024)
QU = (1024, 512)
GN = (1536, 128)
OUT = (1664, 512)
WIDE = 2176
URGENT = 1664


def mm(a, b):
    return lax.dot_general(a, b, (((1,), (0,)), ((), ())), preferred_element_type=F32)


def mm_nt(a, b):
    return lax.dot_general(a, b, (((1,), (1,)), ((), ())), preferred_element_type=F32)


def mm_tn(a, b):
    return lax.dot_general(a, b, (((0,), (0,)), ((), ())), preferred_element_type=F32)


def cols(span):
    return pl.ds(span[0], span[1])


def flat(values):
    return values.reshape(-1, values.shape[-1])


def normal(values):
    mean = jnp.mean(values, axis=-1, keepdims=True)
    centred = values - mean
    spread = jnp.mean(centred * centred, axis=-1, keepdims=True)
    return mean, lax.rsqrt(spread + EPS)


def norm_back(upstream, normed, rstd, gain):
    scaled = upstream * gain
    first = jnp.mean(scaled, axis=-1, keepdims=True)
    second = jnp.mean(scaled * normed, axis=-1, keepdims=True)
    return (scaled - first - normed * second) * rstd


class Place:
    def __init__(self):
        img = lax.axis_index("img")
        lat = lax.axis_index("lat")
        self.i = lax.rem(img, BLOCK)
        self.base = img - self.i
        self.z = lax.div(self.i, 2)
        self.x = lax.rem(self.i, 2)
        self.l = lat
        self.y = lax.div(lat, 2)
        self.c = lax.rem(lat, 2)
        self.z1 = self.z + 1 - 2 * lax.rem(self.z, 2)
        self.z2 = lax.rem(self.z + 2, 4)
        self.z3 = 3 - self.z
        self.mid = jnp.logical_or(self.z == 1, self.z == 2)
        self.end = jnp.logical_or(self.z == 0, self.z == 3)
        self.p = self.x * 2 + self.y
        self.q = self.z * 4 + self.p
        self.px = (1 - self.x) * 2 + self.y
        self.py = self.x * 2 + 1 - self.y
        self.pd = 3 - self.p
        self.lc = self.y * 2 + 1 - self.c
        self.ly = (1 - self.y) * 2 + self.c
        self.ld = 3 - self.l
        self.core = self.dev(self.z, self.x, self.y, 1 - self.c)
        self.xn = self.dev(self.z, 1 - self.x, self.y, self.c)
        self.yn = self.dev(self.z, self.x, 1 - self.y, self.c)
        self.diag = self.dev(self.z, 1 - self.x, 1 - self.y, self.c)
        self.ycore = self.dev(self.z, self.x, 1 - self.y, 1 - self.c)
        self.zn1 = self.dev(self.z1, self.x, self.y, self.c)
        self.zn2 = self.dev(self.z2, self.x, self.y, self.c)
        self.zn3 = self.dev(self.z3, self.x, self.y, self.c)

    def dev(self, z, x, y, c):
        return (self.base + z * 2 + x, y * 2 + c)

    def greet(self):
        barrier = pltpu.get_barrier_semaphore()
        peers = (self.core, self.xn, self.yn, self.diag, self.ycore, self.zn1, self.zn2, self.zn3)
        for peer in peers:
            pl.semaphore_signal(barrier, inc=1, device_id=peer, device_id_type=MESH)
        pl.semaphore_wait(barrier, len(peers))


def guarded(when, action):
    if when is None:
        action()
    else:
        pl.when(when)(action)


class Msg:
    def __init__(self, post, src, dst, dev, into, key=None, when=None):
        self.k = post.count
        post.count += 1
        self.key = self.k if key is None else key
        self.when = when
        self.post, self.src, self.dst, self.dev, self.into = post, src, dst, dev, into
        post.all.append(self)

    def copy(self, src, dst):
        return pltpu.make_async_remote_copy(
            src_ref=src,
            dst_ref=dst,
            send_sem=self.post.send.at[self.k],
            recv_sem=self.post.recv.at[self.key],
            device_id=self.dev,
            device_id_type=MESH,
        )

    def start(self):
        guarded(self.when, lambda: self.copy(self.src, self.dst).start())

    def arrived(self):
        self.copy(self.into, self.into).wait_recv()

    def sent(self):
        guarded(self.when, lambda: self.copy(self.src, self.dst).wait_send())


class Post:
    def __init__(self, send, recv):
        self.send = send
        self.recv = recv
        self.count = 0
        self.all = []

    def msg(self, *a, **k):
        return Msg(self, *a, **k)

    def drain(self):
        for m in self.all:
            m.sent()


class ZGather:
    def __init__(self, post, at, view):
        own = view(at.z)
        self.m1 = post.msg(own, own, at.zn1, view(at.z1))
        self.m2 = post.msg(own, own, at.zn2, view(at.z2))
        self.m3 = post.msg(own, own, at.zn3, view(at.z3), when=at.mid)
        self.relay = post.msg(view(at.z2), view(at.z2), at.zn1, view(at.z3), key=self.m3.k, when=at.mid)

    def start(self):
        self.m1.start()
        self.m2.start()
        self.m3.start()

    def near(self):
        self.m1.arrived()

    def far(self):
        self.m2.arrived()
        self.relay.start()

    def last(self):
        self.m3.arrived()


class PlaneGather:
    def __init__(self, post, at, view, half):
        own = view(at.x, at.y)
        ox, oy = 1 - at.x, 1 - at.y
        self.mx = post.msg(own, own, at.xn, view(ox, at.y))
        self.my = post.msg(own, own, at.yn, view(at.x, oy))
        self.hy = post.msg(half(ox, at.y, 0), half(ox, at.y, 0), at.yn, half(ox, oy, 0))
        self.hx = post.msg(half(at.x, oy, 1), half(at.x, oy, 1), at.xn, half(ox, oy, 1))

    def start(self):
        self.mx.start()
        self.my.start()

    def relay(self):
        self.mx.arrived()
        self.hy.start()
        self.my.arrived()
        self.hx.start()

    def last(self):
        self.hy.arrived()
        self.hx.arrived()


class LatGather:
    def __init__(self, post, at, view):
        self.mc = post.msg(view(at.l), view(at.l), at.core, view(at.lc))
        self.my = post.msg(view(at.l), view(at.l), at.yn, view(at.ly))
        self.fc = post.msg(view(at.ly), view(at.ly), at.core, view(at.ld))

    def start(self):
        self.my.start()
        self.mc.start()

    def relay(self):
        self.my.arrived()
        self.fc.start()

    def last(self):
        self.mc.arrived()
        self.fc.arrived()


class LatReduce:
    def __init__(self, post, at, parts, first, second):
        self.at, self.parts, self.first, self.second = at, parts, first, second
        self.m0 = post.msg(parts.at[at.lc], first.at[0], at.core, first.at[0])
        self.m1 = post.msg(parts.at[at.ld], first.at[1], at.core, first.at[1])
        self.m2 = post.msg(parts.at[at.ly], second, at.yn, second)

    def start(self):
        self.m1.start()
        self.m0.start()

    def relay(self):
        self.m1.arrived()
        ly = self.at.ly
        self.parts[ly] = (self.parts[ly].astype(F32) + self.first[1].astype(F32)).astype(BF16)
        self.m2.start()

    def total(self):
        self.m0.arrived()
        self.m2.arrived()
        near = self.parts[self.at.l].astype(F32) + self.first[0].astype(F32)
        return near + self.second[...].astype(F32)


class PlaneReduce:
    def __init__(self, post, at, part, by, bx, b2):
        x, y = at.x, at.y
        ox, oy = 1 - x, 1 - y
        self.part, self.by, self.bx, self.b2 = part, by, bx, b2
        self.x, self.y, self.ox, self.oy = x, y, ox, oy
        self.my1 = post.msg(part(ox, oy, 0), by.at[1], at.yn, by.at[1])
        self.mx1 = post.msg(part(ox, oy, 1), bx.at[1], at.xn, bx.at[1])
        self.my0 = post.msg(part(x, oy, 0), by.at[0], at.yn, by.at[0])
        self.mx0 = post.msg(part(ox, y, 1), bx.at[0], at.xn, bx.at[0])
        self.f0 = post.msg(part(ox, y, 0), b2.at[0], at.xn, b2.at[0])
        self.f1 = post.msg(part(x, oy, 1), b2.at[1], at.yn, b2.at[1])

    def start(self):
        self.my1.start()
        self.mx1.start()
        self.my0.start()
        self.mx0.start()

    def relay(self):
        self.my1.arrived()
        there = self.part(self.ox, self.y, 0)
        there[...] = (there[...].astype(F32) + self.by[1].astype(F32)).astype(BF16)
        self.f0.start()
        self.mx1.arrived()
        there = self.part(self.x, self.oy, 1)
        there[...] = (there[...].astype(F32) + self.bx[1].astype(F32)).astype(BF16)
        self.f1.start()

    def total(self):
        self.my0.arrived()
        self.f0.arrived()
        low = self.part(self.x, self.y, 0)[...].astype(F32) + self.by[0].astype(F32) + self.b2[0].astype(F32)
        self.mx0.arrived()
        self.f1.arrived()
        high = self.part(self.x, self.y, 1)[...].astype(F32) + self.bx[0].astype(F32) + self.b2[1].astype(F32)
        return low, high


class ZReduce:
    def __init__(self, post, at, term, bufs):
        self.at, self.term, self.bufs = at, term, bufs
        self.m1 = post.msg(term(at.z1), bufs.at[0], at.zn1, bufs.at[0])
        self.m2 = post.msg(term(at.z2), bufs.at[1], at.zn2, bufs.at[1])
        self.m3 = post.msg(term(at.z3), bufs.at[2], at.zn3, bufs.at[2], when=at.mid)
        self.rel = post.msg(term(at.z3), bufs.at[3], at.zn1, bufs.at[3], when=at.end)

    def start(self):
        self.rel.start()
        pl.when(self.at.end)(self.m2.start)
        self.m1.start()
        self.m3.start()

    def relay(self):
        @pl.when(self.at.mid)
        def _():
            self.rel.arrived()
            there = self.term(self.at.z2)
            there[...] = (there[...].astype(F32) + self.bufs[3].astype(F32)).astype(BF16)
            self.m2.start()

    def total(self, out, shape=None):
        self.m1.arrived()
        self.m2.arrived()
        value = self.term(self.at.z)[...].astype(F32) + self.bufs[0].astype(F32) + self.bufs[1].astype(F32)
        out[...] = value

        @pl.when(self.at.mid)
        def _():
            self.m3.arrived()
            out[...] += self.bufs[2].astype(F32)


def head_mask():
    rows = lax.div(lax.broadcasted_iota(jnp.int32, (256, 256), 0), 64)
    lanes = lax.div(lax.broadcasted_iota(jnp.int32, (256, 256), 1), 64)
    return (rows == lanes).astype(F32).astype(BF16)


def spread_heads(part, mask):
    rows = part.reshape(64, 256)
    return jnp.concatenate([rows, rows, rows, rows], axis=0) * mask


def gather_heads(wide):
    lane = lax.div(lax.broadcasted_iota(jnp.int32, (64, 256), 1), 64)
    out = jnp.where(lane == 0, wide[0:64], 0.0)
    for h in range(1, 4):
        out = out + jnp.where(lane == h, wide[64 * h : 64 * h + 64], 0.0)
    return out


def forward(at, post, R):
    images, per_media, _ = R.media.shape
    per_lat = R.latents.shape[1]
    rows = per_media + per_lat
    tokens = images * per_lat

    R.G[at.q, at.c] = R.wpack[...]
    R.UD[at.z, at.c] = R.w_down[...]
    for p in range(4):
        for zz in range(4):
            for cc in range(2):
                R.WS[p, :, 128 * (2 * zz + cc) : 128 * (2 * zz + cc) + 128] = R.w_up[
                    :, 128 * (8 * zz + 2 * p + cc) : 128 * (8 * zz + 2 * p + cc) + 128
                ]
    R.UU[at.q, at.c] = R.WS[at.p]
    R.CA[at.p] = R.cotangent[...].reshape(tokens, 1024)

    at.greet()

    near = pl.ds(0, URGENT)

    def g_view(zz, x, y):
        return R.G.at[zz * 4 + x * 2 + y, at.c, :, near]

    def g_half(zz, x, y, h):
        return R.G.at[zz * 4 + x * 2 + y, at.c, pl.ds(16 * h, 16), near]

    zs = (at.z, at.z1, at.z2, at.z3)
    a_z = ZGather(post, at, lambda zz: g_view(zz, at.x, at.y))
    a_xy = [
        PlaneGather(
            post, at, lambda x, y, zz=zz: g_view(zz, x, y), lambda x, y, h, zz=zz: g_half(zz, x, y, h)
        )
        for zz in zs
    ]
    a_c = [
        post.msg(
            R.G.at[pl.ds(4 * zz, 4), at.c, :, near],
            R.G.at[pl.ds(4 * zz, 4), at.c, :, near],
            at.core,
            R.G.at[pl.ds(4 * zz, 4), 1 - at.c, :, near],
        )
        for zz in zs
    ]
    a_z.start()
    a_xy[0].start()
    up = [
        post.msg(R.WS.at[there], R.UU.at[at.q, at.c], dev, R.UU.at[at.z * 4 + there, at.c])
        for there, dev in ((at.px, at.xn), (at.py, at.yn), (at.pd, at.diag))
    ]
    for m in up:
        m.start()

    def stats(g, carry):
        mean, rstd = normal(R.media[g].astype(F32))
        R.MR[g, 0:per_media, 0:1] = mean
        R.MR[g, 0:per_media, 1:2] = rstd
        mean, rstd = normal(R.latents[g].astype(F32))
        R.MR[g, per_media:rows, 0:1] = mean
        R.MR[g, per_media:rows, 1:2] = rstd
        return carry

    lax.fori_loop(0, images, stats, 0)

    a_z.near()
    a_xy[1].start()
    a_z.far()
    a_xy[2].start()
    a_z.last()
    a_xy[3].start()

    far = pl.ds(URGENT, WIDE - URGENT)

    def b_view(zz, x, y):
        return R.G.at[zz * 4 + x * 2 + y, at.c, :, far]

    def b_half(zz, x, y, h):
        return R.G.at[zz * 4 + x * 2 + y, at.c, pl.ds(16 * h, 16), far]

    b_z = ZGather(post, at, lambda zz: b_view(zz, at.x, at.y))
    b_xy = [
        PlaneGather(
            post, at, lambda x, y, zz=zz: b_view(zz, x, y), lambda x, y, h, zz=zz: b_half(zz, x, y, h)
        )
        for zz in zs
    ]
    b_c = [
        post.msg(
            R.G.at[pl.ds(4 * zz, 4), at.c, :, far],
            R.G.at[pl.ds(4 * zz, 4), at.c, :, far],
            at.core,
            R.G.at[pl.ds(4 * zz, 4), 1 - at.c, :, far],
        )
        for zz in zs
    ]
    d_z = ZGather(post, at, lambda zz: R.UD.at[zz, at.c])
    u_z = ZGather(post, at, lambda zz: R.UU.at[pl.ds(4 * zz, 4), at.c])
    d_c = [post.msg(R.UD.at[zz, at.c], R.UD.at[zz, at.c], at.core, R.UD.at[zz, 1 - at.c]) for zz in zs]
    u_c = [
        post.msg(
            R.UU.at[pl.ds(4 * zz, 4), at.c],
            R.UU.at[pl.ds(4 * zz, 4), at.c],
            at.core,
            R.UU.at[pl.ds(4 * zz, 4), 1 - at.c],
        )
        for zz in zs
    ]
    b_z.start()
    d_z.start()
    d_c[0].start()
    for m in up:
        m.arrived()
    u_z.start()
    u_c[0].start()

    for g in a_xy:
        g.relay()
    for g, m in zip(a_xy, a_c):
        g.last()
        m.start()
    b_xy[0].start()
    b_z.near()
    b_xy[1].start()
    b_z.far()
    b_xy[2].start()
    b_z.last()
    b_xy[3].start()
    cot = PlaneGather(
        post,
        at,
        lambda x, y: R.CA.at[x * 2 + y],
        lambda x, y, h: R.CA.at[x * 2 + y, pl.ds(h * (tokens // 2), tokens // 2)],
    )
    cot.start()
    for m in a_c:
        m.arrived()

    for i in range(8):
        total = jnp.zeros((16, 128), F32)
        for q in (2 * i, 2 * i + 1):
            for c in range(2):
                total = total + R.G[q, c, 0:16, GN[0] : GN[0] + GN[1]].astype(F32)
        R.VV[:, 128 * i : 128 * i + 128] = total

    def low(g, carry):
        normed = (R.media[g].astype(F32) - R.MR[g, 0:per_media, 0:1]) * R.MR[g, 0:per_media, 1:2]
        R.X[g, 0:per_media, :] = (normed * R.VV[0:1, :] + R.VV[1:2, :]).astype(BF16)
        normed = (R.latents[g].astype(F32) - R.MR[g, per_media:rows, 0:1]) * R.MR[g, per_media:rows, 1:2]
        R.X[g, per_media:rows, :] = (normed * R.VV[2:3, :] + R.VV[3:4, :]).astype(BF16)
        return carry

    lax.fori_loop(0, images, low, 0)

    latent_low = flat(R.X[:, per_media:rows, :])
    R.QA[at.l] = mm(latent_low, R.G[:, :, :, QU[0] : QU[0] + QU[1]].reshape(1024, 512)).astype(BF16)
    q_all = LatGather(post, at, lambda l: R.QA.at[l])
    q_all.start()

    def pairs(n, carry):
        weight = R.G[:, :, :, pl.ds(pl.multiple_of(n * 256, 256), 256)].reshape(1024, 256)
        made = mm(R.X[...].reshape(images * rows, 1024), weight).astype(BF16)
        R.PR[:, :, pl.ds(pl.multiple_of(n * 256, 256), 256)] = made.reshape(images, rows, 256)
        return carry

    lax.fori_loop(0, 4, pairs, 0)
    q_all.relay()
    d_z.near()
    d_c[1].start()
    u_z.near()
    u_c[1].start()
    d_z.far()
    u_z.far()
    cot.relay()
    for g in b_xy:
        g.relay()
    q_all.last()

    mask = head_mask()

    def score(g, carry):
        limit = SHORT + (LONG - SHORT) * R.bucket[g] - at.l * per_media
        row = lax.broadcasted_iota(jnp.int32, (rows, 256), 0)
        valid = jnp.logical_or(row >= per_media, row < limit)
        for half in range(2):
            span = pl.ds(256 * half, 256)
            queries = spread_heads(R.QA[:, pl.ds(pl.multiple_of(g * per_lat, per_lat), per_lat), span], mask)
            raw = mm_nt(R.PR[g, :, span], queries) * SCALE
            raw = jnp.where(valid, raw, NEG)
            top = jnp.max(raw, axis=0, keepdims=True)
            total = jnp.sum(jnp.exp(raw - top), axis=0, keepdims=True)
            R.S[2 * g + half] = raw
            R.LS[at.l, pl.ds(2 * g + half, 1), :] = top + jnp.log(total)
        return carry

    lax.fori_loop(0, images, score, 0)
    ls = [
        post.msg(R.LS.at[at.l], R.LS.at[at.l], dev, R.LS.at[there])
        for there, dev in ((at.ly, at.yn), (at.ld, at.ycore), (at.lc, at.core))
    ]
    for m in ls:
        m.start()
    for g, m in zip(b_xy, b_c):
        g.last()
        m.start()
    for m in ls:
        m.arrived()
    top = jnp.maximum(jnp.maximum(R.LS[0], R.LS[1]), jnp.maximum(R.LS[2], R.LS[3]))
    total = jnp.exp(R.LS[0] - top)
    for l in range(1, 4):
        total = total + jnp.exp(R.LS[l] - top)
    R.LG[...] = top + jnp.log(total)

    def mix(g, carry):
        for half in range(2):
            probs = jnp.exp(R.S[2 * g + half] - R.LG[pl.ds(2 * g + half, 1), :])
            R.S[2 * g + half] = probs
            wide = mm_tn(probs.astype(BF16), R.PR[g, :, pl.ds(512 + 256 * half, 256)])
            R.OP[:, pl.ds(pl.multiple_of(g * per_lat, per_lat), per_lat), pl.ds(256 * half, 256)] = (
                gather_heads(wide).reshape(4, per_lat, 256).astype(BF16)
            )
        return carry

    lax.fori_loop(0, images, mix, 0)
    mixed = LatReduce(post, at, R.OP, R.O1, R.O2)
    mixed.start()
    mixed.relay()
    d_z.last()
    u_z.last()
    for m in d_c[2:] + u_c[2:]:
        m.start()
    for m in b_c:
        m.arrived()
    R.MX[...] = mixed.total().astype(BF16)
    left = R.G[:, :, 0:16, OUT[0] : OUT[0] + OUT[1]].reshape(512, 512)
    right = R.G[:, :, 16:32, OUT[0] : OUT[0] + OUT[1]].reshape(512, 512)
    latents = R.latents[...].reshape(tokens, 1024).astype(F32)
    R.RES[:, 0:512] = latents[:, 0:512] + mm(R.MX[...], left)
    R.RES[:, 512:1024] = latents[:, 512:1024] + mm(R.MX[...], right)
    mean, rstd = normal(R.RES[...])
    R.MA[at.p] = ((R.RES[...] - mean) * rstd * R.VV[4:5, :] + R.VV[5:6, :]).astype(BF16)
    mlp = PlaneGather(
        post,
        at,
        lambda x, y: R.MA.at[x * 2 + y],
        lambda x, y, h: R.MA.at[x * 2 + y, pl.ds(h * (tokens // 2), tokens // 2)],
    )
    mlp.start()
    mlp.relay()
    cot.last()
    for m in d_c + u_c:
        m.arrived()
    mlp.last()


def backward(at, post, R):
    images, per_media, _ = R.media.shape
    per_lat = R.latents.shape[1]
    rows = per_media + per_lat
    tokens = images * per_lat
    half_rows = tokens // 2
    zs = (at.z, at.z1, at.z2, at.z3)
    at.greet()

    def gates(f, carry):
        span = pl.ds(pl.multiple_of(f * 256, 256), 256)
        gate = mm(R.MA[...].reshape(4 * tokens, 1024), R.UU[:, :, :, span].reshape(1024, 256))
        back = mm_nt(R.CA[...].reshape(4 * tokens, 1024), R.UD[f].reshape(256, 1024))
        phi = 0.5 * (1.0 + lax.erf(gate * 0.7071067811865476))
        R.ACT[:, :, span] = (gate * phi).astype(BF16).reshape(4, tokens, 256)
        slope = phi + gate * jnp.exp(-0.5 * gate * gate) * 0.3989422804014327
        R.GG[:, :, span] = (back * slope).astype(BF16).reshape(4, tokens, 256)
        return carry

    lax.fori_loop(0, 4, gates, 0)

    def norm_parts(n, carry):
        weight = R.UU[pl.ds(n * 4, 4)].reshape(256, 1024)
        made = mm_nt(R.GG[...].reshape(4 * tokens, 1024), weight)
        R.PT[:, :, pl.ds(pl.multiple_of(n * 256, 256), 256)] = made.astype(BF16).reshape(4, tokens, 256)
        return carry

    lax.fori_loop(0, 4, norm_parts, 0)
    back = PlaneReduce(
        post,
        at,
        lambda x, y, h: R.PT.at[x * 2 + y, pl.ds(h * half_rows, half_rows)],
        R.PY.at[0],
        R.PX.at[0],
        R.P2.at[0],
    )
    back.start()

    back.relay()

    def down_grads(f, carry):
        span = pl.ds(pl.multiple_of(f * 256, 256), 256)
        act = R.ACT[:, :, span].reshape(4 * tokens, 256)
        R.gD[f] = mm_tn(act, R.CA[...].reshape(4 * tokens, 1024)).astype(BF16).reshape(2, 128, 1024)
        return carry

    lax.fori_loop(0, 4, down_grads, 0)
    d_c = post.msg(R.gD.at[:, 1 - at.c], R.RD, at.core, R.RD)
    d_c.start()

    low, high = back.total()
    R.U[0:half_rows] = low
    R.U[half_rows:] = high

    mean, rstd = normal(R.RES[...])
    normed = (R.RES[...] - mean) * rstd
    upstream = R.U[...]
    cot = R.cotangent[...].reshape(tokens, 1024).astype(F32)
    R.GR[...] = cot + norm_back(upstream, normed, rstd, R.VV[4:5, :])
    R.GS[...] = jnp.zeros_like(R.GS)
    R.GS[4:5, :] = jnp.sum(upstream * normed, axis=0, keepdims=True)
    R.GS[5:6, :] = jnp.sum(upstream, axis=0, keepdims=True)
    grad_attn = R.GR[...].astype(BF16)
    left = R.G[:, :, 0:16, OUT[0] : OUT[0] + OUT[1]].reshape(512, 512)
    right = R.G[:, :, 16:32, OUT[0] : OUT[0] + OUT[1]].reshape(512, 512)
    R.GM[at.l] = (mm_nt(grad_attn[:, 0:512], left) + mm_nt(grad_attn[:, 512:1024], right)).astype(BF16)
    gm = LatGather(post, at, lambda l: R.GM.at[l])
    gm.start()
    R.gA[:, :, 0:16, OUT[0] : OUT[0] + OUT[1]] = (
        mm_tn(R.MX[...], grad_attn[:, 0:512]).astype(BF16).reshape(16, 2, 16, 512)
    )
    R.gA[:, :, 16:32, OUT[0] : OUT[0] + OUT[1]] = (
        mm_tn(R.MX[...], grad_attn[:, 512:1024]).astype(BF16).reshape(16, 2, 16, 512)
    )
    gm.relay()

    def up_grads(n, carry):
        span = pl.ds(pl.multiple_of(n * 256, 256), 256)
        low_rows = R.MA[:, :, span].reshape(4 * tokens, 256)
        made = mm_tn(low_rows, R.GG[...].reshape(4 * tokens, 1024)).astype(BF16)
        R.gU[pl.ds(n * 4, 4)] = made.reshape(4, 2, 32, 1024)
        return carry

    lax.fori_loop(0, 4, up_grads, 0)
    u_c = post.msg(R.gU.at[:, 1 - at.c], R.RU, at.core, R.RU)
    u_c.start()

    def out_parts(n, carry):
        span = pl.ds(pl.multiple_of(n * 256, 256), 256)
        made = mm(R.ACT[...].reshape(4 * tokens, 1024), R.UD[:, :, :, span].reshape(1024, 256))
        R.GG[:, :, span] = made.astype(BF16).reshape(4, tokens, 256)
        return carry

    lax.fori_loop(0, 4, out_parts, 0)
    d_c.arrived()

    def add_d(zz, carry):
        R.RD[zz] = (R.RD[zz].astype(F32) + R.gD[zz, at.c].astype(F32)).astype(BF16)
        return carry

    lax.fori_loop(0, 4, add_d, 0)
    d_z = ZReduce(post, at, lambda zz: R.RD.at[zz], R.ZD)
    d_z.start()
    out = PlaneReduce(
        post,
        at,
        lambda x, y, h: R.GG.at[x * 2 + y, pl.ds(h * half_rows, half_rows)],
        R.PY.at[1],
        R.PX.at[1],
        R.P2.at[1],
    )
    out.start()
    gm.last()

    mask = head_mask()

    def grad_probs(g, carry):
        lat_rows = pl.ds(pl.multiple_of(g * per_lat, per_lat), per_lat)
        for half in range(2):
            upper = pl.ds(512 + 256 * half, 256)
            wide = spread_heads(R.GM[:, lat_rows, pl.ds(256 * half, 256)], mask)
            made = mm_nt(R.PR[g, :, upper], wide)
            probs = R.S[2 * g + half]
            R.GP[2 * g + half] = made
            R.DL[at.l, pl.ds(2 * g + half, 1), :] = jnp.sum(probs * made, axis=0, keepdims=True)
            R.gP[g, :, upper] = mm(probs.astype(BF16), wide).astype(BF16)
        return carry

    lax.fori_loop(0, images, grad_probs, 0)
    dl = [
        post.msg(R.DL.at[at.l], R.DL.at[at.l], dev, R.DL.at[there])
        for there, dev in ((at.ly, at.yn), (at.ld, at.ycore), (at.lc, at.core))
    ]
    for m in dl:
        m.start()
    u_c.arrived()

    def add_u(zz, carry):
        span = pl.ds(zz * 4, 4)
        R.RU[span] = (R.RU[span].astype(F32) + R.gU[span, at.c].astype(F32)).astype(BF16)
        return carry

    lax.fori_loop(0, 4, add_u, 0)
    u_z = ZReduce(post, at, lambda zz: R.RU.at[pl.ds(zz * 4, 4)], R.ZU)
    u_z.start()
    out.relay()
    for m in dl:
        m.arrived()
    R.LG2[...] = R.DL[0] + R.DL[1] + R.DL[2] + R.DL[3]

    def grad_scores(g, carry):
        lat_rows = pl.ds(pl.multiple_of(g * per_lat, per_lat), per_lat)
        for half in range(2):
            span = pl.ds(256 * half, 256)
            grads = R.S[2 * g + half] * (R.GP[2 * g + half] - R.LG2[pl.ds(2 * g + half, 1), :])
            grads = grads.astype(BF16)
            wide = mm_tn(grads, R.PR[g, :, span]) * SCALE
            R.QP[:, lat_rows, span] = gather_heads(wide).reshape(4, per_lat, 256).astype(BF16)
            queries = spread_heads(R.QA[:, lat_rows, span], mask)
            R.gP[g, :, span] = (mm(grads, queries) * SCALE).astype(BF16)
        return carry

    lax.fori_loop(0, images, grad_scores, 0)
    gq = LatReduce(post, at, R.QP, R.Q1, R.Q2)
    gq.start()
    d_z.relay()
    u_z.relay()

    def kv_grads(n, carry):
        low_rows = R.X[:, :, pl.ds(pl.multiple_of(n * 256, 256), 256)].reshape(images * rows, 256)
        made = mm_tn(low_rows, R.gP[...].reshape(images * rows, 1024)).astype(BF16)
        R.gA[pl.ds(n * 4, 4), :, :, 0:1024] = made.reshape(4, 2, 32, 1024)
        return carry

    lax.fori_loop(0, 4, kv_grads, 0)
    gq.relay()

    def media_copy(h):
        return pltpu.make_async_copy(R.MG, R.grad_media.at[pl.ds(h * 2, 2)], R.local.at[0])

    def media_grads(h, carry):
        span = pl.ds(h * 2, 2)
        weight = R.G[:, :, :, 0:1024].reshape(1024, 1024)
        upstream = mm_nt(R.gP[span].reshape(2 * rows, 1024), weight).reshape(2, rows, 1024)
        R.U[pl.ds(h * 2 * per_lat, 2 * per_lat)] = upstream[:, per_media:rows, :].reshape(2 * per_lat, 1024)
        upstream = upstream[:, 0:per_media, :]
        rstd = R.MR[span, 0:per_media, 1:2]
        normed = (R.media[span].astype(F32) - R.MR[span, 0:per_media, 0:1]) * rstd
        made = norm_back(upstream, normed, rstd, R.VV[0:1, :])
        pl.when(h >= 1)(lambda: media_copy(h - 1).wait())
        R.MG[...] = made
        media_copy(h).start()
        R.GS[0:1, :] += jnp.sum(flat(upstream * normed), axis=0, keepdims=True)
        R.GS[1:2, :] += jnp.sum(flat(upstream), axis=0, keepdims=True)
        return carry

    lax.fori_loop(0, images // 2, media_grads, 0)
    media_copy(images // 2 - 1).wait()

    grad_query = gq.total().astype(BF16)
    latent_low = flat(R.X[:, per_media:rows, :])
    weight = R.G[:, :, :, QU[0] : QU[0] + QU[1]].reshape(1024, 512)
    upstream = R.U[...] + mm_nt(grad_query, weight)
    rstd = flat(R.MR[:, per_media:rows, 1:2])
    normed = (flat(R.latents[...]).astype(F32) - flat(R.MR[:, per_media:rows, 0:1])) * rstd
    R.grad_latents[...] = (R.GR[...] + norm_back(upstream, normed, rstd, R.VV[2:3, :])).reshape(
        images, per_lat, 1024
    )
    R.GS[2:3, :] = jnp.sum(upstream * normed, axis=0, keepdims=True)
    R.GS[3:4, :] = jnp.sum(upstream, axis=0, keepdims=True)
    R.gA[:, :, :, QU[0] : QU[0] + QU[1]] = (
        mm_tn(latent_low, grad_query).astype(BF16).reshape(16, 2, 32, 512)
    )
    for i in range(8):
        piece = R.GS[:, 128 * i : 128 * i + 128].astype(BF16)
        for q in (2 * i, 2 * i + 1):
            for c in range(2):
                R.gA[q, c, 0:16, GN[0] : GN[0] + GN[1]] = piece
                R.gA[q, c, 16:32, GN[0] : GN[0] + GN[1]] = jnp.zeros((16, 128), BF16)

    w_c = [
        post.msg(R.gA.at[pl.ds(4 * zz, 4), 1 - at.c], R.RA.at[pl.ds(4 * zz, 4)], at.core, R.RA.at[pl.ds(4 * zz, 4)])
        for zz in zs
    ]
    for m in w_c[::-1]:
        m.start()
    w_xy = []
    for k in (3, 2, 1, 0):
        span = pl.ds(4 * zs[k], 4)
        w_c[k].arrived()
        R.RA[span] = (R.RA[span].astype(F32) + R.gA[span, at.c].astype(F32)).astype(BF16)
        w_xy.append(
            PlaneReduce(
                post,
                at,
                lambda x, y, h, zz=zs[k]: R.RA.at[zz * 4 + x * 2 + y, pl.ds(16 * h, 16)],
                R.WY.at[k],
                R.WX.at[k],
                R.W2.at[k],
            )
        )
        w_xy[-1].start()
    low, high = out.total()
    R.latents_out[...] = jnp.concatenate([R.RES[0:half_rows] + low, R.RES[half_rows:] + high], axis=0).astype(
        BF16
    ).reshape(images, per_lat, 1024)
    d_z.total(R.grad_down)
    u_z.total(R.SF)
    R.SU[...] = R.SF[...].astype(BF16)
    R.AU[at.p] = R.SU[at.p]
    up = [
        post.msg(R.SU.at[there], R.AU.at[at.p], dev, R.AU.at[there])
        for there, dev in ((at.px, at.xn), (at.py, at.yn), (at.pd, at.diag))
    ]
    for g in w_xy:
        g.relay()
    for m in up:
        m.start()
    for k, g in zip((3, 2, 1, 0), w_xy):
        low, high = g.total()
        R.RA[zs[k] * 4 + at.p, 0:16, :] = low.astype(BF16)
        R.RA[zs[k] * 4 + at.p, 16:32, :] = high.astype(BF16)
    w_z = ZReduce(post, at, lambda zz: R.RA.at[zz * 4 + at.p], R.ZW)
    w_z.start()
    w_z.relay()
    for m in up:
        m.arrived()
    for p in range(4):
        for zz in range(4):
            for cc in range(2):
                R.grad_up[:, 128 * (8 * zz + 2 * p + cc) : 128 * (8 * zz + 2 * p + cc) + 128] = R.AU[
                    p, :, 128 * (2 * zz + cc) : 128 * (2 * zz + cc) + 128
                ].astype(F32)
    w_z.total(R.grad_pack)


class Refs:
    def __init__(self, names, refs):
        for name, ref in zip(names, refs):
            setattr(self, name, ref)


def build(kernel_body, inputs, outputs, scratch, messages, cid, name):
    in_names = [n for n, _ in inputs]
    out_names = [n for n, _, _ in outputs]
    scratch_names = [n for n, _, _ in scratch]

    def kernel(*refs):
        R = Refs(in_names + out_names + scratch_names, refs)
        at = Place()
        R.local = refs[-3]
        post = Post(refs[-2], refs[-1])
        kernel_body(at, post, R)
        post.drain()
        assert post.count == messages, post.count

    specs = [
        pl.BlockSpec(memory_space=pltpu.SMEM if n == "bucket" else pltpu.VMEM) for n in in_names
    ]
    return pl.pallas_call(
        kernel,
        out_shape=[jax.ShapeDtypeStruct(s, d) for _, s, d in outputs],
        in_specs=specs,
        out_specs=[
            pl.BlockSpec(memory_space=pl.ANY if n == "grad_media" else pltpu.VMEM) for n, _, _ in outputs
        ],
        scratch_shapes=[pltpu.VMEM(s, d) for _, s, d in scratch]
        + [pltpu.SemaphoreType.DMA((2,)), pltpu.SemaphoreType.DMA((messages,)), pltpu.SemaphoreType.DMA((messages,))],
        compiler_params=pltpu.CompilerParams(
            collective_id=cid, has_side_effects=True, vmem_limit_bytes=62 << 20
        ),
        name=name,
    )(*[v for _, v in inputs])


def layer(media, latents, bucket, cotangent, wpack, w_up, w_down):
    images, per_media, _ = media.shape
    per_lat = latents.shape[1]
    rows = per_media + per_lat
    tokens = images * per_lat
    inputs = [
        ("media", media),
        ("latents", latents),
        ("cotangent", cotangent),
        ("bucket", bucket),
        ("wpack", wpack),
        ("w_up", w_up),
        ("w_down", w_down),
    ]
    kept = [
        ("X", (images, rows, 1024), BF16),
        ("MR", (images, rows, 2), F32),
        ("PR", (images, rows, 1024), BF16),
        ("S", (2 * images, rows, 256), F32),
        ("QA", (4, tokens, 512), BF16),
        ("MX", (tokens, 512), BF16),
        ("RES", (tokens, 1024), F32),
        ("MA", (4, tokens, 1024), BF16),
        ("CA", (4, tokens, 1024), BF16),
        ("UD", (4, 2, 128, 1024), BF16),
        ("UU", (16, 2, 32, 1024), BF16),
        ("G", (16, 2, 32, WIDE), BF16),
        ("VV", (16, 1024), F32),
    ]
    scratch_a = [
        ("WS", (4, 32, 1024), BF16),
        ("LS", (4, 2 * images, 256), F32),
        ("LG", (2 * images, 256), F32),
        ("OP", (4, tokens, 512), BF16),
        ("O1", (2, tokens, 512), BF16),
        ("O2", (tokens, 512), BF16),
    ]
    outputs = [
        ("latents_out", (images, per_lat, 1024), BF16),
        ("grad_media", (images, per_media, 1024), F32),
        ("grad_latents", (images, per_lat, 1024), F32),
        ("grad_pack", (32, WIDE), F32),
        ("grad_up", (32, 4096), F32),
        ("grad_down", (128, 1024), F32),
    ]
    scratch_b = [
        ("MG", (2, per_media, 1024), F32),
        ("ACT", (4, tokens, 1024), BF16),
        ("GG", (4, tokens, 1024), BF16),
        ("PT", (4, tokens, 1024), BF16),
        ("PY", (2, 2, tokens // 2, 1024), BF16),
        ("PX", (2, 2, tokens // 2, 1024), BF16),
        ("P2", (2, 2, tokens // 2, 1024), BF16),
        ("gD", (4, 2, 128, 1024), BF16),
        ("gU", (16, 2, 32, 1024), BF16),
        ("RD", (4, 128, 1024), BF16),
        ("RU", (16, 32, 1024), BF16),
        ("ZD", (4, 128, 1024), BF16),
        ("ZU", (4, 4, 32, 1024), BF16),
        ("U", (tokens, 1024), F32),
        ("GR", (tokens, 1024), F32),
        ("GS", (16, 1024), F32),
        ("GM", (4, tokens, 512), BF16),
        ("GP", (2 * images, rows, 256), F32),
        ("gP", (images, rows, 1024), BF16),
        ("DL", (4, 2 * images, 256), F32),
        ("LG2", (2 * images, 256), F32),
        ("QP", (4, tokens, 512), BF16),
        ("Q1", (2, tokens, 512), BF16),
        ("Q2", (tokens, 512), BF16),
        ("gA", (16, 2, 32, WIDE), BF16),
        ("RA", (16, 32, WIDE), BF16),
        ("WY", (4, 2, 16, WIDE), BF16),
        ("WX", (4, 2, 16, WIDE), BF16),
        ("W2", (4, 2, 16, WIDE), BF16),
        ("ZW", (4, 32, WIDE), BF16),
        ("SF", (4, 32, 1024), F32),
        ("SU", (4, 32, 1024), BF16),
        ("AU", (4, 32, 1024), BF16),
    ]
    made = build(forward, inputs, kept, scratch_a, 84, 1, "resampler_forward")
    carried = [(n, v) for (n, _, _), v in zip(kept, made)]
    return build(backward, inputs[:3] + carried, outputs, scratch_b, 66, 2, "resampler_backward")


def solution(mesh):
    sizes = dict(mesh.shape)
    blocks = sizes["img"] // BLOCK
    names = ("img", "lat")

    def block_shard(weight):
        if blocks == 1:
            return weight
        whole = lax.all_gather(weight, names, axis=0, tiled=True)
        each = whole.shape[0] // (BLOCK * sizes["lat"])
        mine = lax.rem(lax.axis_index("img"), BLOCK) * sizes["lat"] + lax.axis_index("lat")
        return lax.dynamic_slice_in_dim(whole, mine * each, each, 0)

    def own_shard(gradient):
        if blocks == 1:
            return gradient
        each = gradient.shape[0]
        mine = lax.rem(lax.axis_index("img"), BLOCK) * sizes["lat"] + lax.axis_index("lat")
        whole = jnp.zeros((each * BLOCK * sizes["lat"],) + gradient.shape[1:], gradient.dtype)
        whole = lax.dynamic_update_slice_in_dim(whole, gradient, mine * each, 0)
        return lax.psum_scatter(whole, names, scatter_dimension=0, tiled=True)

    def on_device(
        media,
        latents,
        bucket,
        gain_media,
        shift_media,
        gain_latent,
        shift_latent,
        gain_mlp,
        shift_mlp,
        w_query,
        w_keyvalue,
        w_output,
        w_up,
        w_down,
        cotangent,
    ):
        lat = lax.axis_index("lat")
        norms = [
            block_shard(v) for v in (gain_media, shift_media, gain_latent, shift_latent, gain_mlp, shift_mlp)
        ]
        norms = jnp.pad(jnp.tile(jnp.stack(norms), (1, 4)), ((0, 26), (0, 0)))
        lanes = jnp.arange(128, dtype=jnp.int32) // 32
        norms = jnp.where(lanes[None, :] == lat, norms, jnp.zeros_like(norms))
        out_rows = block_shard(w_output)
        out_rows = jnp.concatenate([out_rows[:, 0:512], out_rows[:, 512:1024]], axis=0)
        wpack = jnp.concatenate([block_shard(w_keyvalue), block_shard(w_query), norms, out_rows], axis=1)
        latents_out, grad_media, grad_latents, grad_pack, grad_up, grad_down = layer(
            media, latents, bucket, cotangent, wpack, block_shard(w_up), block_shard(w_down)
        )
        norm_grads = lax.dynamic_slice_in_dim(grad_pack[0:6, GN[0] : GN[0] + GN[1]], lat * 32, 32, 1)
        grad_out = jnp.concatenate(
            [grad_pack[0:16, OUT[0] : OUT[0] + OUT[1]], grad_pack[16:32, OUT[0] : OUT[0] + OUT[1]]], axis=1
        )
        return (
            latents_out,
            grad_media,
            grad_latents,
            *[own_shard(norm_grads[k]) for k in range(6)],
            own_shard(grad_pack[:, QU[0] : QU[0] + QU[1]]),
            own_shard(grad_pack[:, KV[0] : KV[0] + KV[1]]),
            own_shard(grad_out),
            own_shard(grad_up),
            own_shard(grad_down),
        )

    rows = P("img", "lat", None)
    shard = P(names)
    wide = P(names, None)
    return jax.shard_map(
        on_device,
        mesh=mesh,
        in_specs=(rows, rows, P("img")) + (shard,) * 6 + (wide,) * 5 + (rows,),
        out_specs=(rows, rows, rows) + (shard,) * 6 + (wide,) * 5,
        check_vma=False,
    )
```

time: 1360 us -> 203 us (0.15)
  waiting for transfers between devices: 1060 us -> 0 us
  Pallas kernels: 0 us -> 182 us
  matrix products: 105 us -> 0 us
  blocking collectives: 82.2 us -> 0 us
  local copies, waits for them, and re-layouts: 55.4 us -> 16.1 us
  other arithmetic: 30.5 us -> 2.18 us
  between operations: 15.5 us -> 0.68 us
    reduce_scatter x6 -> x0, waiting for transfers between devices: 755 us -> none  [the longest x1 187 us: on_device(): lax.psum_scatter(grad_down, ('img', 'lat'), scatter_dimension=0, tiled=True)]
    all_gather x6 -> x0, waiting for transfers between devices: 301 us -> none  [the longest x1 77.2 us: on_device(): lax.all_gather(w_up, ('img', 'lat'), axis=0, tiled=True)]
    pallas_call x0 -> x2, Pallas kernels: none -> 182 us  [build(): pl.pallas_call(kernel, out_shape=[jax.ShapeDtypeStruct(s, d) for _, s, d...]
    dot_general x24 -> x0, matrix products: 105 us -> none  [the longest x6 34.3 us: weight_grad(): jnp.einsum('gtd,gte->de', values, gradient, preferred_element_type=jnp.fl...]
    unnamed x2 -> x0, blocking collectives: 82.2 us -> none
    slice x3 -> x5, local copies, waits for them, and re-layouts: 24.5 us -> 5.23 us  [the longest x1 1.57 us: on_device(): grad_pack[:, KV[0]:KV[0] + KV[1]]]
  transfers between devices with their start and end apart: 12 -> 0, of which waited for: 12 -> 0; matrix products, arithmetic and copies ran while one was open for 9% -> 0% of each run, Pallas kernels for 0% -> 0%
where the time goes in v1:
time: 203 us; the launch traced here: 201 us
  Pallas kernels  182 us (90%)
  local copies, waits for them, and re-layouts  16.1 us (8%)
  other arithmetic  2.18 us (1%)
    pallas_call x2, Pallas kernels, build(): pl.pallas_call(kernel, out_shape=[jax.ShapeDtypeStruct(s, d) for _, s, d...  182 us
    unnamed x11, local copies, waits for them, and re-layouts  9.42 us

profile of v1, /device:TPU:0, one launch (start us, length us, event | category | flops | bytes accessed | tf_op | source)
XLA Modules:
  0.0 200.8 jit_solution(13784949436739940566)
XLA Ops:
  0.7 0.8 stack.27
  1.4 0.1 tile.10
  1.5 0.7 fusion.2
  2.3 1.5 maximum_maximum_fusion.refs_4_
  3.8 83.5 %resampler_forward.1 = (bf16[8,160,1024]{2,1,0:T(8,128)(2,1)}, f32[8,160,2]{2,1,0:T(8,128)}, bf16[8,160,1024]{2,1,0:T(8,128)(2,1)}, f32[16,160,256]{2,1,0:T(8,12...) custom-call(bf16[8,144,1024]{2,1,0:T(8,128)(2,1)} %refs_0_.3, ...), custom_call_target="tpu_custom_call" | custom-call | tf_op jit(solution)/shard_map/resampler_forward/pallas_call | solution.py:894
  87.3 98.3 %resampler_backward.1 = (bf16[8,16,1024]{2,1,0:T(8,128)(2,1)}, f32[8,144,1024]{2,1,0:T(8,128)}, f32[8,16,1024]{2,1,0:T(8,128)}, f32[32,2176]{1,0:T(8,128)}, f32[32,4096]{1,0:T(8,128)}, /*index=5*/f32[128,1024]{1,0:T(8,128)}) custom-call(bf16[8,144,1024]{2,1,0:T(8,128)(2,1)} %refs_0_.3, bf16[8,16,1024]{2,1,0:T(8,128)(2,1)} %refs_1_.3, ...), custom_call_target="tpu_custom_call" | custom-call | tf_op jit(solution)/shard_map/resampler_backward/pallas_call | solution.py:894
  185.6 0.7 slice.41
  186.3 0.1 constant_dynamic-slice_fusion
  186.3 0.5 slice_bitcast_fusion
  186.9 1.5 slice.48
  188.4 0.8 fusion.1
  189.1 1.6 slice.49
  190.7 0.6 pad_maximum_fusion
  191.3 1.7 copy.34
  193.0 0.0 copy-start.2
  193.0 0.0 copy-start.1
  193.0 0.0 copy-start
  193.0 5.4 %copy.35 = f32[8,144,1024]{2,1,0:T(8,128)} copy(f32[8,144,1024]{2,1,0:T(8,128)} %get-tuple-element.77) | data formatting | bytes 9437184
  198.4 0.0 copy-done.2
  198.4 0.8 copy.36
  199.2 0.0 copy-done.1
  199.2 0.8 copy.37
  200.0 0.0 copy-done
  200.0 0.8 copy.38
  (3 shorter events, 0.0 us)
Async XLA Ops:
  193.0 5.4 %copy-start.2 = (f32[8,16,1024]{2,1,0:T(8,128)S(1)}, f32[8,16,1024]{2,1,0:T(8,128)}, u32[]{:S(2)}) copy-start(f32[8,16,1024]{2,1,0:T(8,128)} %get-tuple-element.78) | copy-start | bytes 1572868
  193.0 6.2 %copy-start.1 = (f32[32,4096]{1,0:T(8,128)S(1)}, f32[32,4096]{1,0:T(8,128)}, u32[]{:S(2)}) copy-start(f32[32,4096]{1,0:T(8,128)} %get-tuple-element.88) | copy-start | bytes 1572868
  193.0 7.0 %copy-start = (f32[128,1024]{1,0:T(8,128)S(1)}, f32[128,1024]{1,0:T(8,128)}, u32[]{:S(2)}) copy-start(f32[128,1024]{1,0:T(8,128)} %get-tuple-element.89) | copy-start | bytes 1572868

commit v2 on v1

v2 whole, which is shorter than its diff:
```python
import jax
import jax.numpy as jnp
from jax import lax
from jax.experimental import pallas as pl
from jax.experimental.pallas import tpu as pltpu
from jax.sharding import PartitionSpec as P

MESH = pl.DeviceIdType.MESH
BF16 = jnp.bfloat16
F32 = jnp.float32

SHORT = 256
LONG = 576
HEADS = 8
EPS = 1e-05
SCALE = 0.125
NEG = -1e30

BLOCK = 8

QU = (0, 512)
GN = (512, 128)
KEY = (640, 512)
VAL = (1152, 512)
KV = (640, 1024)
OUT = (1664, 512)
WIDE = 2176
GQG = (0, 640)
GOUT = (640, 512)
NARROW = 1152
MESSAGES = 183


def mm(a, b):
    return lax.dot_general(a, b, (((1,), (0,)), ((), ())), preferred_element_type=F32)


def mm_nt(a, b):
    return lax.dot_general(a, b, (((1,), (1,)), ((), ())), preferred_element_type=F32)


def mm_tn(a, b):
    return lax.dot_general(a, b, (((0,), (0,)), ((), ())), preferred_element_type=F32)


def cols(span):
    return pl.ds(span[0], span[1])


def flat(values):
    return values.reshape(-1, values.shape[-1])


def normal(values):
    mean = jnp.mean(values, axis=-1, keepdims=True)
    centred = values - mean
    spread = jnp.mean(centred * centred, axis=-1, keepdims=True)
    return mean, lax.rsqrt(spread + EPS)


def norm_back(upstream, normed, rstd, gain):
    scaled = upstream * gain
    first = jnp.mean(scaled, axis=-1, keepdims=True)
    second = jnp.mean(scaled * normed, axis=-1, keepdims=True)
    return (scaled - first - normed * second) * rstd


class Place:
    def __init__(self):
        img = lax.axis_index("img")
        lat = lax.axis_index("lat")
        self.i = lax.rem(img, BLOCK)
        self.base = img - self.i
        self.z = lax.div(self.i, 2)
        self.x = lax.rem(self.i, 2)
        self.l = lat
        self.y = lax.div(lat, 2)
        self.c = lax.rem(lat, 2)
        self.z1 = self.z + 1 - 2 * lax.rem(self.z, 2)
        self.z2 = lax.rem(self.z + 2, 4)
        self.z3 = 3 - self.z
        self.mid = jnp.logical_or(self.z == 1, self.z == 2)
        self.zs = (self.z, self.z1, self.z2, self.z3)
        self.end = jnp.logical_or(self.z == 0, self.z == 3)
        self.p = self.x * 2 + self.y
        self.q = self.z * 4 + self.p
        self.px = (1 - self.x) * 2 + self.y
        self.py = self.x * 2 + 1 - self.y
        self.pd = 3 - self.p
        self.lc = self.y * 2 + 1 - self.c
        self.ly = (1 - self.y) * 2 + self.c
        self.ld = 3 - self.l
        self.core = self.dev(self.z, self.x, self.y, 1 - self.c)
        self.xn = self.dev(self.z, 1 - self.x, self.y, self.c)
        self.yn = self.dev(self.z, self.x, 1 - self.y, self.c)
        self.diag = self.dev(self.z, 1 - self.x, 1 - self.y, self.c)
        self.ycore = self.dev(self.z, self.x, 1 - self.y, 1 - self.c)
        self.zn1 = self.dev(self.z1, self.x, self.y, self.c)
        self.zn2 = self.dev(self.z2, self.x, self.y, self.c)
        self.zn3 = self.dev(self.z3, self.x, self.y, self.c)

    def dev(self, z, x, y, c):
        return (self.base + z * 2 + x, y * 2 + c)

    def greet(self):
        barrier = pltpu.get_barrier_semaphore()
        peers = (self.core, self.xn, self.yn, self.diag, self.ycore, self.zn1, self.zn2, self.zn3)
        for peer in peers:
            pl.semaphore_signal(barrier, inc=1, device_id=peer, device_id_type=MESH)
        pl.semaphore_wait(barrier, len(peers))


def guarded(when, action):
    if when is None:
        action()
    else:
        pl.when(when)(action)


class Msg:
    def __init__(self, post, src, dst, dev, into, key=None, when=None):
        self.k = post.count
        post.count += 1
        self.key = self.k if key is None else key
        self.when = when
        self.post, self.src, self.dst, self.dev, self.into = post, src, dst, dev, into
        self.done = False
        post.all.append(self)

    def copy(self, src, dst):
        return pltpu.make_async_remote_copy(
            src_ref=src,
            dst_ref=dst,
            send_sem=self.post.send.at[self.k],
            recv_sem=self.post.recv.at[self.key],
            device_id=self.dev,
            device_id_type=MESH,
        )

    def start(self):
        guarded(self.when, lambda: self.copy(self.src, self.dst).start())

    def arrived(self):
        self.copy(self.into, self.into).wait_recv()

    def sent(self):
        if self.done:
            return
        self.done = True
        guarded(self.when, lambda: self.copy(self.src, self.dst).wait_send())


class Post:
    def __init__(self, send, recv):
        self.send = send
        self.recv = recv
        self.count = 0
        self.all = []

    def msg(self, *a, **k):
        return Msg(self, *a, **k)

    def drain(self):
        for m in self.all:
            m.sent()


class ZGather:
    def __init__(self, post, at, view):
        own = view(at.z)
        self.m1 = post.msg(own, own, at.zn1, view(at.z1))
        self.m2 = post.msg(own, own, at.zn2, view(at.z2))
        self.m3 = post.msg(own, own, at.zn3, view(at.z3), when=at.mid)
        self.relay = post.msg(view(at.z2), view(at.z2), at.zn1, view(at.z3), key=self.m3.k, when=at.mid)

    def start(self):
        self.m1.start()
        self.m2.start()
        self.m3.start()

    def near(self):
        self.m1.arrived()

    def far(self):
        self.m2.arrived()
        self.relay.start()

    def last(self):
        self.m3.arrived()


class PlaneGather:
    def __init__(self, post, at, view, half):
        own = view(at.x, at.y)
        ox, oy = 1 - at.x, 1 - at.y
        self.mx = post.msg(own, own, at.xn, view(ox, at.y))
        self.my = post.msg(own, own, at.yn, view(at.x, oy))
        self.hy = post.msg(half(ox, at.y, 0), half(ox, at.y, 0), at.yn, half(ox, oy, 0))
        self.hx = post.msg(half(at.x, oy, 1), half(at.x, oy, 1), at.xn, half(ox, oy, 1))

    def start(self):
        self.mx.start()
        self.my.start()

    def relay(self):
        self.mx.arrived()
        self.hy.start()
        self.my.arrived()
        self.hx.start()

    def last(self):
        self.hy.arrived()
        self.hx.arrived()


class Spread:
    def __init__(self, post, at, G, span):
        lanes = cols(span)

        def view(zz, x, y):
            return G.at[zz, x * 2 + y, at.c, :, lanes]

        def half(zz, x, y, h):
            return G.at[zz, x * 2 + y, at.c, pl.ds(16 * h, 16), lanes]

        own = view(at.z, at.x, at.y)
        self.z = [
            post.msg(own, own, dev, view(zz, at.x, at.y))
            for zz, dev in ((at.z1, at.zn1), (at.z2, at.zn2), (at.z3, at.zn3))
        ]
        self.plane = [
            PlaneGather(
                post, at, lambda x, y, zz=zz: view(zz, x, y), lambda x, y, h, zz=zz: half(zz, x, y, h)
            )
            for zz in at.zs
        ]
        self.core = [
            post.msg(
                G.at[zz, :, at.c, :, lanes], G.at[zz, :, at.c, :, lanes], at.core, G.at[zz, :, 1 - at.c, :, lanes]
            )
            for zz in at.zs
        ]

    def start(self):
        for m in self.z:
            m.start()

    def into_plane(self):
        for k in range(3):
            self.z[k].arrived()
            self.plane[k + 1].start()

    def relay(self):
        for g in self.plane:
            g.relay()

    def to_core(self):
        for g, m in zip(self.plane, self.core):
            g.last()
            m.start()

    def arrived(self):
        for m in self.core:
            m.arrived()


class LatGather:
    def __init__(self, post, at, view):
        self.mc = post.msg(view(at.l), view(at.l), at.core, view(at.lc))
        self.my = post.msg(view(at.l), view(at.l), at.yn, view(at.ly))
        self.fc = post.msg(view(at.ly), view(at.ly), at.core, view(at.ld))

    def start(self):
        self.my.start()
        self.mc.start()

    def relay(self):
        self.my.arrived()
        self.fc.start()

    def last(self):
        self.mc.arrived()
        self.fc.arrived()


class LatReduce:
    def __init__(self, post, at, parts, first, second):
        self.at, self.parts, self.first, self.second = at, parts, first, second
        self.m0 = post.msg(parts.at[at.lc], first.at[0], at.core, first.at[0])
        self.m1 = post.msg(parts.at[at.ld], first.at[1], at.core, first.at[1])
        self.m2 = post.msg(parts.at[at.ly], second, at.yn, second)

    def start(self):
        self.m1.start()
        self.m0.start()

    def relay(self):
        self.m1.arrived()
        ly = self.at.ly
        self.parts[ly] = (self.parts[ly].astype(F32) + self.first[1].astype(F32)).astype(BF16)
        self.m2.start()

    def total(self):
        self.m0.arrived()
        self.m2.arrived()
        near = self.parts[self.at.l].astype(F32) + self.first[0].astype(F32)
        return near + self.second[...].astype(F32)


class PlaneReduce:
    def __init__(self, post, at, part, by, bx, b2):
        x, y = at.x, at.y
        ox, oy = 1 - x, 1 - y
        self.part, self.by, self.bx, self.b2 = part, by, bx, b2
        self.x, self.y, self.ox, self.oy = x, y, ox, oy
        self.my1 = post.msg(part(ox, oy, 0), by(1), at.yn, by(1))
        self.mx1 = post.msg(part(ox, oy, 1), bx(1), at.xn, bx(1))
        self.my0 = post.msg(part(x, oy, 0), by(0), at.yn, by(0))
        self.mx0 = post.msg(part(ox, y, 1), bx(0), at.xn, bx(0))
        self.f0 = post.msg(part(ox, y, 0), b2(0), at.xn, b2(0))
        self.f1 = post.msg(part(x, oy, 1), b2(1), at.yn, b2(1))

    def start(self):
        self.my1.start()
        self.mx1.start()

    def relay(self):
        self.my1.arrived()
        there = self.part(self.ox, self.y, 0)
        there[...] = (there[...].astype(F32) + self.by(1)[...].astype(F32)).astype(BF16)
        self.f0.start()
        self.mx1.arrived()
        there = self.part(self.x, self.oy, 1)
        there[...] = (there[...].astype(F32) + self.bx(1)[...].astype(F32)).astype(BF16)
        self.f1.start()
        self.my0.start()
        self.mx0.start()

    def total(self):
        self.my0.arrived()
        self.f0.arrived()
        low = self.part(self.x, self.y, 0)[...].astype(F32) + self.by(0)[...].astype(F32)
        low = low + self.b2(0)[...].astype(F32)
        self.mx0.arrived()
        self.f1.arrived()
        high = self.part(self.x, self.y, 1)[...].astype(F32) + self.bx(0)[...].astype(F32)
        return low, high + self.b2(1)[...].astype(F32)


class ZReduce:
    def __init__(self, post, at, term, buf):
        self.at, self.term, self.buf = at, term, buf
        self.m1 = post.msg(term(at.z1), buf(0), at.zn1, buf(0))
        self.m2 = post.msg(term(at.z2), buf(1), at.zn2, buf(1))
        self.m3 = post.msg(term(at.z3), buf(2), at.zn3, buf(2), when=at.mid)
        self.rel = post.msg(term(at.z3), buf(3), at.zn1, buf(3), when=at.end)

    def start(self):
        self.rel.start()
        pl.when(self.at.end)(self.m2.start)
        self.m1.start()
        self.m3.start()

    def relay(self):
        @pl.when(self.at.mid)
        def _():
            self.rel.arrived()
            there = self.term(self.at.z2)
            there[...] = (there[...].astype(F32) + self.buf(3)[...].astype(F32)).astype(BF16)
            self.m2.start()

    def total(self, out):
        self.m1.arrived()
        self.m2.arrived()
        value = self.term(self.at.z)[...].astype(F32) + self.buf(0)[...].astype(F32)
        out[...] = value + self.buf(1)[...].astype(F32)

        @pl.when(self.at.mid)
        def _():
            self.m3.arrived()
            out[...] += self.buf(2)[...].astype(F32)


class Collect:
    def __init__(self, post, at, grads, near, by, bx, b2, bz, src, dst):
        self.at, self.grads, self.near, self.src = at, grads, near, src
        self.lanes, self.there = cols(src), cols(dst)
        self.core = post.msg(
            grads.at[:, :, 1 - at.c, :, self.lanes], near.at[:, :, :, self.lanes], at.core,
            near.at[:, :, :, self.lanes],
        )
        self.plane = PlaneReduce(
            post,
            at,
            lambda x, y, h: near.at[:, x * 2 + y, pl.ds(16 * h, 16), self.lanes],
            lambda k: by.at[k, :, :, self.there],
            lambda k: bx.at[k, :, :, self.there],
            lambda k: b2.at[k, :, :, self.there],
        )
        self.z = ZReduce(
            post, at, lambda zz: near.at[zz, at.p, :, self.lanes], lambda k: bz.at[k, :, self.there]
        )

    def start(self):
        self.core.start()

    def into_plane(self):
        self.core.arrived()

        def add(zz, carry):
            mine = self.grads[zz, :, self.at.c, :, self.lanes].astype(F32)
            self.near[zz, :, :, self.lanes] = (self.near[zz, :, :, self.lanes].astype(F32) + mine).astype(BF16)
            return carry

        lax.fori_loop(0, 4, add, 0)
        self.plane.start()

    def relay(self):
        self.plane.relay()

    def into_z(self):
        low, high = self.plane.total()
        self.near[:, self.at.p, 0:16, self.lanes] = low.astype(BF16)
        self.near[:, self.at.p, 16:32, self.lanes] = high.astype(BF16)
        self.z.start()

    def z_relay(self):
        self.z.relay()

    def total(self, out):
        self.z.total(out)


def head_mask():
    rows = lax.div(lax.broadcasted_iota(jnp.int32, (256, 256), 0), 64)
    lanes = lax.div(lax.broadcasted_iota(jnp.int32, (256, 256), 1), 64)
    return (rows == lanes).astype(F32).astype(BF16)


def spread_heads(part, mask):
    rows = part.reshape(64, 256)
    return jnp.concatenate([rows, rows, rows, rows], axis=0) * mask


def gather_heads(wide):
    lane = lax.div(lax.broadcasted_iota(jnp.int32, (64, 256), 1), 64)
    out = jnp.where(lane == 0, wide[0:64], 0.0)
    for h in range(1, 4):
        out = out + jnp.where(lane == h, wide[64 * h : 64 * h + 64], 0.0)
    return out


def span256(n):
    return pl.ds(pl.multiple_of(n * 256, 256), 256)


def kernel_body(at, post, R):
    images, per_media, _ = R.MED.shape
    per_lat = R.latents.shape[1]
    rows = per_media + per_lat
    tokens = images * per_lat
    half_rows = tokens // 2
    zs = at.zs

    media_in = pltpu.make_async_copy(R.media, R.MED, R.local.at[0])
    media_in.start()
    R.G[at.z, at.p, at.c, :, cols(QU)] = R.w_query[...]
    R.G[at.z, at.p, at.c, :, cols(KV)] = R.w_keyvalue[...]
    R.G[at.z, at.p, at.c, 0:16, cols(OUT)] = R.w_output[:, 0:512]
    R.G[at.z, at.p, at.c, 16:32, cols(OUT)] = R.w_output[:, 512:1024]
    norms = R.norms[...].astype(F32)
    norms = jnp.concatenate([norms, norms, norms, norms], axis=1)
    lanes = lax.div(lax.broadcasted_iota(jnp.int32, (16, 128), 1), 32)
    R.G[at.z, at.p, at.c, 0:16, cols(GN)] = jnp.where(lanes == at.l, norms, 0.0).astype(BF16)
    R.G[at.z, at.p, at.c, 16:32, cols(GN)] = jnp.zeros((16, 128), BF16)
    R.UD[at.z, at.c] = R.w_down[...]
    for p in range(4):
        for zz in range(4):
            for cc in range(2):
                R.WS[p, :, 128 * (2 * zz + cc) : 128 * (2 * zz + cc) + 128] = R.w_up[
                    :, 128 * (8 * zz + 2 * p + cc) : 128 * (8 * zz + 2 * p + cc) + 128
                ]
    R.UU[at.z, at.p, at.c] = R.WS[at.p]
    R.CA[at.p] = R.cotangent[...].reshape(tokens, 1024)

    with jax.named_scope("greet"):
        at.greet()

    first = Spread(post, at, R.G, (0, 1152))
    second = Spread(post, at, R.G, VAL)
    third = Spread(post, at, R.G, OUT)
    up = [
        post.msg(R.WS.at[there], R.UU.at[at.z, at.p, at.c], dev, R.UU.at[at.z, there, at.c])
        for there, dev in ((at.px, at.xn), (at.py, at.yn), (at.pd, at.diag))
    ]
    d_z = ZGather(post, at, lambda zz: R.UD.at[zz, at.c])
    u_z = ZGather(post, at, lambda zz: R.UU.at[zz, :, at.c])
    d_c = [post.msg(R.UD.at[zz, at.c], R.UD.at[zz, at.c], at.core, R.UD.at[zz, 1 - at.c]) for zz in zs]
    u_c = [
        post.msg(R.UU.at[zz, :, at.c], R.UU.at[zz, :, at.c], at.core, R.UU.at[zz, :, 1 - at.c]) for zz in zs
    ]
    cot = PlaneGather(
        post,
        at,
        lambda x, y: R.CA.at[x * 2 + y],
        lambda x, y, h: R.CA.at[x * 2 + y, pl.ds(h * half_rows, half_rows)],
    )

    first.start()
    first.plane[0].start()
    for m in up:
        m.start()

    def stats(g, carry):
        mean, rstd = normal(R.MED[g].astype(F32))
        R.MR[g, 0:per_media, 0:1] = mean
        R.MR[g, 0:per_media, 1:2] = rstd
        mean, rstd = normal(R.latents[g].astype(F32))
        R.MR[g, per_media:rows, 0:1] = mean
        R.MR[g, per_media:rows, 1:2] = rstd
        return carry

    media_in.wait()
    loop(images, stats)
    first.into_plane()
    second.start()
    d_z.start()
    d_c[0].start()
    first.relay()
    for m in up:
        m.arrived()
    u_z.start()
    u_c[0].start()
    first.to_core()
    second.plane[0].start()
    second.into_plane()
    third.start()
    first.arrived()

    for i in range(8):
        total = jnp.zeros((16, 128), F32)
        for p in (2 * (i % 2), 2 * (i % 2) + 1):
            for c in range(2):
                total = total + R.G[i // 2, p, c, 0:16, cols(GN)].astype(F32)
        R.VV[:, 128 * i : 128 * i + 128] = total

    latents = flat(R.latents[...]).astype(F32)
    normed = (latents - flat(R.MR[:, per_media:rows, 0:1])) * flat(R.MR[:, per_media:rows, 1:2])
    latent_low = (normed * R.VV[2:3, :] + R.VV[3:4, :]).astype(BF16)
    R.X[:, per_media:rows, :] = latent_low.reshape(images, per_lat, 1024)
    R.QA[at.l] = mm(latent_low, R.G[:, :, :, :, cols(QU)].reshape(1024, 512)).astype(BF16)
    q_all = LatGather(post, at, lambda l: R.QA.at[l])
    q_all.start()

    def low(g, carry):
        normed = (R.MED[g].astype(F32) - R.MR[g, 0:per_media, 0:1]) * R.MR[g, 0:per_media, 1:2]
        R.X[g, 0:per_media, :] = (normed * R.VV[0:1, :] + R.VV[1:2, :]).astype(BF16)
        return carry

    loop(images, low)
    second.relay()

    def pairs(n, carry):
        weight = R.G[:, :, :, :, pl.ds(pl.multiple_of(KV[0] + n * 256, 128), 256)].reshape(1024, 256)
        made = mm(R.X[...].reshape(images * rows, 1024), weight).astype(BF16)
        R.PR[:, :, span256(n)] = made.reshape(images, rows, 256)
        return carry

    loop((0, 2), pairs)
    q_all.relay()
    second.to_core()
    third.plane[0].start()
    third.into_plane()
    q_all.last()

    mask = head_mask()

    def score(g, carry):
        limit = SHORT + (LONG - SHORT) * R.bucket[g] - at.l * per_media
        row = lax.broadcasted_iota(jnp.int32, (rows, 256), 0)
        valid = jnp.logical_or(row >= per_media, row < limit)
        for half in range(2):
            span = pl.ds(256 * half, 256)
            queries = spread_heads(R.QA[:, pl.ds(pl.multiple_of(g * per_lat, per_lat), per_lat), span], mask)
            raw = mm_nt(R.PR[g, :, span], queries) * SCALE
            raw = jnp.where(valid, raw, NEG)
            top = jnp.max(raw, axis=0, keepdims=True)
            total = jnp.sum(jnp.exp(raw - top), axis=0, keepdims=True)
            R.S[2 * g + half] = raw
            R.LS[at.l, pl.ds(2 * g + half, 1), :] = top + jnp.log(total)
        return carry

    loop(images, score)
    ls = [
        post.msg(R.LS.at[at.l], R.LS.at[at.l], dev, R.LS.at[there])
        for there, dev in ((at.ly, at.yn), (at.ld, at.ycore), (at.lc, at.core))
    ]
    for m in ls:
        m.start()
    second.arrived()
    loop((2, 4), pairs)
    third.relay()
    cot.start()
    for m in ls:
        m.arrived()
    top = jnp.maximum(jnp.maximum(R.LS[0], R.LS[1]), jnp.maximum(R.LS[2], R.LS[3]))
    total = jnp.exp(R.LS[0] - top)
    for l in range(1, 4):
        total = total + jnp.exp(R.LS[l] - top)
    R.LG[...] = top + jnp.log(total)

    def mix(g, carry):
        for half in range(2):
            probs = jnp.exp(R.S[2 * g + half] - R.LG[pl.ds(2 * g + half, 1), :]).astype(BF16)
            R.PB[2 * g + half] = probs
            wide = mm_tn(probs, R.PR[g, :, pl.ds(512 + 256 * half, 256)])
            R.OP[:, pl.ds(pl.multiple_of(g * per_lat, per_lat), per_lat), pl.ds(256 * half, 256)] = (
                gather_heads(wide).reshape(4, per_lat, 256).astype(BF16)
            )
        return carry

    loop(images, mix)
    mixed = LatReduce(post, at, R.OP, R.O1, R.O2)
    mixed.start()
    d_z.near()
    d_c[1].start()
    u_z.near()
    u_c[1].start()
    mixed.relay()
    third.to_core()
    d_z.far()
    d_c[2].start()
    u_z.far()
    u_c[2].start()
    cot.relay()
    third.arrived()
    R.MX[...] = mixed.total().astype(BF16)
    left = R.G[:, :, :, 0:16, cols(OUT)].reshape(512, 512)
    right = R.G[:, :, :, 16:32, cols(OUT)].reshape(512, 512)
    latents = flat(R.latents[...]).astype(F32)
    R.RES[:, 0:512] = latents[:, 0:512] + mm(R.MX[...], left)
    R.RES[:, 512:1024] = latents[:, 512:1024] + mm(R.MX[...], right)
    mean, rstd = normal(R.RES[...])
    R.MA[at.p] = ((R.RES[...] - mean) * rstd * R.VV[4:5, :] + R.VV[5:6, :]).astype(BF16)
    mlp = PlaneGather(
        post,
        at,
        lambda x, y: R.MA.at[x * 2 + y],
        lambda x, y, h: R.MA.at[x * 2 + y, pl.ds(h * half_rows, half_rows)],
    )
    mlp.start()
    mlp.relay()
    cot.last()
    d_z.last()
    u_z.last()
    d_c[3].start()
    u_c[3].start()
    for m in d_c + u_c:
        m.arrived()
    mlp.last()

    def gates(f, carry):
        gate = mm(R.MA[...].reshape(4 * tokens, 1024), R.UU[:, :, :, :, span256(f)].reshape(1024, 256))
        back = mm_nt(R.CA[...].reshape(4 * tokens, 1024), R.UD[f].reshape(256, 1024))
        phi = 0.5 * (1.0 + lax.erf(gate * 0.7071067811865476))
        R.ACT[:, :, span256(f)] = (gate * phi).astype(BF16).reshape(4, tokens, 256)
        slope = phi + gate * jnp.exp(-0.5 * gate * gate) * 0.3989422804014327
        R.GG[:, :, span256(f)] = (back * slope).astype(BF16).reshape(4, tokens, 256)
        return carry

    loop(4, gates)

    def norm_parts(n, carry):
        made = mm_nt(R.GG[...].reshape(4 * tokens, 1024), R.UU[n].reshape(256, 1024))
        R.PT[:, :, span256(n)] = made.astype(BF16).reshape(4, tokens, 256)
        return carry

    loop(4, norm_parts)
    back = PlaneReduce(
        post,
        at,
        lambda x, y, h: R.PT.at[x * 2 + y, pl.ds(h * half_rows, half_rows)],
        lambda k: R.PY.at[0, k],
        lambda k: R.PX.at[0, k],
        lambda k: R.P2.at[0, k],
    )
    back.start()

    def down_grads(f, carry):
        act = R.ACT[:, :, span256(f)].reshape(4 * tokens, 256)
        R.gD[f] = mm_tn(act, R.CA[...].reshape(4 * tokens, 1024)).astype(BF16).reshape(2, 128, 1024)
        return carry

    loop(4, down_grads)
    gd_c = post.msg(R.gD.at[:, 1 - at.c], R.RD, at.core, R.RD)
    gd_c.start()
    back.relay()

    def up_grads(n, carry):
        low_rows = R.MA[:, :, span256(n)].reshape(4 * tokens, 256)
        made = mm_tn(low_rows, R.GG[...].reshape(4 * tokens, 1024)).astype(BF16)
        R.gU[n] = made.reshape(4, 2, 32, 1024)
        return carry

    loop(4, up_grads)
    gu_c = post.msg(R.gU.at[:, :, 1 - at.c], R.RU, at.core, R.RU)
    gu_c.start()
    gd_c.arrived()

    def add_d(zz, carry):
        R.RD[zz] = (R.RD[zz].astype(F32) + R.gD[zz, at.c].astype(F32)).astype(BF16)
        return carry

    loop(4, add_d)
    gd_z = ZReduce(post, at, lambda zz: R.RD.at[zz], lambda k: R.ZD.at[k])
    gd_z.start()

    def out_parts(n, carry):
        made = mm(R.ACT[...].reshape(4 * tokens, 1024), R.UD[:, :, :, span256(n)].reshape(1024, 256))
        R.GG[:, :, span256(n)] = made.astype(BF16).reshape(4, tokens, 256)
        return carry

    loop(4, out_parts)
    gu_c.arrived()

    def add_u(zz, carry):
        R.RU[zz] = (R.RU[zz].astype(F32) + R.gU[zz, :, at.c].astype(F32)).astype(BF16)
        return carry

    loop(4, add_u)
    gu_z = ZReduce(post, at, lambda zz: R.RU.at[zz], lambda k: R.ZU.at[k])
    gu_z.start()
    out = PlaneReduce(
        post,
        at,
        lambda x, y, h: R.GG.at[x * 2 + y, pl.ds(h * half_rows, half_rows)],
        lambda k: R.PY.at[1, k],
        lambda k: R.PX.at[1, k],
        lambda k: R.P2.at[1, k],
    )
    low_part, high_part = back.total()
    R.U[0:half_rows] = low_part
    R.U[half_rows:] = high_part

    mean, rstd = normal(R.RES[...])
    normed = (R.RES[...] - mean) * rstd
    upstream = R.U[...]
    R.GR[...] = flat(R.cotangent[...]).astype(F32) + norm_back(upstream, normed, rstd, R.VV[4:5, :])
    R.GS[...] = jnp.zeros_like(R.GS)
    R.GS[4:5, :] = jnp.sum(upstream * normed, axis=0, keepdims=True)
    R.GS[5:6, :] = jnp.sum(upstream, axis=0, keepdims=True)
    grad_attn = R.GR[...].astype(BF16)
    left = R.G[:, :, :, 0:16, cols(OUT)].reshape(512, 512)
    right = R.G[:, :, :, 16:32, cols(OUT)].reshape(512, 512)
    R.GM[at.l] = (mm_nt(grad_attn[:, 0:512], left) + mm_nt(grad_attn[:, 512:1024], right)).astype(BF16)
    gm = LatGather(post, at, lambda l: R.GM.at[l])
    gm.start()
    grad_attn = R.GR[...].astype(BF16)
    made = mm_tn(R.MX[...], grad_attn[:, 0:512]).astype(BF16)
    R.gA[:, :, :, 0:16, cols(GOUT)] = made.reshape(4, 4, 2, 16, 512)
    made = mm_tn(R.MX[...], grad_attn[:, 512:1024]).astype(BF16)
    R.gA[:, :, :, 16:32, cols(GOUT)] = made.reshape(4, 4, 2, 16, 512)
    w_out = Collect(post, at, R.gA, R.RA, R.WY, R.WX, R.W2, R.ZW, GOUT, OUT)
    w_out.start()
    gm.relay()
    gm.last()

    def grad_probs(g, carry):
        lat_rows = pl.ds(pl.multiple_of(g * per_lat, per_lat), per_lat)
        for half in range(2):
            upper = pl.ds(512 + 256 * half, 256)
            wide = spread_heads(R.GM[:, lat_rows, pl.ds(256 * half, 256)], mask)
            made = mm_nt(R.PR[g, :, upper], wide)
            probs = R.PB[2 * g + half]
            R.S[2 * g + half] = made
            R.DL[at.l, pl.ds(2 * g + half, 1), :] = jnp.sum(probs.astype(F32) * made, axis=0, keepdims=True)
            R.gP[g, :, upper] = mm(probs, wide).astype(BF16)
        return carry

    loop(images, grad_probs)
    dl = [
        post.msg(R.DL.at[at.l], R.DL.at[at.l], dev, R.DL.at[there])
        for there, dev in ((at.ly, at.yn), (at.ld, at.ycore), (at.lc, at.core))
    ]
    for m in dl:
        m.start()
    w_out.into_plane()

    def kv_grads(n, carry):
        low_rows = R.X[:, :, span256(lax.rem(n, 4))].reshape(images * rows, 256)
        lanes = pl.ds(pl.multiple_of(lax.div(n, 4) * 512, 512), 512)
        made = mm_tn(low_rows, R.gP[:, :, lanes].reshape(images * rows, 512)).astype(BF16)
        R.gU[lax.rem(n, 4), :, :, :, lanes] = made.reshape(4, 2, 32, 512)
        return carry

    gu_c.sent()
    loop((4, 8), kv_grads)
    w_val = Collect(post, at, R.gU, R.RK, R.WY, R.WX, R.W2, R.ZW, (512, 512), VAL)
    w_val.start()
    for m in dl:
        m.arrived()
    R.LG[...] = R.DL[0] + R.DL[1] + R.DL[2] + R.DL[3]

    def grad_scores(g, carry):
        lat_rows = pl.ds(pl.multiple_of(g * per_lat, per_lat), per_lat)
        for half in range(2):
            span = pl.ds(256 * half, 256)
            grads = R.PB[2 * g + half].astype(F32) * (R.S[2 * g + half] - R.LG[pl.ds(2 * g + half, 1), :])
            grads = grads.astype(BF16)
            wide = mm_tn(grads, R.PR[g, :, span]) * SCALE
            R.QP[:, lat_rows, span] = gather_heads(wide).reshape(4, per_lat, 256).astype(BF16)
            queries = spread_heads(R.QA[:, lat_rows, span], mask)
            R.gP[g, :, span] = (mm(grads, queries) * SCALE).astype(BF16)
        return carry

    loop(images, grad_scores)
    gq = LatReduce(post, at, R.QP, R.Q1, R.Q2)
    gq.start()
    w_out.relay()
    w_val.into_plane()
    loop((0, 4), kv_grads)
    w_key = Collect(post, at, R.gU, R.RK, R.WY, R.WX, R.W2, R.ZW, (0, 512), KEY)
    w_key.start()
    gq.relay()
    gd_z.relay()
    gu_z.relay()
    w_out.into_z()
    w_val.relay()
    w_key.into_plane()

    def media_copy(h):
        return pltpu.make_async_copy(R.MG, R.grad_media.at[pl.ds(h * 2, 2)], R.local.at[0])

    def media_grads(h, carry):
        span = pl.ds(h * 2, 2)
        weight = R.G[:, :, :, :, cols(KV)].reshape(1024, 1024)
        upstream = mm_nt(R.gP[span].reshape(2 * rows, 1024), weight).reshape(2, rows, 1024)
        R.U[pl.ds(h * 2 * per_lat, 2 * per_lat)] = upstream[:, per_media:rows, :].reshape(2 * per_lat, 1024)
        upstream = upstream[:, 0:per_media, :]
        rstd = R.MR[span, 0:per_media, 1:2]
        normed = (R.MED[span].astype(F32) - R.MR[span, 0:per_media, 0:1]) * rstd
        made = norm_back(upstream, normed, rstd, R.VV[0:1, :]).astype(R.MG.dtype)
        pl.when(h >= 1)(lambda: media_copy(h - 1).wait())
        R.MG[...] = made
        media_copy(h).start()
        R.GS[0:1, :] += jnp.sum(flat(upstream * normed), axis=0, keepdims=True)
        R.GS[1:2, :] += jnp.sum(flat(upstream), axis=0, keepdims=True)
        return carry

    loop((0, images // 4), media_grads)
    w_val.into_z()
    w_key.relay()
    w_out.z_relay()
    loop((images // 4, images // 2), media_grads)
    media_copy(images // 2 - 1).wait()
    w_val.z_relay()

    grad_query = gq.total().astype(BF16)
    latent_low = flat(R.X[:, per_media:rows, :])
    upstream = R.U[...] + mm_nt(grad_query, R.G[:, :, :, :, cols(QU)].reshape(1024, 512))
    rstd = flat(R.MR[:, per_media:rows, 1:2])
    normed = (flat(R.latents[...]).astype(F32) - flat(R.MR[:, per_media:rows, 0:1])) * rstd
    R.grad_latents[...] = (R.GR[...] + norm_back(upstream, normed, rstd, R.VV[2:3, :])).reshape(
        images, per_lat, 1024
    )
    R.GS[2:3, :] = jnp.sum(upstream * normed, axis=0, keepdims=True)
    R.GS[3:4, :] = jnp.sum(upstream, axis=0, keepdims=True)
    R.gA[:, :, :, :, cols(QU)] = mm_tn(latent_low, grad_query).astype(BF16).reshape(4, 4, 2, 32, 512)
    for i in range(8):
        piece = R.GS[:, 128 * i : 128 * i + 128].astype(BF16)
        for p in (2 * (i % 2), 2 * (i % 2) + 1):
            for c in range(2):
                R.gA[i // 2, p, c, 0:16, cols(GN)] = piece
                R.gA[i // 2, p, c, 16:32, cols(GN)] = jnp.zeros((16, 128), BF16)
    w_qg = Collect(post, at, R.gA, R.RA, R.WY, R.WX, R.W2, R.ZW, GQG, GQG)
    w_qg.start()
    w_key.into_z()
    w_qg.into_plane()
    out.start()
    gd_z.total(R.grad_down)
    gu_z.total(R.SF)
    R.SU[...] = R.SF[...].astype(BF16)
    R.AU[at.p] = R.SU[at.p]
    up = [
        post.msg(R.SU.at[there], R.AU.at[at.p], dev, R.AU.at[there])
        for there, dev in ((at.px, at.xn), (at.py, at.yn), (at.pd, at.diag))
    ]
    for m in up:
        m.start()
    w_qg.relay()
    out.relay()
    w_key.z_relay()
    w_out.total(R.grad_pack.at[:, cols(OUT)])
    w_val.total(R.grad_pack.at[:, cols(VAL)])
    w_qg.into_z()
    w_qg.z_relay()
    low_part, high_part = out.total()
    R.latents_out[...] = jnp.concatenate(
        [R.RES[0:half_rows] + low_part, R.RES[half_rows:] + high_part], axis=0
    ).astype(BF16).reshape(images, per_lat, 1024)
    w_key.total(R.grad_pack.at[:, cols(KEY)])
    for m in up:
        m.arrived()
    for p in range(4):
        for zz in range(4):
            for cc in range(2):
                R.grad_up[:, 128 * (8 * zz + 2 * p + cc) : 128 * (8 * zz + 2 * p + cc) + 128] = R.AU[
                    p, :, 128 * (2 * zz + cc) : 128 * (2 * zz + cc) + 128
                ].astype(F32)
    w_qg.total(R.grad_pack.at[:, cols(GQG)])


def loop(bounds, step):
    first, last = bounds if isinstance(bounds, tuple) else (0, bounds)
    with jax.named_scope(step.__name__):
        lax.fori_loop(first, last, step, 0)


PLACES = {"bucket": pltpu.SMEM, "media": pl.ANY, "grad_media": pl.ANY}


class Refs:
    def __init__(self, names, refs):
        for name, ref in zip(names, refs):
            setattr(self, name, ref)


def build(kernel_body, inputs, outputs, scratch, messages, cid, name):
    in_names = [n for n, _ in inputs]
    out_names = [n for n, _, _ in outputs]
    scratch_names = [n for n, _, _ in scratch]

    def kernel(*refs):
        R = Refs(in_names + out_names + scratch_names, refs)
        at = Place()
        R.local = refs[-3]
        post = Post(refs[-2], refs[-1])
        kernel_body(at, post, R)
        post.drain()
        assert post.count == messages, post.count

    specs = [
        pl.BlockSpec(memory_space=PLACES.get(n, pltpu.VMEM)) for n in in_names
    ]
    return pl.pallas_call(
        kernel,
        out_shape=[jax.ShapeDtypeStruct(s, d) for _, s, d in outputs],
        in_specs=specs,
        out_specs=[
            pl.BlockSpec(memory_space=PLACES.get(n, pltpu.VMEM)) for n, _, _ in outputs
        ],
        scratch_shapes=[pltpu.VMEM(s, d) for _, s, d in scratch]
        + [pltpu.SemaphoreType.DMA((2,)), pltpu.SemaphoreType.DMA((messages,)), pltpu.SemaphoreType.DMA((messages,))],
        compiler_params=pltpu.CompilerParams(
            collective_id=cid, has_side_effects=True, vmem_limit_bytes=62 << 20
        ),
        name=name,
    )(*[v for _, v in inputs])


def layer(media, latents, bucket, cotangent, norms, w_query, w_keyvalue, w_output, w_up, w_down):
    images, per_media, _ = media.shape
    per_lat = latents.shape[1]
    rows = per_media + per_lat
    tokens = images * per_lat
    inputs = [
        ("media", media),
        ("latents", latents),
        ("cotangent", cotangent),
        ("bucket", bucket),
        ("norms", norms),
        ("w_query", w_query),
        ("w_keyvalue", w_keyvalue),
        ("w_output", w_output),
        ("w_up", w_up),
        ("w_down", w_down),
    ]
    outputs = [
        ("latents_out", (images, per_lat, 1024), BF16),
        ("grad_media", (images, per_media, 1024), BF16),
        ("grad_latents", (images, per_lat, 1024), F32),
        ("grad_pack", (32, WIDE), F32),
        ("grad_up", (32, 4096), F32),
        ("grad_down", (128, 1024), F32),
    ]
    scratch = [
        ("MED", (images, per_media, 1024), BF16),
        ("X", (images, rows, 1024), BF16),
        ("MR", (images, rows, 2), F32),
        ("PR", (images, rows, 1024), BF16),
        ("S", (2 * images, rows, 256), F32),
        ("PB", (2 * images, rows, 256), BF16),
        ("QA", (4, tokens, 512), BF16),
        ("MX", (tokens, 512), BF16),
        ("RES", (tokens, 1024), F32),
        ("MA", (4, tokens, 1024), BF16),
        ("CA", (4, tokens, 1024), BF16),
        ("UD", (4, 2, 128, 1024), BF16),
        ("UU", (4, 4, 2, 32, 1024), BF16),
        ("G", (4, 4, 2, 32, WIDE), BF16),
        ("VV", (16, 1024), F32),
        ("WS", (4, 32, 1024), BF16),
        ("LS", (4, 2 * images, 256), F32),
        ("LG", (2 * images, 256), F32),
        ("OP", (4, tokens, 512), BF16),
        ("O1", (2, tokens, 512), BF16),
        ("O2", (tokens, 512), BF16),
        ("MG", (2, per_media, 1024), BF16),
        ("ACT", (4, tokens, 1024), BF16),
        ("GG", (4, tokens, 1024), BF16),
        ("PT", (4, tokens, 1024), BF16),
        ("PY", (2, 2, tokens // 2, 1024), BF16),
        ("PX", (2, 2, tokens // 2, 1024), BF16),
        ("P2", (2, 2, tokens // 2, 1024), BF16),
        ("gD", (4, 2, 128, 1024), BF16),
        ("gU", (4, 4, 2, 32, 1024), BF16),
        ("RD", (4, 128, 1024), BF16),
        ("RU", (4, 4, 32, 1024), BF16),
        ("ZD", (4, 128, 1024), BF16),
        ("ZU", (4, 4, 32, 1024), BF16),
        ("U", (tokens, 1024), F32),
        ("GR", (tokens, 1024), F32),
        ("GS", (16, 1024), F32),
        ("GM", (4, tokens, 512), BF16),
        ("gP", (images, rows, 1024), BF16),
        ("DL", (4, 2 * images, 256), F32),
        ("QP", (4, tokens, 512), BF16),
        ("Q1", (2, tokens, 512), BF16),
        ("Q2", (tokens, 512), BF16),
        ("gA", (4, 4, 2, 32, NARROW), BF16),
        ("RA", (4, 4, 32, NARROW), BF16),
        ("RK", (4, 4, 32, 1024), BF16),
        ("WY", (2, 4, 16, WIDE), BF16),
        ("WX", (2, 4, 16, WIDE), BF16),
        ("W2", (2, 4, 16, WIDE), BF16),
        ("ZW", (4, 32, WIDE), BF16),
        ("SF", (4, 32, 1024), F32),
        ("SU", (4, 32, 1024), BF16),
        ("AU", (4, 32, 1024), BF16),
    ]
    return build(kernel_body, inputs, outputs, scratch, MESSAGES, 1, "resampler")


def solution(mesh):
    sizes = dict(mesh.shape)
    blocks = sizes["img"] // BLOCK
    names = ("img", "lat")

    def block_shard(weight):
        if blocks == 1:
            return weight
        whole = lax.all_gather(weight, names, axis=0, tiled=True)
        each = whole.shape[0] // (BLOCK * sizes["lat"])
        mine = lax.rem(lax.axis_index("img"), BLOCK) * sizes["lat"] + lax.axis_index("lat")
        return lax.dynamic_slice_in_dim(whole, mine * each, each, 0)

    def own_shard(gradient):
        if blocks == 1:
            return gradient
        each = gradient.shape[0]
        mine = lax.rem(lax.axis_index("img"), BLOCK) * sizes["lat"] + lax.axis_index("lat")
        whole = jnp.zeros((each * BLOCK * sizes["lat"],) + gradient.shape[1:], gradient.dtype)
        whole = lax.dynamic_update_slice_in_dim(whole, gradient, mine * each, 0)
        return lax.psum_scatter(whole, names, scatter_dimension=0, tiled=True)

    def on_device(
        media,
        latents,
        bucket,
        gain_media,
        shift_media,
        gain_latent,
        shift_latent,
        gain_mlp,
        shift_mlp,
        w_query,
        w_keyvalue,
        w_output,
        w_up,
        w_down,
        cotangent,
    ):
        lat = lax.axis_index("lat")
        norms = [
            block_shard(v) for v in (gain_media, shift_media, gain_latent, shift_latent, gain_mlp, shift_mlp)
        ]
        norms = jnp.pad(jnp.stack(norms), ((0, 10), (0, 0)))
        latents_out, grad_media, grad_latents, grad_pack, grad_up, grad_down = layer(
            media,
            latents,
            bucket,
            cotangent,
            norms,
            *[block_shard(v) for v in (w_query, w_keyvalue, w_output, w_up, w_down)],
        )
        norm_grads = lax.dynamic_slice_in_dim(grad_pack[0:6, GN[0] : GN[0] + GN[1]], lat * 32, 32, 1)
        grad_out = jnp.concatenate(
            [grad_pack[0:16, OUT[0] : OUT[0] + OUT[1]], grad_pack[16:32, OUT[0] : OUT[0] + OUT[1]]], axis=1
        )
        return (
            latents_out,
            grad_media.astype(F32),
            grad_latents,
            *[own_shard(norm_grads[k]) for k in range(6)],
            own_shard(grad_pack[:, QU[0] : QU[0] + QU[1]]),
            own_shard(grad_pack[:, KV[0] : KV[0] + KV[1]]),
            own_shard(grad_out),
            own_shard(grad_up),
            own_shard(grad_down),
        )

    rows = P("img", "lat", None)
    shard = P(names)
    wide = P(names, None)
    return jax.shard_map(
        on_device,
        mesh=mesh,
        in_specs=(rows, rows, P("img")) + (shard,) * 6 + (wide,) * 5 + (rows,),
        out_specs=(rows, rows, rows) + (shard,) * 6 + (wide,) * 5,
        check_vma=False,
    )
```

time: 203 us -> 172 us (0.85)
  Pallas kernels: 182 us -> 155 us
  local copies, waits for them, and re-layouts: 16.1 us -> 9.57 us
  other arithmetic: 2.18 us -> 5.12 us
    pallas_call x2 -> x1, Pallas kernels: 182 us -> 155 us  [build(): pl.pallas_call(kernel, out_shape=[jax.ShapeDtypeStruct(s, d) for _, s, d...]
    unnamed x11 -> x12, local copies, waits for them, and re-layouts: 9.42 us -> 3.1 us
    convert_element_type x0 -> x1, other arithmetic: none -> 4.49 us  [on_device(): grad_media.astype(F32)]
where the time goes in v2:
time: 172 us; the launch traced here: 170 us
  Pallas kernels  155 us (90%)
  local copies, waits for them, and re-layouts  9.57 us (6%)
  other arithmetic  5.12 us (3%)
    pallas_call x1, Pallas kernels, build(): pl.pallas_call(kernel, out_shape=[jax.ShapeDtypeStruct(s, d) for _, s, d...  155 us
    convert_element_type x1, other arithmetic, on_device(): grad_media.astype(F32)  4.49 us

profile of v2, /device:TPU:0, one launch (start us, length us, event | category | flops | bytes accessed | tf_op | source)
XLA Modules:
  0.0 170.1 jit_solution(5742391556566997776)
XLA Ops:
  0.7 0.8 stack.27
  1.4 0.6 pad.4.refs_4_
  2.0 154.8 %resampler.1 = (bf16[8,16,1024]{2,1,0:T(8,128)(2,1)}, bf16[8,144,1024]{2,1,0:T(8,128)(2,1)}, f32[8,16,1024]{2,1,0:T(8,128)}, f32[32,2176]{1,0:T(8,128)}, f32[32,4096]{1,0:T(8,128)}, /*index=5*/f32[128,1024]{1,0:T(8,128)}) custom-call(bf16[8,144,1024]{2,1,0:T(8,128)(2,1)} %refs_0_.1, bf16[8,16,1024]{2,1,0:T(8,128)(2,1)} %refs_1_.1, ...), custom_call_target="tpu_custom_call" | custom-call | tf_op jit(solution)/shard_map/resampler/pallas_call | solution.py:945
  156.8 0.7 slice.33
  157.5 0.1 constant_dynamic-slice_fusion
  157.5 0.5 slice_bitcast_fusion
  158.1 1.5 slice.40
  159.5 0.8 fusion
  160.3 1.6 slice.41
  161.9 0.6 pad_maximum_fusion
  162.5 0.0 copy-start.3
  162.5 0.0 copy-start.2
  162.5 0.0 copy-start.1
  162.5 4.5 %convert_element_type.5 = f32[8,144,1024]{2,1,0:T(8,128)} convert(bf16[8,144,1024]{2,1,0:T(8,128)(2,1)} %get-tuple-element.21) | non-fusion elementwise | flops 1179648 | bytes 7077888 | tf_op jit(solution)/shard_map/convert_element_type | solution.py:1102
  167.0 0.0 copy-done.3
  167.0 0.0 copy-start
  167.0 0.7 copy.33
  167.7 0.0 copy-done.2
  167.7 0.8 copy.34
  168.5 0.0 copy-done.1
  168.5 0.8 copy.35
  169.3 0.0 copy-done
  169.3 0.8 copy.36
Async XLA Ops:
  162.5 4.5 %copy-start.3 = (bf16[8,16,1024]{2,1,0:T(8,128)(2,1)S(1)}, bf16[8,16,1024]{2,1,0:T(8,128)(2,1)}, u32[]{:S(2)}) copy-start(bf16[8,16,1024]{2,1,0:T(8,128)(2,1)} %get-tuple-element.48) | copy-start | bytes 786436
  162.5 5.2 %copy-start.2 = (f32[8,16,1024]{2,1,0:T(8,128)S(1)}, f32[8,16,1024]{2,1,0:T(8,128)}, u32[]{:S(2)}) copy-start(f32[8,16,1024]{2,1,0:T(8,128)} %get-tuple-element.50) | copy-start | bytes 1572868
  162.5 6.0 %copy-start.1 = (f32[32,4096]{1,0:T(8,128)S(1)}, f32[32,4096]{1,0:T(8,128)}, u32[]{:S(2)}) copy-start(f32[32,4096]{1,0:T(8,128)} %get-tuple-element.60) | copy-start | bytes 1572868
  167.0 2.3 %copy-start = (f32[128,1024]{1,0:T(8,128)S(1)}, f32[128,1024]{1,0:T(8,128)}, u32[]{:S(2)}) copy-start(f32[128,1024]{1,0:T(8,128)} %get-tuple-element.61) | copy-start | bytes 1572868

commit v3 on v2

--- a/solution.py
+++ b/solution.py
@@ -25,10 +25,9 @@
 KV = (640, 1024)
 OUT = (1664, 512)
 WIDE = 2176
-GQG = (0, 640)
 GOUT = (640, 512)
 NARROW = 1152
-MESSAGES = 183
+MESSAGES = 256
 
 
 def mm(a, b):
@@ -147,7 +146,8 @@
         if self.done:
             return
         self.done = True
-        guarded(self.when, lambda: self.copy(self.src, self.dst).wait_send())
+        with jax.named_scope('S_%d' % self.k):
+            guarded(self.when, lambda: self.copy(self.src, self.dst).wait_send())
 
 
 class Post:
@@ -166,27 +166,44 @@
 
 
 class ZGather:
-    def __init__(self, post, at, view):
+    def __init__(self, post, at, view, core):
         own = view(at.z)
+        self.at = at
         self.m1 = post.msg(own, own, at.zn1, view(at.z1))
         self.m2 = post.msg(own, own, at.zn2, view(at.z2))
         self.m3 = post.msg(own, own, at.zn3, view(at.z3), when=at.mid)
         self.relay = post.msg(view(at.z2), view(at.z2), at.zn1, view(at.z3), key=self.m3.k, when=at.mid)
+        early = jnp.where(at.mid, at.z2, at.z1)
+        late = jnp.where(at.mid, at.z1, at.z2)
+        self.core = [core(zz) for zz in (at.z, early, late, at.z3)]
 
     def start(self):
-        self.m1.start()
-        self.m2.start()
-        self.m3.start()
-
-    def near(self):
-        self.m1.arrived()
+        pl.when(self.at.mid)(self.m1.start)
+        pl.when(self.at.end)(self.m2.start)
+        self.core[0].start()
 
     def far(self):
-        self.m2.arrived()
-        self.relay.start()
+        @pl.when(self.at.mid)
+        def _():
+            self.m2.arrived()
+            self.relay.start()
+            self.m3.start()
+            self.m2.start()
+
+        pl.when(self.at.end)(self.m1.start)
 
     def last(self):
+        pl.when(self.at.end)(self.m1.arrived)
+        self.core[1].start()
+        pl.when(self.at.mid)(self.m1.arrived)
+        pl.when(self.at.end)(self.m2.arrived)
+        self.core[2].start()
         self.m3.arrived()
+        self.core[3].start()
+
+    def all(self):
+        for m in self.core:
+            m.arrived()
 
 
 class PlaneGather:
@@ -211,6 +228,40 @@
     def last(self):
         self.hy.arrived()
         self.hx.arrived()
+
+
+class HalfGather:
+    def __init__(self, post, at, half):
+        x, y = at.x, at.y
+        ox, oy = 1 - x, 1 - y
+
+        def msg(part, dev, into):
+            return post.msg(part, part, dev, into)
+
+        self.x0 = msg(half(x, y, 0), at.xn, half(ox, y, 0))
+        self.y1 = msg(half(x, y, 1), at.yn, half(x, oy, 1))
+        self.x1 = msg(half(x, y, 1), at.xn, half(ox, y, 1))
+        self.y0 = msg(half(x, y, 0), at.yn, half(x, oy, 0))
+        self.hy = msg(half(ox, y, 0), at.yn, half(ox, oy, 0))
+        self.hx = msg(half(x, oy, 1), at.xn, half(ox, oy, 1))
+
+    def start(self):
+        self.x0.start()
+        self.y1.start()
+
+    def relay(self):
+        self.x0.arrived()
+        self.hy.start()
+        self.y1.arrived()
+        self.hx.start()
+
+    def rest(self):
+        self.x1.start()
+        self.y0.start()
+
+    def last(self):
+        for m in (self.x1, self.y0, self.hy, self.hx):
+            m.arrived()
 
 
 class Spread:
@@ -250,6 +301,14 @@
             self.z[k].arrived()
             self.plane[k + 1].start()
 
+    def along_z(self):
+        for m in self.z:
+            m.arrived()
+
+    def over_plane(self):
+        for g in self.plane:
+            g.start()
+
     def relay(self):
         for g in self.plane:
             g.relay()
@@ -324,6 +383,10 @@
         self.my1.start()
         self.mx1.start()
 
+    def rest(self):
+        self.my0.start()
+        self.mx0.start()
+
     def relay(self):
         self.my1.arrived()
         there = self.part(self.ox, self.y, 0)
@@ -333,8 +396,6 @@
         there = self.part(self.x, self.oy, 1)
         there[...] = (there[...].astype(F32) + self.bx(1)[...].astype(F32)).astype(BF16)
         self.f1.start()
-        self.my0.start()
-        self.mx0.start()
 
     def total(self):
         self.my0.arrived()
@@ -355,11 +416,15 @@
         self.m3 = post.msg(term(at.z3), buf(2), at.zn3, buf(2), when=at.mid)
         self.rel = post.msg(term(at.z3), buf(3), at.zn1, buf(3), when=at.end)
 
-    def start(self):
+    def start_last(self):
         self.rel.start()
+        self.m3.start()
+
+    def start_far(self):
         pl.when(self.at.end)(self.m2.start)
+
+    def start_near(self):
         self.m1.start()
-        self.m3.start()
 
     def relay(self):
         @pl.when(self.at.mid)
@@ -379,6 +444,26 @@
         def _():
             self.m3.arrived()
             out[...] += self.buf(2)[...].astype(F32)
+
+
+class ZDirect:
+    def __init__(self, post, at, term, buf):
+        self.at, self.term, self.buf = at, term, buf
+        self.msgs = [
+            post.msg(term(zz), buf(k), dev, buf(k))
+            for k, (zz, dev) in enumerate(((at.z1, at.zn1), (at.z2, at.zn2), (at.z3, at.zn3)))
+        ]
+
+    def start(self):
+        for m in self.msgs[::-1]:
+            m.start()
+
+    def total(self, out):
+        value = self.term(self.at.z)[...].astype(F32)
+        for k, m in enumerate(self.msgs):
+            m.arrived()
+            value = value + self.buf(k)[...].astype(F32)
+        out[...] = value
 
 
 class Collect:
@@ -397,7 +482,7 @@
             lambda k: bx.at[k, :, :, self.there],
             lambda k: b2.at[k, :, :, self.there],
         )
-        self.z = ZReduce(
+        self.z = ZDirect(
             post, at, lambda zz: near.at[zz, at.p, :, self.lanes], lambda k: bz.at[k, :, self.there]
         )
 
@@ -414,6 +499,7 @@
 
         lax.fori_loop(0, 4, add, 0)
         self.plane.start()
+        self.plane.rest()
 
     def relay(self):
         self.plane.relay()
@@ -424,8 +510,47 @@
         self.near[:, self.at.p, 16:32, self.lanes] = high.astype(BF16)
         self.z.start()
 
-    def z_relay(self):
-        self.z.relay()
+    def total(self, out):
+        self.z.total(out)
+
+
+class CollectNorms:
+    def __init__(self, post, at, grads, near, by, bx, b2, bz, span):
+        self.at, self.grads, self.near, self.lanes = at, grads, near, cols(span)
+        low = pl.ds(0, 16)
+
+        def part(p):
+            return near.at[:, p, low, self.lanes]
+
+        theirs = grads.at[:, :, 1 - at.c, low, self.lanes]
+        here = near.at[:, :, low, self.lanes]
+        self.core = post.msg(theirs, here, at.core, here)
+        self.bufs = [b.at[0, :, :, self.lanes] for b in (bx, by, b2)]
+        self.plane = [
+            post.msg(part(p), buf, dev, buf)
+            for p, buf, dev in zip((at.px, at.py, at.pd), self.bufs, (at.xn, at.yn, at.diag))
+        ]
+        self.z = ZDirect(
+            post, at, lambda zz: near.at[zz, at.p, low, self.lanes], lambda k: bz.at[k, low, self.lanes]
+        )
+
+    def start(self):
+        self.core.start()
+
+    def into_plane(self):
+        self.core.arrived()
+        mine = self.grads[:, :, self.at.c, 0:16, self.lanes].astype(F32)
+        self.near[:, :, 0:16, self.lanes] = (self.near[:, :, 0:16, self.lanes].astype(F32) + mine).astype(BF16)
+        for m in self.plane:
+            m.start()
+
+    def into_z(self):
+        total = self.near[:, self.at.p, 0:16, self.lanes].astype(F32)
+        for m, buf in zip(self.plane, self.bufs):
+            m.arrived()
+            total = total + buf[...].astype(F32)
+        self.near[:, self.at.p, 0:16, self.lanes] = total.astype(BF16)
+        self.z.start()
 
     def total(self, out):
         self.z.total(out)
@@ -447,6 +572,13 @@
     out = jnp.where(lane == 0, wide[0:64], 0.0)
     for h in range(1, 4):
         out = out + jnp.where(lane == h, wide[64 * h : 64 * h + 64], 0.0)
+    return out
+
+
+def pick(values, k):
+    out = values[-1]
+    for i in range(len(values) - 2, -1, -1):
+        out = jnp.where(k == i, values[i], out)
     return out
 
 
@@ -468,7 +600,8 @@
     R.G[at.z, at.p, at.c, :, cols(KV)] = R.w_keyvalue[...]
     R.G[at.z, at.p, at.c, 0:16, cols(OUT)] = R.w_output[:, 0:512]
     R.G[at.z, at.p, at.c, 16:32, cols(OUT)] = R.w_output[:, 512:1024]
-    norms = R.norms[...].astype(F32)
+    norms = [ref[...].astype(F32).reshape(1, 32) for ref in (R.n0, R.n1, R.n2, R.n3, R.n4, R.n5)]
+    norms = jnp.concatenate(norms + [jnp.zeros((10, 32), F32)], axis=0)
     norms = jnp.concatenate([norms, norms, norms, norms], axis=1)
     lanes = lax.div(lax.broadcasted_iota(jnp.int32, (16, 128), 1), 32)
     R.G[at.z, at.p, at.c, 0:16, cols(GN)] = jnp.where(lanes == at.l, norms, 0.0).astype(BF16)
@@ -486,28 +619,31 @@
     with jax.named_scope("greet"):
         at.greet()
 
-    first = Spread(post, at, R.G, (0, 1152))
+    first = Spread(post, at, R.G, (0, 640))
+    keys = Spread(post, at, R.G, KEY)
     second = Spread(post, at, R.G, VAL)
     third = Spread(post, at, R.G, OUT)
     up = [
         post.msg(R.WS.at[there], R.UU.at[at.z, at.p, at.c], dev, R.UU.at[at.z, there, at.c])
         for there, dev in ((at.px, at.xn), (at.py, at.yn), (at.pd, at.diag))
     ]
-    d_z = ZGather(post, at, lambda zz: R.UD.at[zz, at.c])
-    u_z = ZGather(post, at, lambda zz: R.UU.at[zz, :, at.c])
-    d_c = [post.msg(R.UD.at[zz, at.c], R.UD.at[zz, at.c], at.core, R.UD.at[zz, 1 - at.c]) for zz in zs]
-    u_c = [
-        post.msg(R.UU.at[zz, :, at.c], R.UU.at[zz, :, at.c], at.core, R.UU.at[zz, :, 1 - at.c]) for zz in zs
-    ]
-    cot = PlaneGather(
+    d_z = ZGather(
         post,
         at,
-        lambda x, y: R.CA.at[x * 2 + y],
-        lambda x, y, h: R.CA.at[x * 2 + y, pl.ds(h * half_rows, half_rows)],
+        lambda zz: R.UD.at[zz, at.c],
+        lambda zz: post.msg(R.UD.at[zz, at.c], R.UD.at[zz, at.c], at.core, R.UD.at[zz, 1 - at.c]),
     )
+    u_z = ZGather(
+        post,
+        at,
+        lambda zz: R.UU.at[zz, :, at.c],
+        lambda zz: post.msg(R.UU.at[zz, :, at.c], R.UU.at[zz, :, at.c], at.core, R.UU.at[zz, :, 1 - at.c]),
+    )
+    cot = HalfGather(post, at, lambda x, y, h: R.CA.at[x * 2 + y, pl.ds(h * half_rows, half_rows)])
 
     first.start()
     first.plane[0].start()
+    keys.plane[0].start()
     for m in up:
         m.start()
 
@@ -522,19 +658,15 @@
 
     media_in.wait()
     loop(images, stats)
+    keys.start()
     first.into_plane()
     second.start()
+    first.relay()
+    keys.into_plane()
+    third.start()
+    first.to_core()
     d_z.start()
-    d_c[0].start()
-    first.relay()
-    for m in up:
-        m.arrived()
-    u_z.start()
-    u_c[0].start()
-    first.to_core()
-    second.plane[0].start()
-    second.into_plane()
-    third.start()
+    keys.relay()
     first.arrived()
 
     for i in range(8):
@@ -551,14 +683,16 @@
     R.QA[at.l] = mm(latent_low, R.G[:, :, :, :, cols(QU)].reshape(1024, 512)).astype(BF16)
     q_all = LatGather(post, at, lambda l: R.QA.at[l])
     q_all.start()
+    second.plane[0].mx.start()
 
     def low(g, carry):
         normed = (R.MED[g].astype(F32) - R.MR[g, 0:per_media, 0:1]) * R.MR[g, 0:per_media, 1:2]
         R.X[g, 0:per_media, :] = (normed * R.VV[0:1, :] + R.VV[1:2, :]).astype(BF16)
         return carry
 
+    keys.to_core()
     loop(images, low)
-    second.relay()
+    keys.arrived()
 
     def pairs(n, carry):
         weight = R.G[:, :, :, :, pl.ds(pl.multiple_of(KV[0] + n * 256, 128), 256)].reshape(1024, 256)
@@ -568,9 +702,14 @@
 
     loop((0, 2), pairs)
     q_all.relay()
-    second.to_core()
-    third.plane[0].start()
-    third.into_plane()
+    second.along_z()
+    second.plane[0].my.start()
+    for g in second.plane[1:]:
+        g.start()
+    for m in up:
+        m.arrived()
+    u_z.start()
+    d_z.far()
     q_all.last()
 
     mask = head_mask()
@@ -591,16 +730,22 @@
         return carry
 
     loop(images, score)
+    second.relay()
     ls = [
         post.msg(R.LS.at[at.l], R.LS.at[at.l], dev, R.LS.at[there])
         for there, dev in ((at.ly, at.yn), (at.ld, at.ycore), (at.lc, at.core))
     ]
     for m in ls:
         m.start()
+    third.along_z()
+    third.over_plane()
+    second.to_core()
     second.arrived()
     loop((2, 4), pairs)
     third.relay()
     cot.start()
+    cot.rest()
+    u_z.far()
     for m in ls:
         m.arrived()
     top = jnp.maximum(jnp.maximum(R.LS[0], R.LS[1]), jnp.maximum(R.LS[2], R.LS[3]))
@@ -622,16 +767,8 @@
     loop(images, mix)
     mixed = LatReduce(post, at, R.OP, R.O1, R.O2)
     mixed.start()
-    d_z.near()
-    d_c[1].start()
-    u_z.near()
-    u_c[1].start()
     mixed.relay()
     third.to_core()
-    d_z.far()
-    d_c[2].start()
-    u_z.far()
-    u_c[2].start()
     cot.relay()
     third.arrived()
     R.MX[...] = mixed.total().astype(BF16)
@@ -642,39 +779,73 @@
     R.RES[:, 512:1024] = latents[:, 512:1024] + mm(R.MX[...], right)
     mean, rstd = normal(R.RES[...])
     R.MA[at.p] = ((R.RES[...] - mean) * rstd * R.VV[4:5, :] + R.VV[5:6, :]).astype(BF16)
-    mlp = PlaneGather(
-        post,
-        at,
-        lambda x, y: R.MA.at[x * 2 + y],
-        lambda x, y, h: R.MA.at[x * 2 + y, pl.ds(h * half_rows, half_rows)],
-    )
+    mlp = HalfGather(post, at, lambda x, y, h: R.MA.at[x * 2 + y, pl.ds(h * half_rows, half_rows)])
     mlp.start()
+    mlp.rest()
     mlp.relay()
     cot.last()
     d_z.last()
     u_z.last()
-    d_c[3].start()
-    u_c[3].start()
-    for m in d_c + u_c:
-        m.arrived()
+    d_z.all()
+
+    def cot_back(f, carry):
+        made = mm_nt(R.CA[...].reshape(4 * tokens, 1024), R.UD[f].reshape(256, 1024))
+        R.S[pl.ds(4 * f, 4), 0:tokens, :] = made.reshape(4, tokens, 256)
+        return carry
+
+    loop(4, cot_back)
+    u_z.all()
     mlp.last()
 
-    def gates(f, carry):
+    def gates(k, carry):
+        f = pick(zs, k)
         gate = mm(R.MA[...].reshape(4 * tokens, 1024), R.UU[:, :, :, :, span256(f)].reshape(1024, 256))
-        back = mm_nt(R.CA[...].reshape(4 * tokens, 1024), R.UD[f].reshape(256, 1024))
+        back = R.S[pl.ds(4 * f, 4), 0:tokens, :].reshape(4 * tokens, 256)
         phi = 0.5 * (1.0 + lax.erf(gate * 0.7071067811865476))
         R.ACT[:, :, span256(f)] = (gate * phi).astype(BF16).reshape(4, tokens, 256)
         slope = phi + gate * jnp.exp(-0.5 * gate * gate) * 0.3989422804014327
         R.GG[:, :, span256(f)] = (back * slope).astype(BF16).reshape(4, tokens, 256)
         return carry
 
-    loop(4, gates)
-
     def norm_parts(n, carry):
         made = mm_nt(R.GG[...].reshape(4 * tokens, 1024), R.UU[n].reshape(256, 1024))
         R.PT[:, :, span256(n)] = made.astype(BF16).reshape(4, tokens, 256)
         return carry
 
+    gd_c = [post.msg(R.gD.at[zz, 1 - at.c], R.RD.at[zz], at.core, R.RD.at[zz]) for zz in zs]
+    gu_c = [post.msg(R.gU.at[zz, :, 1 - at.c], R.RU.at[zz], at.core, R.RU.at[zz]) for zz in zs]
+    gd_z = ZReduce(post, at, lambda zz: R.RD.at[zz], lambda k: R.ZD.at[k])
+    gu_z = ZReduce(post, at, lambda zz: R.RU.at[zz], lambda k: R.ZU.at[k])
+
+    def down_grads(k, carry):
+        f = pick(zs, k)
+        act = R.ACT[:, :, span256(f)].reshape(4 * tokens, 256)
+        R.gD[f] = mm_tn(act, R.CA[...].reshape(4 * tokens, 1024)).astype(BF16).reshape(2, 128, 1024)
+        return carry
+
+    def up_grads(k, carry):
+        n = pick(zs, k)
+        low_rows = R.MA[:, :, span256(n)].reshape(4 * tokens, 256)
+        made = mm_tn(low_rows, R.GG[...].reshape(4 * tokens, 1024)).astype(BF16)
+        R.gU[n] = made.reshape(4, 2, 32, 1024)
+        return carry
+
+    def add_d(k):
+        gd_c[k].arrived()
+        R.RD[zs[k]] = (R.RD[zs[k]].astype(F32) + R.gD[zs[k], at.c].astype(F32)).astype(BF16)
+
+    def add_u(k):
+        gu_c[k].arrived()
+        R.RU[zs[k]] = (R.RU[zs[k]].astype(F32) + R.gU[zs[k], :, at.c].astype(F32)).astype(BF16)
+
+    loop((3, 4), gates)
+    loop((3, 4), down_grads)
+    gd_c[3].start()
+    loop((0, 3), gates)
+    loop((3, 4), up_grads)
+    gu_c[3].start()
+    add_d(3)
+    gd_z.start_last()
     loop(4, norm_parts)
     back = PlaneReduce(
         post,
@@ -686,34 +857,27 @@
     )
     back.start()
 
-    def down_grads(f, carry):
-        act = R.ACT[:, :, span256(f)].reshape(4 * tokens, 256)
-        R.gD[f] = mm_tn(act, R.CA[...].reshape(4 * tokens, 1024)).astype(BF16).reshape(2, 128, 1024)
-        return carry
-
-    loop(4, down_grads)
-    gd_c = post.msg(R.gD.at[:, 1 - at.c], R.RD, at.core, R.RD)
-    gd_c.start()
+    add_u(3)
+    gu_z.start_last()
+    loop((2, 3), down_grads)
+    gd_c[2].start()
+    loop((2, 3), up_grads)
+    gu_c[2].start()
+    back.rest()
+    loop((0, 2), down_grads)
+    gd_c[1].start()
+    gd_c[0].start()
+    add_d(2)
+    gd_z.start_far()
+    add_u(2)
+    gu_z.start_far()
     back.relay()
-
-    def up_grads(n, carry):
-        low_rows = R.MA[:, :, span256(n)].reshape(4 * tokens, 256)
-        made = mm_tn(low_rows, R.GG[...].reshape(4 * tokens, 1024)).astype(BF16)
-        R.gU[n] = made.reshape(4, 2, 32, 1024)
-        return carry
-
-    loop(4, up_grads)
-    gu_c = post.msg(R.gU.at[:, :, 1 - at.c], R.RU, at.core, R.RU)
-    gu_c.start()
-    gd_c.arrived()
-
-    def add_d(zz, carry):
-        R.RD[zz] = (R.RD[zz].astype(F32) + R.gD[zz, at.c].astype(F32)).astype(BF16)
-        return carry
-
-    loop(4, add_d)
-    gd_z = ZReduce(post, at, lambda zz: R.RD.at[zz], lambda k: R.ZD.at[k])
-    gd_z.start()
+    loop((0, 2), up_grads)
+    gu_c[1].start()
+    gu_c[0].start()
+    add_d(1)
+    gd_z.start_near()
+    add_d(0)
 
     def out_parts(n, carry):
         made = mm(R.ACT[...].reshape(4 * tokens, 1024), R.UD[:, :, :, span256(n)].reshape(1024, 256))
@@ -721,15 +885,10 @@
         return carry
 
     loop(4, out_parts)
-    gu_c.arrived()
-
-    def add_u(zz, carry):
-        R.RU[zz] = (R.RU[zz].astype(F32) + R.gU[zz, :, at.c].astype(F32)).astype(BF16)
-        return carry
-
-    loop(4, add_u)
-    gu_z = ZReduce(post, at, lambda zz: R.RU.at[zz], lambda k: R.ZU.at[k])
-    gu_z.start()
+    add_u(1)
+    gu_z.start_near()
+    add_u(0)
+
     out = PlaneReduce(
         post,
         at,
@@ -755,6 +914,8 @@
     R.GM[at.l] = (mm_nt(grad_attn[:, 0:512], left) + mm_nt(grad_attn[:, 512:1024], right)).astype(BF16)
     gm = LatGather(post, at, lambda l: R.GM.at[l])
     gm.start()
+    out.mx1.start()
+    out.mx0.start()
     grad_attn = R.GR[...].astype(BF16)
     made = mm_tn(R.MX[...], grad_attn[:, 0:512]).astype(BF16)
     R.gA[:, :, :, 0:16, cols(GOUT)] = made.reshape(4, 4, 2, 16, 512)
@@ -764,6 +925,8 @@
     w_out.start()
     gm.relay()
     gm.last()
+    out.my1.start()
+    out.my0.start()
 
     def grad_probs(g, carry):
         lat_rows = pl.ds(pl.multiple_of(g * per_lat, per_lat), per_lat)
@@ -793,10 +956,14 @@
         R.gU[lax.rem(n, 4), :, :, :, lanes] = made.reshape(4, 2, 32, 512)
         return carry
 
-    gu_c.sent()
+    for m in gu_c:
+        m.sent()
     loop((4, 8), kv_grads)
     w_val = Collect(post, at, R.gU, R.RK, R.WY, R.WX, R.W2, R.ZW, (512, 512), VAL)
     w_val.start()
+    gd_z.relay()
+    gu_z.relay()
+    out.relay()
     for m in dl:
         m.arrived()
     R.LG[...] = R.DL[0] + R.DL[1] + R.DL[2] + R.DL[3]
@@ -822,11 +989,6 @@
     w_key = Collect(post, at, R.gU, R.RK, R.WY, R.WX, R.W2, R.ZW, (0, 512), KEY)
     w_key.start()
     gq.relay()
-    gd_z.relay()
-    gu_z.relay()
-    w_out.into_z()
-    w_val.relay()
-    w_key.into_plane()
 
     def media_copy(h):
         return pltpu.make_async_copy(R.MG, R.grad_media.at[pl.ds(h * 2, 2)], R.local.at[0])
@@ -847,37 +1009,48 @@
         R.GS[1:2, :] += jnp.sum(flat(upstream), axis=0, keepdims=True)
         return carry
 
-    loop((0, images // 4), media_grads)
-    w_val.into_z()
+    loop((0, 1), media_grads)
+    w_key.into_plane()
+    loop((1, 2), media_grads)
+    w_val.relay()
+    w_out.into_z()
+    loop((2, 3), media_grads)
+    with jax.named_scope("query"):
+        grad_query = gq.total().astype(BF16)
+        latent_low = flat(R.X[:, per_media:rows, :])
+        R.gA[:, :, :, :, cols(QU)] = mm_tn(latent_low, grad_query).astype(BF16).reshape(4, 4, 2, 32, 512)
+        R.GQ[...] = grad_query
+    w_que = Collect(post, at, R.gA, R.RA, R.WY, R.WX, R.W2, R.ZW, QU, QU)
+    w_que.start()
+    loop((3, 4), media_grads)
     w_key.relay()
-    w_out.z_relay()
-    loop((images // 4, images // 2), media_grads)
+    w_que.into_plane()
     media_copy(images // 2 - 1).wait()
-    w_val.z_relay()
-
-    grad_query = gq.total().astype(BF16)
-    latent_low = flat(R.X[:, per_media:rows, :])
-    upstream = R.U[...] + mm_nt(grad_query, R.G[:, :, :, :, cols(QU)].reshape(1024, 512))
+
+    upstream = R.U[...] + mm_nt(R.GQ[...], R.G[:, :, :, :, cols(QU)].reshape(1024, 512))
     rstd = flat(R.MR[:, per_media:rows, 1:2])
     normed = (flat(R.latents[...]).astype(F32) - flat(R.MR[:, per_media:rows, 0:1])) * rstd
-    R.grad_latents[...] = (R.GR[...] + norm_back(upstream, normed, rstd, R.VV[2:3, :])).reshape(
-        images, per_lat, 1024
-    )
     R.GS[2:3, :] = jnp.sum(upstream * normed, axis=0, keepdims=True)
     R.GS[3:4, :] = jnp.sum(upstream, axis=0, keepdims=True)
-    R.gA[:, :, :, :, cols(QU)] = mm_tn(latent_low, grad_query).astype(BF16).reshape(4, 4, 2, 32, 512)
     for i in range(8):
         piece = R.GS[:, 128 * i : 128 * i + 128].astype(BF16)
         for p in (2 * (i % 2), 2 * (i % 2) + 1):
             for c in range(2):
                 R.gA[i // 2, p, c, 0:16, cols(GN)] = piece
                 R.gA[i // 2, p, c, 16:32, cols(GN)] = jnp.zeros((16, 128), BF16)
-    w_qg = Collect(post, at, R.gA, R.RA, R.WY, R.WX, R.W2, R.ZW, GQG, GQG)
-    w_qg.start()
-    w_key.into_z()
-    w_qg.into_plane()
-    out.start()
-    gd_z.total(R.grad_down)
+    w_nrm = CollectNorms(post, at, R.gA, R.RA, R.WY, R.WX, R.W2, R.ZW, GN)
+    w_nrm.start()
+    w_que.relay()
+    with jax.named_scope('T_w_val_into_z'):
+        w_val.into_z()
+    w_nrm.into_plane()
+    with jax.named_scope('T_w_key_into_z'):
+        w_key.into_z()
+    R.grad_latents[...] = (R.GR[...] + norm_back(upstream, normed, rstd, R.VV[2:3, :])).reshape(
+        images, per_lat, 1024
+    )
+    with jax.named_scope('T_gd_z_total'):
+        gd_z.total(R.grad_down)
     gu_z.total(R.SF)
     R.SU[...] = R.SF[...].astype(BF16)
     R.AU[at.p] = R.SU[at.p]
@@ -887,18 +1060,22 @@
     ]
     for m in up:
         m.start()
-    w_qg.relay()
-    out.relay()
-    w_key.z_relay()
-    w_out.total(R.grad_pack.at[:, cols(OUT)])
-    w_val.total(R.grad_pack.at[:, cols(VAL)])
-    w_qg.into_z()
-    w_qg.z_relay()
+    with jax.named_scope('T_w_nrm_into_z'):
+        w_nrm.into_z()
     low_part, high_part = out.total()
     R.latents_out[...] = jnp.concatenate(
         [R.RES[0:half_rows] + low_part, R.RES[half_rows:] + high_part], axis=0
     ).astype(BF16).reshape(images, per_lat, 1024)
-    w_key.total(R.grad_pack.at[:, cols(KEY)])
+    with jax.named_scope('T_w_que_into_z'):
+        w_que.into_z()
+    with jax.named_scope('T_w_out_total'):
+        w_out.total(R.grad_pack.at[:, cols(OUT)])
+    with jax.named_scope('T_w_val_total'):
+        w_val.total(R.grad_pack.at[:, cols(VAL)])
+    with jax.named_scope('T_w_key_total'):
+        w_key.total(R.grad_pack.at[:, cols(KEY)])
+    with jax.named_scope('T_w_nrm_total'):
+        w_nrm.total(R.grad_pack.at[0:16, cols(GN)])
     for m in up:
         m.arrived()
     for p in range(4):
@@ -907,7 +1084,8 @@
                 R.grad_up[:, 128 * (8 * zz + 2 * p + cc) : 128 * (8 * zz + 2 * p + cc) + 128] = R.AU[
                     p, :, 128 * (2 * zz + cc) : 128 * (2 * zz + cc) + 128
                 ].astype(F32)
-    w_qg.total(R.grad_pack.at[:, cols(GQG)])
+    with jax.named_scope('T_w_que_total'):
+        w_que.total(R.grad_pack.at[:, cols(QU)])
 
 
 def loop(bounds, step):
@@ -937,7 +1115,7 @@
         post = Post(refs[-2], refs[-1])
         kernel_body(at, post, R)
         post.drain()
-        assert post.count == messages, post.count
+        assert post.count <= messages, post.count
 
     specs = [
         pl.BlockSpec(memory_space=PLACES.get(n, pltpu.VMEM)) for n in in_names
@@ -958,7 +1136,7 @@
     )(*[v for _, v in inputs])
 
 
-def layer(media, latents, bucket, cotangent, norms, w_query, w_keyvalue, w_output, w_up, w_down):
+def layer(media, latents, bucket, cotangent, n0, n1, n2, n3, n4, n5, w_query, w_keyvalue, w_output, w_up, w_down):
     images, per_media, _ = media.shape
     per_lat = latents.shape[1]
     rows = per_media + per_lat
@@ -968,7 +1146,12 @@
         ("latents", latents),
         ("cotangent", cotangent),
         ("bucket", bucket),
-        ("norms", norms),
+        ("n0", n0),
+        ("n1", n1),
+        ("n2", n2),
+        ("n3", n3),
+        ("n4", n4),
+        ("n5", n5),
         ("w_query", w_query),
         ("w_keyvalue", w_keyvalue),
         ("w_output", w_output),
@@ -1027,18 +1210,66 @@
         ("QP", (4, tokens, 512), BF16),
         ("Q1", (2, tokens, 512), BF16),
         ("Q2", (tokens, 512), BF16),
+        ("GQ", (tokens, 512), BF16),
         ("gA", (4, 4, 2, 32, NARROW), BF16),
         ("RA", (4, 4, 32, NARROW), BF16),
         ("RK", (4, 4, 32, 1024), BF16),
         ("WY", (2, 4, 16, WIDE), BF16),
         ("WX", (2, 4, 16, WIDE), BF16),
         ("W2", (2, 4, 16, WIDE), BF16),
-        ("ZW", (4, 32, WIDE), BF16),
+        ("ZW", (3, 32, WIDE), BF16),
         ("SF", (4, 32, 1024), F32),
         ("SU", (4, 32, 1024), BF16),
         ("AU", (4, 32, 1024), BF16),
     ]
     return build(kernel_body, inputs, outputs, scratch, MESSAGES, 1, "resampler")
+
+
+def finish_body(
+    out_in, media_in, latents_in, pack, up_in, down_in, out, media, latents, n0, n1, n2, n3, n4, n5, wq, wkv, wo, wu, wd
+):
+    rows = wo.shape[0]
+    media[...] = media_in[...].astype(F32)
+
+    @pl.when(pl.program_id(0) == 0)
+    def _():
+        out[...] = out_in[...]
+        latents[...] = latents_in[...]
+        wu[...] = up_in[...]
+        wd[...] = down_in[...]
+        wq[...] = pack[:, cols(QU)]
+        wkv[...] = pack[:, cols(KV)]
+        wo[:, 0:512] = pack[0:rows, cols(OUT)]
+        wo[:, 512:1024] = pack[rows : 2 * rows, cols(OUT)]
+        mine = pltpu.roll(pack[0:8, cols(GN)], lax.rem(128 - 32 * lax.axis_index("lat"), 128), 1)
+        for k, ref in enumerate((n0, n1, n2, n3, n4, n5)):
+            ref[...] = mine[k, 0:32]
+
+
+def finish(latents_out, grad_media, grad_latents, grad_pack, grad_up, grad_down):
+    images, per_media, width = grad_media.shape
+    block = pl.BlockSpec((2, per_media, width), lambda g: (g, 0, 0))
+
+    def whole(shape):
+        return pl.BlockSpec(shape, lambda g: (0,) * len(shape))
+
+    shapes = [
+        jax.ShapeDtypeStruct(latents_out.shape, BF16),
+        jax.ShapeDtypeStruct(grad_media.shape, F32),
+        jax.ShapeDtypeStruct(grad_latents.shape, F32),
+    ] + [
+        jax.ShapeDtypeStruct(shape, F32)
+        for shape in ((32,),) * 6 + ((32, 512), (32, 1024), (16, 1024), grad_up.shape, grad_down.shape)
+    ]
+    values = (latents_out, grad_media, grad_latents, grad_pack, grad_up, grad_down)
+    return pl.pallas_call(
+        finish_body,
+        grid=(images // 2,),
+        out_shape=shapes,
+        in_specs=[block if k == 1 else whole(v.shape) for k, v in enumerate(values)],
+        out_specs=[block if k == 1 else whole(v.shape) for k, v in enumerate(shapes)],
+        name="finish",
+    )(*values)
 
 
 def solution(mesh):
@@ -1080,34 +1311,11 @@
         w_down,
         cotangent,
     ):
-        lat = lax.axis_index("lat")
-        norms = [
-            block_shard(v) for v in (gain_media, shift_media, gain_latent, shift_latent, gain_mlp, shift_mlp)
-        ]
-        norms = jnp.pad(jnp.stack(norms), ((0, 10), (0, 0)))
-        latents_out, grad_media, grad_latents, grad_pack, grad_up, grad_down = layer(
-            media,
-            latents,
-            bucket,
-            cotangent,
-            norms,
-            *[block_shard(v) for v in (w_query, w_keyvalue, w_output, w_up, w_down)],
-        )
-        norm_grads = lax.dynamic_slice_in_dim(grad_pack[0:6, GN[0] : GN[0] + GN[1]], lat * 32, 32, 1)
-        grad_out = jnp.concatenate(
-            [grad_pack[0:16, OUT[0] : OUT[0] + OUT[1]], grad_pack[16:32, OUT[0] : OUT[0] + OUT[1]]], axis=1
-        )
-        return (
-            latents_out,
-            grad_media.astype(F32),
-            grad_latents,
-            *[own_shard(norm_grads[k]) for k in range(6)],
-            own_shard(grad_pack[:, QU[0] : QU[0] + QU[1]]),
-            own_shard(grad_pack[:, KV[0] : KV[0] + KV[1]]),
-            own_shard(grad_out),
-            own_shard(grad_up),
-            own_shard(grad_down),
-        )
+        norms = (gain_media, shift_media, gain_latent, shift_latent, gain_mlp, shift_mlp)
+        weights = (w_query, w_keyvalue, w_output, w_up, w_down)
+        made = layer(media, latents, bucket, cotangent, *[block_shard(v) for v in norms + weights])
+        made = finish(*made)
+        return (*made[:3], *[own_shard(v) for v in made[3:]])
 
     rows = P("img", "lat", None)
     shard = P(names)

time: 172 us -> 134 us (0.78); the launches traced: 170 us -> 134 us
  Pallas kernels: 155 us -> 133 us
  local copies, waits for them, and re-layouts: 9.57 us -> 0 us
  other arithmetic: 5.12 us -> 0 us
    pallas_call x1, Pallas kernels: 155 us -> 128 us  [build(): pl.pallas_call(kernel, out_shape=[jax.ShapeDtypeStruct(s, d) for _, s, d...]
    pallas_call x0 -> x1, Pallas kernels: none -> 5.93 us  [finish(): pl.pallas_call(finish_body, grid=(images // 2,), out_shape=shapes, in_spe...]
    slice x4 -> x0, local copies, waits for them, and re-layouts: 4.5 us -> none  [the longest x1 1.57 us: on_device(): grad_pack[:, KV[0]:KV[0] + KV[1]]]
    convert_element_type x1 -> x0, other arithmetic: 4.49 us -> none  [on_device(): grad_media.astype(F32)]
    unnamed x12 -> x0, local copies, waits for them, and re-layouts: 3.1 us -> none
where the time goes in v3:
time: 134 us
  Pallas kernels  133 us (99%)
    pallas_call x1, Pallas kernels, build(): pl.pallas_call(kernel, out_shape=[jax.ShapeDtypeStruct(s, d) for _, s, d...  128 us
    pallas_call x1, Pallas kernels, finish(): pl.pallas_call(finish_body, grid=(images // 2,), out_shape=shapes, in_spe...  5.93 us

profile of v3, /device:TPU:0, one launch (start us, length us, event | category | flops | bytes accessed | tf_op | source)
XLA Modules:
  0.0 134.3 jit_solution(10425853072471852239)
XLA Ops:
  0.7 127.5 %resampler.1 = (bf16[8,16,1024]{2,1,0:T(8,128)(2,1)}, bf16[8,144,1024]{2,1,0:T(8,128)(2,1)}, f32[8,16,1024]{2,1,0:T(8,128)}, f32[32,2176]{1,0:T(8,128)}, f32[32,4096]{1,0:T(8,128)}, /*index=5*/f32[128,1024]{1,0:T(8,128)}) custom-call(bf16[8,144,1024]{2,1,0:T(8,128)(2,1)} %refs_0_.1, bf16[8,16,1024]{2,1,0:T(8,128)(2,1)} %refs_1_.1, ...), custom_call_target="tpu_custom_call" | custom-call | tf_op jit(solution)/shard_map/resampler/pallas_call | solution.py:1123
  128.2 5.9 %finish.1 = (bf16[8,16,1024]{2,1,0:T(8,128)(2,1)}, f32[8,144,1024]{2,1,0:T(8,128)}, f32[8,16,1024]{2,1,0:T(8,128)}, f32[32]{0:T(128)}, f32[32]{0:T(128)}, /*inde...) custom-call(bf16[8,16,1024]{2,1,0:T(8,128)(2,1)} %get-tuple-element., ...), custom_call_target="tpu_custom_call" | custom-call | tf_op jit(solution)/shard_map/finish/pallas_call | solution.py:1265

commit v4 on v3

v4 whole, which is shorter than its diff:
```python
import jax
import jax.numpy as jnp
from jax import lax
from jax.experimental import pallas as pl
from jax.experimental.pallas import tpu as pltpu
from jax.sharding import PartitionSpec as P

MESH = pl.DeviceIdType.MESH
BF16 = jnp.bfloat16
F32 = jnp.float32

SHORT = 256
LONG = 576
HEADS = 8
EPS = 1e-05
SCALE = 0.125
NEG = -1e30

BLOCK = 8

QU = (0, 512)
GN = (512, 128)
KEY = (640, 512)
VAL = (1152, 512)
KV = (640, 1024)
OUT = (1664, 512)
WIDE = 2176
GOUT = (640, 512)
NARROW = 1152
MESSAGES = (106, 132)


def mm(a, b):
    return lax.dot_general(a, b, (((1,), (0,)), ((), ())), preferred_element_type=F32)


def mm_nt(a, b):
    return lax.dot_general(a, b, (((1,), (1,)), ((), ())), preferred_element_type=F32)


def mm_tn(a, b):
    return lax.dot_general(a, b, (((0,), (0,)), ((), ())), preferred_element_type=F32)


def cols(span):
    return pl.ds(span[0], span[1])


def flat(values):
    return values.reshape(-1, values.shape[-1])


def normal(values):
    mean = jnp.mean(values, axis=-1, keepdims=True)
    centred = values - mean
    spread = jnp.mean(centred * centred, axis=-1, keepdims=True)
    return mean, lax.rsqrt(spread + EPS)


def norm_back(upstream, normed, rstd, gain):
    scaled = upstream * gain
    first = jnp.mean(scaled, axis=-1, keepdims=True)
    second = jnp.mean(scaled * normed, axis=-1, keepdims=True)
    return (scaled - first - normed * second) * rstd


class Place:
    def __init__(self):
        img = lax.axis_index("img")
        lat = lax.axis_index("lat")
        self.i = lax.rem(img, BLOCK)
        self.base = img - self.i
        self.z = lax.div(self.i, 2)
        self.x = lax.rem(self.i, 2)
        self.l = lat
        self.y = lax.div(lat, 2)
        self.c = lax.rem(lat, 2)
        self.z1 = self.z + 1 - 2 * lax.rem(self.z, 2)
        self.z2 = lax.rem(self.z + 2, 4)
        self.z3 = 3 - self.z
        self.mid = jnp.logical_or(self.z == 1, self.z == 2)
        self.zs = (self.z, self.z1, self.z2, self.z3)
        self.end = jnp.logical_or(self.z == 0, self.z == 3)
        self.p = self.x * 2 + self.y
        self.q = self.z * 4 + self.p
        self.px = (1 - self.x) * 2 + self.y
        self.py = self.x * 2 + 1 - self.y
        self.pd = 3 - self.p
        self.lc = self.y * 2 + 1 - self.c
        self.ly = (1 - self.y) * 2 + self.c
        self.ld = 3 - self.l
        self.core = self.dev(self.z, self.x, self.y, 1 - self.c)
        self.xn = self.dev(self.z, 1 - self.x, self.y, self.c)
        self.yn = self.dev(self.z, self.x, 1 - self.y, self.c)
        self.diag = self.dev(self.z, 1 - self.x, 1 - self.y, self.c)
        self.ycore = self.dev(self.z, self.x, 1 - self.y, 1 - self.c)
        self.zn1 = self.dev(self.z1, self.x, self.y, self.c)
        self.zn2 = self.dev(self.z2, self.x, self.y, self.c)
        self.zn3 = self.dev(self.z3, self.x, self.y, self.c)

    def dev(self, z, x, y, c):
        return (self.base + z * 2 + x, y * 2 + c)

    def greet(self):
        barrier = pltpu.get_barrier_semaphore()
        peers = (self.core, self.xn, self.yn, self.diag, self.ycore, self.zn1, self.zn2, self.zn3)
        for peer in peers:
            pl.semaphore_signal(barrier, inc=1, device_id=peer, device_id_type=MESH)
        pl.semaphore_wait(barrier, len(peers))


def guarded(when, action):
    if when is None:
        action()
    else:
        pl.when(when)(action)


class Msg:
    def __init__(self, post, src, dst, dev, into, key=None, when=None):
        self.k = post.sends
        post.sends += 1
        self.key = post.key() if key is None else key
        self.when = when
        self.post, self.src, self.dst, self.dev, self.into = post, src, dst, dev, into
        self.done = False
        post.group.append(self)

    def copy(self, src, dst):
        return pltpu.make_async_remote_copy(
            src_ref=src,
            dst_ref=dst,
            send_sem=self.post.send.at[self.k],
            recv_sem=self.post.recv.at[self.key],
            device_id=self.dev,
            device_id_type=MESH,
        )

    def start(self):
        guarded(self.when, lambda: self.copy(self.src, self.dst).start())

    def arrived(self):
        self.copy(self.into, self.into).wait_recv()

    def sent(self):
        if self.done:
            return
        self.done = True
        guarded(self.when, lambda: self.copy(self.src, self.dst).wait_send())


class Post:
    def __init__(self, send, recv):
        self.send, self.recv = send, recv
        self.sends = self.most = self.keys = 0
        self.group, self.spare = [], []

    def key(self):
        if self.spare:
            return self.spare.pop(0)
        self.keys += 1
        return self.keys - 1

    def msg(self, *a, **k):
        return Msg(self, *a, **k)

    def recycle(self):
        group, self.group = self.group, []
        self.most, self.sends = max(self.most, self.sends), 0
        return group

    def drain(self):
        for m in self.recycle():
            m.sent()


class ZGather:
    def __init__(self, post, at, view, core):
        own = view(at.z)
        self.at = at
        self.m1 = post.msg(own, own, at.zn1, view(at.z1))
        self.m2 = post.msg(own, own, at.zn2, view(at.z2))
        self.m3 = post.msg(own, own, at.zn3, view(at.z3), when=at.mid)
        self.relay = post.msg(view(at.z2), view(at.z2), at.zn1, view(at.z3), key=self.m3.key, when=at.mid)
        early = jnp.where(at.mid, at.z2, at.z1)
        late = jnp.where(at.mid, at.z1, at.z2)
        self.core = [core(zz) for zz in (at.z, early, late, at.z3)]

    def start(self):
        pl.when(self.at.mid)(self.m1.start)
        pl.when(self.at.end)(self.m2.start)
        self.core[0].start()

    def far(self):
        @pl.when(self.at.mid)
        def _():
            self.m2.arrived()
            self.relay.start()
            self.m3.start()
            self.m2.start()

        pl.when(self.at.end)(self.m1.start)

    def early(self):
        pl.when(self.at.end)(self.m1.arrived)
        self.core[1].start()

    def last(self):
        pl.when(self.at.mid)(self.m1.arrived)
        pl.when(self.at.end)(self.m2.arrived)
        self.core[2].start()
        self.m3.arrived()
        self.core[3].start()

    def all(self):
        for m in self.core:
            m.arrived()


class PlaneGather:
    def __init__(self, post, at, view, half):
        own = view(at.x, at.y)
        ox, oy = 1 - at.x, 1 - at.y
        self.mx = post.msg(own, own, at.xn, view(ox, at.y))
        self.my = post.msg(own, own, at.yn, view(at.x, oy))
        self.hy = post.msg(half(ox, at.y, 0), half(ox, at.y, 0), at.yn, half(ox, oy, 0))
        self.hx = post.msg(half(at.x, oy, 1), half(at.x, oy, 1), at.xn, half(ox, oy, 1))

    def start(self):
        self.mx.start()
        self.my.start()

    def relay(self):
        self.mx.arrived()
        self.hy.start()
        self.my.arrived()
        self.hx.start()

    def last(self):
        self.hy.arrived()
        self.hx.arrived()


class HalfGather:
    def __init__(self, post, at, half):
        x, y = at.x, at.y
        ox, oy = 1 - x, 1 - y

        def msg(part, dev, into):
            return post.msg(part, part, dev, into)

        self.x0 = msg(half(x, y, 0), at.xn, half(ox, y, 0))
        self.y1 = msg(half(x, y, 1), at.yn, half(x, oy, 1))
        self.x1 = msg(half(x, y, 1), at.xn, half(ox, y, 1))
        self.y0 = msg(half(x, y, 0), at.yn, half(x, oy, 0))
        self.hy = msg(half(ox, y, 0), at.yn, half(ox, oy, 0))
        self.hx = msg(half(x, oy, 1), at.xn, half(ox, oy, 1))

    def start(self):
        self.x0.start()
        self.y1.start()

    def relay0(self):
        self.x0.arrived()
        self.hy.start()

    def relay1(self):
        self.y1.arrived()
        self.hx.start()

    def relay(self):
        self.relay0()
        self.relay1()

    def rest(self):
        self.y0.start()
        self.x1.start()

    def last0(self):
        self.y0.arrived()
        self.hy.arrived()

    def last1(self):
        self.x1.arrived()
        self.hx.arrived()

    def last(self):
        self.last0()
        self.last1()


class Spread:
    def __init__(self, post, at, G, span):
        lanes = cols(span)

        def view(zz, x, y):
            return G.at[zz, x * 2 + y, at.c, :, lanes]

        def half(zz, x, y, h):
            return G.at[zz, x * 2 + y, at.c, pl.ds(16 * h, 16), lanes]

        own = view(at.z, at.x, at.y)
        self.z = [
            post.msg(own, own, dev, view(zz, at.x, at.y))
            for zz, dev in ((at.z1, at.zn1), (at.z2, at.zn2), (at.z3, at.zn3))
        ]
        self.plane = [
            PlaneGather(
                post, at, lambda x, y, zz=zz: view(zz, x, y), lambda x, y, h, zz=zz: half(zz, x, y, h)
            )
            for zz in at.zs
        ]
        self.core = [
            post.msg(
                G.at[zz, :, at.c, :, lanes], G.at[zz, :, at.c, :, lanes], at.core, G.at[zz, :, 1 - at.c, :, lanes]
            )
            for zz in at.zs
        ]

    def start(self):
        for m in self.z:
            m.start()

    def into_plane(self):
        for k in range(3):
            self.z[k].arrived()
            self.plane[k + 1].start()

    def relay(self):
        for g in self.plane:
            g.relay()

    def to_core(self):
        for g, m in zip(self.plane, self.core):
            g.last()
            m.start()

    def arrived(self):
        for m in self.core:
            m.arrived()


class SpreadWide:
    def __init__(self, post, at, G, span, along_x):
        lanes = cols(span)

        def block(zz):
            return G.at[zz, at.p, at.c, :, lanes]

        def column(p):
            return G.at[:, p, at.c, :, lanes]

        own = block(at.z)
        self.z = [
            post.msg(own, own, dev, block(zz))
            for zz, dev in ((at.z1, at.zn1), (at.z2, at.zn2), (at.z3, at.zn3))
        ]
        near, far = ((at.px, at.xn), (at.py, at.yn)) if along_x else ((at.py, at.yn), (at.px, at.xn))
        self.one = post.msg(column(at.p), column(at.p), near[1], column(near[0]))
        self.two = post.msg(column(at.p), column(at.p), far[1], column(far[0]))
        self.on = post.msg(column(near[0]), column(near[0]), far[1], column(at.pd))
        self.core = post.msg(
            G.at[:, :, at.c, :, lanes], G.at[:, :, at.c, :, lanes], at.core, G.at[:, :, 1 - at.c, :, lanes]
        )

    def start(self):
        for m in self.z:
            m.start()

    def along_z(self):
        for m in self.z:
            m.arrived()

    def relay(self):
        self.one.arrived()
        self.on.start()

    def to_core(self):
        self.two.arrived()
        self.on.arrived()
        self.core.start()

    def arrived(self):
        self.core.arrived()


class LatGather:
    def __init__(self, post, at, view):
        self.mc = post.msg(view(at.l), view(at.l), at.core, view(at.lc))
        self.my = post.msg(view(at.l), view(at.l), at.yn, view(at.ly))
        self.fc = post.msg(view(at.ly), view(at.ly), at.core, view(at.ld))

    def start(self):
        self.my.start()
        self.mc.start()

    def relay(self):
        self.my.arrived()
        self.fc.start()

    def last(self):
        self.mc.arrived()
        self.fc.arrived()


class LatReduce:
    def __init__(self, post, at, parts, first, second):
        self.at, self.parts, self.first, self.second = at, parts, first, second
        self.m0 = post.msg(parts.at[at.lc], first.at[0], at.core, first.at[0])
        self.m1 = post.msg(parts.at[at.ld], first.at[1], at.core, first.at[1])
        self.m2 = post.msg(parts.at[at.ly], second, at.yn, second)

    def start(self):
        self.m1.start()
        self.m0.start()

    def relay(self):
        self.m1.arrived()
        ly = self.at.ly
        self.parts[ly] = (self.parts[ly].astype(F32) + self.first[1].astype(F32)).astype(BF16)
        self.m2.start()

    def total(self):
        self.m0.arrived()
        self.m2.arrived()
        near = self.parts[self.at.l].astype(F32) + self.first[0].astype(F32)
        return near + self.second[...].astype(F32)


class HalfReduce:
    def __init__(self, post, at, half, part, near, other, last):
        x, y = at.x, at.y
        ox, oy = 1 - x, 1 - y
        self.near, self.other, self.end = near, other, last
        self.own = part(x, y)
        first, second = (at.yn, at.xn) if half == 0 else (at.xn, at.yn)
        self.there = part(ox, y) if half == 0 else part(x, oy)
        beside = part(x, oy) if half == 0 else part(ox, y)
        self.m1 = post.msg(part(ox, oy), other, first, other)
        self.m0 = post.msg(beside, near, first, near)
        self.f = post.msg(self.there, last, second, last)

    def start(self):
        self.m1.start()
        self.m0.start()

    def relay(self):
        self.m1.arrived()
        self.there[...] = (self.there[...].astype(F32) + self.other[...].astype(F32)).astype(BF16)
        self.f.start()

    def total(self):
        self.m0.arrived()
        self.f.arrived()
        return self.own[...].astype(F32) + self.near[...].astype(F32) + self.end[...].astype(F32)


class PlaneReduceX:
    def __init__(self, post, at, part, mine, other, last, pieces):
        ox, oy = 1 - at.x, 1 - at.y
        self.mine, self.other, self.end = mine, other, last
        self.own, self.there = part(at.x, at.y), part(at.x, oy)
        self.m1 = post.msg(part(ox, oy), other, at.xn, other)
        self.m0 = post.msg(part(ox, at.y), mine, at.xn, mine)
        size = self.there.shape[0] // pieces
        self.f = []
        for k in range(pieces):
            piece = last.at[pl.ds(k * size, size)]
            self.f.append(post.msg(self.there.at[pl.ds(k * size, size)], piece, at.yn, piece))

    def start(self):
        self.m1.start()
        self.m0.start()

    def relay(self):
        self.m1.arrived()
        self.there[...] = (self.there[...].astype(F32) + self.other[...].astype(F32)).astype(BF16)
        self.f[0].start()

    def rest(self):
        self.f[1].start()

    def total(self):
        self.m0.arrived()
        for m in self.f:
            m.arrived()
        total = self.own[...].astype(F32) + self.mine[...].astype(F32)
        return total + self.end[...].astype(F32)


class ZReduce:
    def __init__(self, post, at, term, buf):
        self.at, self.term, self.buf = at, term, buf
        self.m1 = post.msg(term(at.z1), buf(0), at.zn1, buf(0))
        self.m2 = post.msg(term(at.z2), buf(1), at.zn2, buf(1))
        self.m3 = post.msg(term(at.z3), buf(2), at.zn3, buf(2), when=at.mid)
        self.rel = post.msg(term(at.z3), buf(3), at.zn1, buf(3), when=at.end)

    def start_last(self):
        self.rel.start()
        self.m3.start()

    def start_far(self):
        pl.when(self.at.end)(self.m2.start)

    def start_near(self):
        self.m1.start()

    def relay(self):
        @pl.when(self.at.mid)
        def _():
            self.rel.arrived()
            there = self.term(self.at.z2)
            there[...] = (there[...].astype(F32) + self.buf(3)[...].astype(F32)).astype(BF16)
            self.m2.start()

    def total(self, out):
        self.m1.arrived()
        self.m2.arrived()
        value = self.term(self.at.z)[...].astype(F32) + self.buf(0)[...].astype(F32)
        out[...] = value + self.buf(1)[...].astype(F32)

        @pl.when(self.at.mid)
        def _():
            self.m3.arrived()
            out[...] += self.buf(2)[...].astype(F32)


class ZDirect:
    def __init__(self, post, at, term, buf):
        self.at, self.term, self.buf = at, term, buf
        self.msgs = [
            post.msg(term(zz), buf(k), dev, buf(k))
            for k, (zz, dev) in enumerate(((at.z1, at.zn1), (at.z2, at.zn2), (at.z3, at.zn3)))
        ]

    def start(self):
        for m in self.msgs[::-1]:
            m.start()

    def total(self, out):
        value = self.term(self.at.z)[...].astype(F32)
        for k, m in enumerate(self.msgs):
            m.arrived()
            value = value + self.buf(k)[...].astype(F32)
        out[...] = value


class Collect:
    def __init__(self, post, at, grads, near, bufs, bz, src, dst, buf, spare):
        self.at, self.grads, self.near, self.src = at, grads, near, src
        post.spare = list(spare)
        self.lanes, self.there = cols(src), cols(dst)
        into = pl.ds(buf, src[1])
        self.core = post.msg(
            grads.at[:, :, 1 - at.c, :, self.lanes], near.at[:, :, :, self.lanes], at.core,
            near.at[:, :, :, self.lanes],
        )
        self.plane = [
            HalfReduce(
                post,
                at,
                h,
                lambda x, y, h=h: near.at[:, x * 2 + y, pl.ds(16 * h, 16), self.lanes],
                *[b.at[h, :, :, into] for b in bufs],
            )
            for h in range(2)
        ]
        post.spare = []
        self.z = ZDirect(
            post, at, lambda zz: near.at[zz, at.p, :, self.lanes], lambda k: bz.at[k, :, self.there]
        )

    def start(self):
        self.core.start()

    def into_plane(self):
        self.core.arrived()

        def add(zz, carry):
            mine = self.grads[zz, :, self.at.c, :, self.lanes].astype(F32)
            self.near[zz, :, :, self.lanes] = (self.near[zz, :, :, self.lanes].astype(F32) + mine).astype(BF16)
            return carry

        lax.fori_loop(0, 4, add, 0)
        for h in self.plane:
            h.start()

    def relay(self):
        for h in self.plane:
            h.relay()

    def into_z(self):
        for k, h in enumerate(self.plane):
            self.near[:, self.at.p, 16 * k : 16 * k + 16, self.lanes] = h.total().astype(BF16)
        self.z.start()

    def total(self, out):
        self.z.total(out)


class CollectNorms:
    def __init__(self, post, at, grads, near, by, bx, b2, bz, span, spare):
        self.at, self.grads, self.near, self.lanes = at, grads, near, cols(span)
        post.spare = list(spare)
        low = pl.ds(0, 16)

        def part(p):
            return near.at[:, p, low, self.lanes]

        theirs = grads.at[:, :, 1 - at.c, low, self.lanes]
        here = near.at[:, :, low, self.lanes]
        self.core = post.msg(theirs, here, at.core, here)
        self.bufs = [b.at[0, :, :, self.lanes] for b in (bx, by, b2)]
        self.plane = [
            post.msg(part(p), buf, dev, buf)
            for p, buf, dev in zip((at.px, at.py, at.pd), self.bufs, (at.xn, at.yn, at.diag))
        ]
        post.spare = []
        self.z = ZDirect(
            post, at, lambda zz: near.at[zz, at.p, low, self.lanes], lambda k: bz.at[k, low, self.lanes]
        )

    def start(self):
        self.core.start()

    def into_plane(self):
        self.core.arrived()
        mine = self.grads[:, :, self.at.c, 0:16, self.lanes].astype(F32)
        self.near[:, :, 0:16, self.lanes] = (self.near[:, :, 0:16, self.lanes].astype(F32) + mine).astype(BF16)
        for m in self.plane:
            m.start()

    def into_z(self):
        total = self.near[:, self.at.p, 0:16, self.lanes].astype(F32)
        for m, buf in zip(self.plane, self.bufs):
            m.arrived()
            total = total + buf[...].astype(F32)
        self.near[:, self.at.p, 0:16, self.lanes] = total.astype(BF16)
        self.z.start()

    def total(self, out):
        self.z.total(out)


def head_mask():
    rows = lax.div(lax.broadcasted_iota(jnp.int32, (256, 256), 0), 64)
    lanes = lax.div(lax.broadcasted_iota(jnp.int32, (256, 256), 1), 64)
    return (rows == lanes).astype(F32).astype(BF16)


def spread_heads(part, mask):
    rows = part.reshape(64, 256)
    return jnp.concatenate([rows, rows, rows, rows], axis=0) * mask


def gather_heads(wide):
    lane = lax.div(lax.broadcasted_iota(jnp.int32, (64, 256), 1), 64)
    out = jnp.where(lane == 0, wide[0:64], 0.0)
    for h in range(1, 4):
        out = out + jnp.where(lane == h, wide[64 * h : 64 * h + 64], 0.0)
    return out


def pick(values, k):
    out = values[-1]
    for i in range(len(values) - 2, -1, -1):
        out = jnp.where(k == i, values[i], out)
    return out


def span256(n):
    return pl.ds(pl.multiple_of(n * 256, 256), 256)


class Names:
    def __getattr__(self, name):
        return name


class Steps:
    def __init__(self):
        self.made = {}

    def __getattr__(self, name):
        def keep(*actions):
            assert name not in self.made, name
            self.made[name] = actions

        return keep


def order(s):
    return (
        s.load, s.greet, s.staged, s.first_z, s.first_0, s.keys_0, s.cot_a, s.up_a, s.stats, s.keys_z, s.first_1,
        s.first_2, s.first_3, s.second_z, s.first_r0, s.first_r1, s.first_r2, s.first_r3, s.keys_1, s.keys_2,
        s.keys_3, s.third_z, s.first_c0, s.first_c1, s.first_c2, s.first_c3, s.down_a, s.up_in, s.up_z, s.keys_r0,
        s.keys_r1, s.keys_r2, s.keys_r3, s.first_in, s.query, s.q_a, s.second_in, s.second_a, s.keys_c0, s.keys_c1,
        s.keys_c2, s.keys_c3, s.low, s.second_b, s.keys_in, s.pairs_k, s.q_b, s.second_r, s.q_in, s.down_far,
        s.up_far, s.third_in, s.third_a, s.third_b, s.cot_b, s.score_0, s.ls_0, s.cot_r, s.score_1, s.ls_1,
        s.second_c, s.third_r, s.second_done, s.pairs_v, s.ls_in0, s.mix_0, s.mixed_a0, s.ls_in1, s.mix_1,
        s.mixed_a1, s.mixed_b0, s.mixed_b1, s.third_c, s.third_done, s.mixed_in0, s.mixed_in1, s.resid, s.mlp_a,
        s.mlp_b, s.mlp_r0, s.mlp_r1, s.cot_in, s.down_early, s.up_early, s.down_last, s.up_mid, s.down_done,
        s.cot_back, s.up_end, s.up_done, s.mlp_in0, s.gates_0, s.parts_0, s.recycle, s.back_a0, s.mlp_in1, s.gates_1,
        s.parts_1, s.back_a1, s.grad_d3, s.grad_u3, s.grad_d2, s.add_d3, s.grad_u2, s.add_u3, s.back_r0, s.grad_d1,
        s.grad_d0, s.back_r1, s.add_d2, s.add_u2, s.grad_u1, s.grad_u0, s.add_d1, s.add_d0, s.out_parts, s.add_u1,
        s.add_u0, s.back_in0, s.norm_0, s.gm_a0, s.back_in1, s.norm_1, s.gm_a1, s.out_a, s.w_out, s.out_core,
        s.gm_b0, s.gm_in0, s.gm_b1, s.probs_0, s.dl_0, s.gm_in1, s.probs_1, s.dl_1, s.value_0, s.dl_in0, s.out_plane,
        s.scores_0, s.gq_a0, s.dl_in1, s.scores_1, s.gq_a1, s.value_1, s.value_core, s.far_d, s.far_u, s.gq_b0,
        s.gq_b1, s.key_0, s.value_plane, s.out_relay, s.key_1, s.key_core, s.key_plane, s.media_0, s.media_1,
        s.value_relay, s.media_2, s.out_r, s.media_3, s.gq_in, s.query_core, s.norms, s.norms_core, s.key_relay,
        s.out_z, s.value_z, s.grad_latents, s.norms_plane, s.query_plane, s.key_z, s.query_relay, s.out_b, s.sum_d,
        s.sum_u, s.norms_z, s.query_z, s.out_sum, s.value_sum, s.key_sum, s.norms_sum, s.up_out, s.out_in,
        s.query_sum,
    )


def kernel_body(at, post, R):
    images, per_media, _ = R.MED.shape
    per_lat = R.latents.shape[1]
    rows = per_media + per_lat
    tokens = images * per_lat
    half_rows = tokens // 2
    each = images // 2
    zs = at.zs
    halves = (pl.ds(0, half_rows), pl.ds(half_rows, half_rows))
    do = Steps()

    own = R.G.at[at.z, at.p, at.c]
    loads = [
        pltpu.make_async_copy(src, dst, R.local.at[k])
        for k, (src, dst) in enumerate(
            (
                (R.in_media, R.MED),
                (R.in_latents, R.latents),
                (R.in_cotangent, R.cotangent),
                (R.in_query, own.at[:, cols(QU)]),
                (R.in_keyvalue, own.at[:, cols(KV)]),
                (R.in_output.at[:, pl.ds(0, 512)], own.at[pl.ds(0, 16), cols(OUT)]),
                (R.in_output.at[:, pl.ds(512, 512)], own.at[pl.ds(16, 16), cols(OUT)]),
                (R.in_up, R.w_up),
                (R.in_down, R.UD.at[at.z, at.c]),
            )
        )
    ]

    @do.load
    def _():
        for c in loads[3:] + loads[2:3] + loads[:2]:
            c.start()
        norms = [ref[...].astype(F32).reshape(1, 32) for ref in (R.n0, R.n1, R.n2, R.n3, R.n4, R.n5)]
        norms = jnp.concatenate(norms + [jnp.zeros((10, 32), F32)], axis=0)
        norms = jnp.concatenate([norms, norms, norms, norms], axis=1)
        lanes = lax.div(lax.broadcasted_iota(jnp.int32, (16, 128), 1), 32)
        R.G[at.z, at.p, at.c, 0:16, cols(GN)] = jnp.where(lanes == at.l, norms, 0.0).astype(BF16)
        R.G[at.z, at.p, at.c, 16:32, cols(GN)] = jnp.zeros((16, 128), BF16)

    do.greet(at.greet)

    @do.staged
    def _():
        for c in loads[3:]:
            c.wait()
        for p in range(4):
            for zz in range(4):
                for cc in range(2):
                    R.WS[p, :, 128 * (2 * zz + cc) : 128 * (2 * zz + cc) + 128] = R.w_up[
                        :, 128 * (8 * zz + 2 * p + cc) : 128 * (8 * zz + 2 * p + cc) + 128
                    ]
        R.UU[at.z, at.p, at.c] = R.WS[at.p]
        loads[2].wait()
        R.CA[at.p] = R.cotangent[...].reshape(tokens, 1024)

    first = Spread(post, at, R.G, (0, 640))
    keys = Spread(post, at, R.G, KEY)
    second = SpreadWide(post, at, R.G, VAL, True)
    third = SpreadWide(post, at, R.G, OUT, False)
    for name, stream in (("first", first), ("keys", keys)):
        getattr(do, name + "_z")(stream.start)
        getattr(do, name + "_0")(stream.plane[0].start)
        for k in range(1, 4):
            getattr(do, "%s_%d" % (name, k))(stream.z[k - 1].arrived, stream.plane[k].start)
        for k in range(4):
            getattr(do, "%s_r%d" % (name, k))(stream.plane[k].relay)
            getattr(do, "%s_c%d" % (name, k))(stream.plane[k].last, stream.core[k].start)
        getattr(do, name + "_in")(stream.arrived)
    for name, stream in (("second", second), ("third", third)):
        getattr(do, name + "_z")(stream.start)
        getattr(do, name + "_in")(stream.along_z)
        getattr(do, name + "_a")(stream.one.start)
        getattr(do, name + "_b")(stream.two.start)
        getattr(do, name + "_r")(stream.relay)
        getattr(do, name + "_c")(stream.to_core)
        getattr(do, name + "_done")(stream.arrived)

    up = [
        post.msg(R.WS.at[there], R.UU.at[at.z, at.p, at.c], dev, R.UU.at[at.z, there, at.c])
        for there, dev in ((at.px, at.xn), (at.py, at.yn), (at.pd, at.diag))
    ]
    do.up_a(*[m.start for m in up])
    do.up_in(*[m.arrived for m in up])
    d_z = ZGather(
        post,
        at,
        lambda zz: R.UD.at[zz, at.c],
        lambda zz: post.msg(R.UD.at[zz, at.c], R.UD.at[zz, at.c], at.core, R.UD.at[zz, 1 - at.c]),
    )
    u_z = ZGather(
        post,
        at,
        lambda zz: R.UU.at[zz, :, at.c],
        lambda zz: post.msg(R.UU.at[zz, :, at.c], R.UU.at[zz, :, at.c], at.core, R.UU.at[zz, :, 1 - at.c]),
    )
    do.down_a(d_z.start)
    do.down_far(d_z.far)
    do.down_early(d_z.early)
    do.down_last(d_z.last)
    do.down_done(d_z.all)
    do.up_z(u_z.start)
    do.up_far(u_z.far)
    do.up_early(u_z.early)
    do.up_mid(lambda: pl.when(at.mid)(u_z.last))
    do.up_end(lambda: pl.when(at.end)(u_z.last))
    do.up_done(u_z.all)

    cot = HalfGather(post, at, lambda x, y, h: R.CA.at[x * 2 + y, halves[h]])
    do.cot_a(cot.start)
    do.cot_b(cot.rest)
    do.cot_r(cot.relay)
    do.cot_in(cot.last)

    @do.stats
    def _():
        def stats(g, carry):
            mean, rstd = normal(R.MED[g].astype(F32))
            R.MR[g, 0:per_media, 0:1] = mean
            R.MR[g, 0:per_media, 1:2] = rstd
            mean, rstd = normal(R.latents[g].astype(F32))
            R.MR[g, per_media:rows, 0:1] = mean
            R.MR[g, per_media:rows, 1:2] = rstd
            return carry

        loads[0].wait()
        loads[1].wait()
        loop(images, stats)

    @do.query
    def _():
        for i in range(8):
            total = jnp.zeros((16, 128), F32)
            for p in (2 * (i % 2), 2 * (i % 2) + 1):
                for c in range(2):
                    total = total + R.G[i // 2, p, c, 0:16, cols(GN)].astype(F32)
            R.VV[:, 128 * i : 128 * i + 128] = total
        latents = flat(R.latents[...]).astype(F32)
        normed = (latents - flat(R.MR[:, per_media:rows, 0:1])) * flat(R.MR[:, per_media:rows, 1:2])
        latent_low = (normed * R.VV[2:3, :] + R.VV[3:4, :]).astype(BF16)
        R.X[:, per_media:rows, :] = latent_low.reshape(images, per_lat, 1024)
        R.QA[at.l] = mm(latent_low, R.G[:, :, :, :, cols(QU)].reshape(1024, 512)).astype(BF16)

    q_all = LatGather(post, at, lambda l: R.QA.at[l])
    do.q_a(q_all.start)
    do.q_b(q_all.relay)
    do.q_in(q_all.last)

    @do.low
    def _():
        def low(g, carry):
            normed = (R.MED[g].astype(F32) - R.MR[g, 0:per_media, 0:1]) * R.MR[g, 0:per_media, 1:2]
            R.X[g, 0:per_media, :] = (normed * R.VV[0:1, :] + R.VV[1:2, :]).astype(BF16)
            return carry

        loop(images, low)

    def pairs(n, carry):
        weight = R.G[:, :, :, :, pl.ds(pl.multiple_of(KV[0] + n * 256, 128), 256)].reshape(1024, 256)
        made = mm(R.X[...].reshape(images * rows, 1024), weight).astype(BF16)
        R.PR[:, :, span256(n)] = made.reshape(images, rows, 256)
        return carry

    do.pairs_k(lambda: loop((0, 2), pairs))
    do.pairs_v(lambda: loop((2, 4), pairs))

    mask = head_mask()

    def lat_rows(g):
        return pl.ds(pl.multiple_of(g * per_lat, per_lat), per_lat)

    def score(g, carry):
        limit = SHORT + (LONG - SHORT) * R.bucket[g] - at.l * per_media
        row = lax.broadcasted_iota(jnp.int32, (rows, 256), 0)
        valid = jnp.logical_or(row >= per_media, row < limit)
        for half in range(2):
            span = pl.ds(256 * half, 256)
            raw = mm_nt(R.PR[g, :, span], spread_heads(R.QA[:, lat_rows(g), span], mask)) * SCALE
            raw = jnp.where(valid, raw, NEG)
            top = jnp.max(raw, axis=0, keepdims=True)
            total = jnp.sum(jnp.exp(raw - top), axis=0, keepdims=True)
            R.S[2 * g + half] = raw
            R.LS[at.l, pl.ds(2 * g + half, 1), :] = top + jnp.log(total)
        return carry

    def mix(g, carry):
        for half in range(2):
            probs = jnp.exp(R.S[2 * g + half] - R.LG[pl.ds(2 * g + half, 1), :]).astype(BF16)
            R.PB[2 * g + half] = probs
            wide = mm_tn(probs, R.PR[g, :, pl.ds(512 + 256 * half, 256)])
            R.OP[:, lat_rows(g), pl.ds(256 * half, 256)] = (
                gather_heads(wide).reshape(4, per_lat, 256).astype(BF16)
            )
        return carry

    def exchange(ref, span):
        return [
            post.msg(ref.at[at.l, span], ref.at[at.l, span], dev, ref.at[there, span])
            for there, dev in ((at.ly, at.yn), (at.ld, at.ycore), (at.lc, at.core))
        ]

    def log_total(span):
        parts = [R.LS[l, span, :] for l in range(4)]
        top = jnp.maximum(jnp.maximum(parts[0], parts[1]), jnp.maximum(parts[2], parts[3]))
        total = sum(jnp.exp(part - top) for part in parts)
        R.LG[span, :] = top + jnp.log(total)

    lat_keys = []
    for h in range(2):
        here = (each * h, each * h + each)
        span = pl.ds(2 * each * h, 2 * each)
        getattr(do, "score_%d" % h)(lambda here=here: loop(here, score))
        ls = exchange(R.LS, span)
        getattr(do, "ls_%d" % h)(*[m.start for m in ls])
        getattr(do, "ls_in%d" % h)(*[m.arrived for m in ls], lambda span=span: log_total(span))
        getattr(do, "mix_%d" % h)(lambda here=here: loop(here, mix))
        mixed = LatReduce(post, at, R.OP.at[:, halves[h]], R.O1.at[:, halves[h]], R.O2.at[halves[h]])
        lat_keys.append([m.key for m in ls + [mixed.m0, mixed.m1, mixed.m2]])
        getattr(do, "mixed_a%d" % h)(mixed.start)
        getattr(do, "mixed_b%d" % h)(mixed.relay)

        @getattr(do, "mixed_in%d" % h)
        def _(mixed=mixed, h=h):
            R.MX[halves[h], :] = mixed.total().astype(BF16)

    def out_weight():
        left = R.G[:, :, :, 0:16, cols(OUT)].reshape(512, 512)
        return left, R.G[:, :, :, 16:32, cols(OUT)].reshape(512, 512)

    @do.resid
    def _():
        left, right = out_weight()
        latents = flat(R.latents[...]).astype(F32)
        R.RES[:, 0:512] = latents[:, 0:512] + mm(R.MX[...], left)
        R.RES[:, 512:1024] = latents[:, 512:1024] + mm(R.MX[...], right)
        mean, rstd = normal(R.RES[...])
        R.RN[:, 0:1] = mean
        R.RN[:, 1:2] = rstd
        R.MA[at.p] = ((R.RES[...] - mean) * rstd * R.VV[4:5, :] + R.VV[5:6, :]).astype(BF16)

    mlp = HalfGather(post, at, lambda x, y, h: R.MA.at[x * 2 + y, halves[h]])
    do.mlp_a(mlp.start)
    do.mlp_b(mlp.rest)
    do.mlp_r0(mlp.relay0)
    do.mlp_r1(mlp.relay1)
    do.mlp_in0(mlp.last0)
    do.mlp_in1(mlp.last1)

    do.recycle(*[m.sent for m in post.recycle()])
    planes = [m.key for w in (first, keys) for g in w.plane for m in (g.mx, g.my, g.hy, g.hx)]
    cores = [m.key for w in (first, keys) for m in w.core]

    @do.cot_back
    def _():
        def cot_back(f, carry):
            made = mm_nt(R.CA[...].reshape(4 * tokens, 1024), R.UD[f].reshape(256, 1024))
            R.S[pl.ds(4 * f, 4), 0:tokens, :] = made.reshape(4, tokens, 256)
            return carry

        loop(4, cot_back)

    def gates(h):
        part = halves[h]

        def gates(f, carry):
            weight = R.UU[:, :, :, :, span256(f)].reshape(1024, 256)
            gate = mm(R.MA[:, part, :].reshape(4 * half_rows, 1024), weight)
            back = R.S[pl.ds(4 * f, 4), part, :].reshape(4 * half_rows, 256)
            phi = 0.5 * (1.0 + lax.erf(gate * 0.7071067811865476))
            R.ACT[:, part, span256(f)] = (gate * phi).astype(BF16).reshape(4, half_rows, 256)
            slope = phi + gate * jnp.exp(-0.5 * gate * gate) * 0.3989422804014327
            R.GG[:, part, span256(f)] = (back * slope).astype(BF16).reshape(4, half_rows, 256)
            return carry

        loop(4, gates)

    def norm_parts(h):
        part = halves[h]

        def norm_parts(n, carry):
            made = mm_nt(R.GG[:, part, :].reshape(4 * half_rows, 1024), R.UU[n].reshape(256, 1024))
            R.PT[:, part, span256(n)] = made.astype(BF16).reshape(4, half_rows, 256)
            return carry

        loop(4, norm_parts)

    post.spare = [m.key for w in (second, third) for m in (w.one, w.two, w.on)]
    for h in range(2):
        getattr(do, "gates_%d" % h)(lambda h=h: gates(h))
        getattr(do, "parts_%d" % h)(lambda h=h: norm_parts(h))
        back = HalfReduce(
            post, at, h, lambda x, y, h=h: R.PT.at[x * 2 + y, halves[h]], R.PY.at[h], R.PX.at[h], R.P2.at[h]
        )
        getattr(do, "back_a%d" % h)(back.start)
        getattr(do, "back_r%d" % h)(back.relay)

        @getattr(do, "back_in%d" % h)
        def _(back=back, h=h):
            R.U[halves[h], :] = back.total()

    def down_grads(k, carry):
        f = pick(zs, k)
        act = R.ACT[:, :, span256(f)].reshape(4 * tokens, 256)
        R.gD[f] = mm_tn(act, R.CA[...].reshape(4 * tokens, 1024)).astype(BF16).reshape(2, 128, 1024)
        return carry

    def up_grads(k, carry):
        n = pick(zs, k)
        low_rows = R.MA[:, :, span256(n)].reshape(4 * tokens, 256)
        made = mm_tn(low_rows, R.GG[...].reshape(4 * tokens, 1024)).astype(BF16)
        R.gU[n] = made.reshape(4, 2, 32, 1024)
        return carry

    gd_z = ZReduce(post, at, lambda zz: R.RD.at[zz], lambda k: R.ZD.at[k])
    gu_z = ZReduce(post, at, lambda zz: R.RU.at[zz], lambda k: R.ZU.at[k])
    nothing = lambda: None
    gu_c = []
    post.spare = cores
    for k in range(4):
        zz = zs[k]
        gd = post.msg(R.gD.at[zz, 1 - at.c], R.RD.at[zz], at.core, R.RD.at[zz])
        gu = post.msg(R.gU.at[zz, :, 1 - at.c], R.RU.at[zz], at.core, R.RU.at[zz])
        gu_c.append(gu)
        getattr(do, "grad_d%d" % k)(lambda k=k: loop((k, k + 1), down_grads), gd.start)
        getattr(do, "grad_u%d" % k)(lambda k=k: loop((k, k + 1), up_grads), gu.start)

        def add_d(zz=zz):
            R.RD[zz] = (R.RD[zz].astype(F32) + R.gD[zz, at.c].astype(F32)).astype(BF16)

        def add_u(zz=zz):
            R.RU[zz] = (R.RU[zz].astype(F32) + R.gU[zz, :, at.c].astype(F32)).astype(BF16)

        send = (nothing, "start_near", "start_far", "start_last")[k]
        getattr(do, "add_d%d" % k)(gd.arrived, add_d, getattr(gd_z, send) if k else nothing)
        getattr(do, "add_u%d" % k)(gu.arrived, add_u, getattr(gu_z, send) if k else nothing)
    do.far_d(gd_z.relay)
    do.far_u(gu_z.relay)

    @do.out_parts
    def _():
        def out_parts(n, carry):
            made = mm(R.ACT[...].reshape(4 * tokens, 1024), R.UD[:, :, :, span256(n)].reshape(1024, 256))
            R.GG[:, :, span256(n)] = made.astype(BF16).reshape(4, tokens, 256)
            return carry

        loop(4, out_parts)

    out = PlaneReduceX(post, at, lambda x, y: R.GG.at[x * 2 + y], R.OX.at[0], R.OX.at[1], R.OY, 2)
    do.out_a(out.start)
    do.out_r(out.relay)
    do.out_b(out.rest)

    post.spare = [m.key for m in (q_all.mc, q_all.my, q_all.fc, second.core, third.core)]
    for h in range(2):

        @getattr(do, "norm_%d" % h)
        def _(h=h):
            part = halves[h]
            normed = (R.RES[part, :] - R.RN[part, 0:1]) * R.RN[part, 1:2]
            cots = R.CA[at.p, part, :].astype(F32)
            R.GR[part, :] = cots + norm_back(R.U[part, :], normed, R.RN[part, 1:2], R.VV[4:5, :])
            grad_attn = R.GR[part, :].astype(BF16)
            left, right = out_weight()
            made = mm_nt(grad_attn[:, 0:512], left) + mm_nt(grad_attn[:, 512:1024], right)
            R.GM[at.l, part, :] = made.astype(BF16)

        gm = LatGather(post, at, lambda l, h=h: R.GM.at[l, halves[h]])
        getattr(do, "gm_a%d" % h)(gm.start)
        getattr(do, "gm_b%d" % h)(gm.relay)
        getattr(do, "gm_in%d" % h)(gm.last)

    @do.w_out
    def _():
        upstream = R.U[...]
        normed = (R.RES[...] - R.RN[:, 0:1]) * R.RN[:, 1:2]
        R.GS[...] = jnp.zeros_like(R.GS)
        R.GS[4:5, :] = jnp.sum(upstream * normed, axis=0, keepdims=True)
        R.GS[5:6, :] = jnp.sum(upstream, axis=0, keepdims=True)
        grad_attn = R.GR[...].astype(BF16)
        made = mm_tn(R.MX[...], grad_attn[:, 0:512]).astype(BF16)
        R.gA[:, :, :, 0:16, cols(GOUT)] = made.reshape(4, 4, 2, 16, 512)
        made = mm_tn(R.MX[...], grad_attn[:, 512:1024]).astype(BF16)
        R.gA[:, :, :, 16:32, cols(GOUT)] = made.reshape(4, 4, 2, 16, 512)

    bufs = (R.WY, R.WX, R.W2)
    for name, made in (
        ("out", Collect(post, at, R.gA, R.RA, bufs, R.ZW, GOUT, OUT, OUT[0], planes[0:7])),
        ("value", Collect(post, at, R.gU, R.RK, bufs, R.ZW, (512, 512), VAL, VAL[0], planes[7:14])),
        ("key", Collect(post, at, R.gU, R.RK, bufs, R.ZW, (0, 512), KEY, KEY[0], planes[14:21])),
        ("query", Collect(post, at, R.gA, R.RA, bufs, R.ZW, QU, QU, QU[0], planes[21:28])),
        ("norms", CollectNorms(post, at, R.gA, R.RA, R.WY, R.WX, R.W2, R.ZW, GN, planes[28:32])),
    ):
        getattr(do, name + "_core")(made.start)
        getattr(do, name + "_plane")(made.into_plane)
        if name != "norms":
            getattr(do, name + "_relay")(made.relay)
        getattr(do, name + "_z")(made.into_z)
        span = {"out": OUT, "value": VAL, "key": KEY, "query": QU, "norms": GN}[name]
        height = 16 if name == "norms" else 32
        getattr(do, name + "_sum")(lambda made=made, span=span, height=height: made.total(
            R.grad_pack.at[pl.ds(0, height), cols(span)]
        ))

    def grad_probs(g, carry):
        for half in range(2):
            upper = pl.ds(512 + 256 * half, 256)
            wide = spread_heads(R.GM[:, lat_rows(g), pl.ds(256 * half, 256)], mask)
            made = mm_nt(R.PR[g, :, upper], wide)
            probs = R.PB[2 * g + half]
            R.S[2 * g + half] = made
            R.DL[at.l, pl.ds(2 * g + half, 1), :] = jnp.sum(probs.astype(F32) * made, axis=0, keepdims=True)
            R.gP[g, :, upper] = mm(probs, wide).astype(BF16)
        return carry

    def grad_scores(g, carry):
        for half in range(2):
            span = pl.ds(256 * half, 256)
            grads = R.PB[2 * g + half].astype(F32) * (R.S[2 * g + half] - R.LG[pl.ds(2 * g + half, 1), :])
            grads = grads.astype(BF16)
            wide = mm_tn(grads, R.PR[g, :, span]) * SCALE
            R.QP[:, lat_rows(g), span] = gather_heads(wide).reshape(4, per_lat, 256).astype(BF16)
            queries = spread_heads(R.QA[:, lat_rows(g), span], mask)
            R.gP[g, :, span] = (mm(grads, queries) * SCALE).astype(BF16)
        return carry

    def row_terms(span):
        R.LG[span, :] = R.DL[0, span, :] + R.DL[1, span, :] + R.DL[2, span, :] + R.DL[3, span, :]

    sums = []
    for h in range(2):
        here = (each * h, each * h + each)
        span = pl.ds(2 * each * h, 2 * each)
        post.spare = lat_keys[h]
        getattr(do, "probs_%d" % h)(lambda here=here: loop(here, grad_probs))
        dl = exchange(R.DL, span)
        getattr(do, "dl_%d" % h)(*[m.start for m in dl])
        getattr(do, "dl_in%d" % h)(*[m.arrived for m in dl], lambda span=span: row_terms(span))
        getattr(do, "scores_%d" % h)(lambda here=here: loop(here, grad_scores))
        gq = LatReduce(post, at, R.QP.at[:, halves[h]], R.Q1.at[:, halves[h]], R.Q2.at[halves[h]])
        getattr(do, "gq_a%d" % h)(gq.start)
        getattr(do, "gq_b%d" % h)(gq.relay)
        sums.append(gq)

    def kv_grads(n, carry):
        low_rows = R.X[:, :, span256(lax.rem(n, 4))].reshape(images * rows, 256)
        lanes = pl.ds(pl.multiple_of(lax.div(n, 4) * 512, 512), 512)
        made = mm_tn(low_rows, R.gP[:, :, lanes].reshape(images * rows, 512)).astype(BF16)
        R.gU[lax.rem(n, 4), :, :, :, lanes] = made.reshape(4, 2, 32, 512)
        return carry

    do.value_0(*[m.sent for m in gu_c], lambda: loop((4, 6), kv_grads))
    do.value_1(lambda: loop((6, 8), kv_grads))
    do.key_0(lambda: loop((0, 2), kv_grads))
    do.key_1(lambda: loop((2, 4), kv_grads))

    def media_copy(h):
        return pltpu.make_async_copy(R.MG, R.to_media.at[pl.ds(h * 2, 2)], R.local.at[9])

    def media_grads(h, carry):
        span = pl.ds(h * 2, 2)
        weight = R.G[:, :, :, :, cols(KV)].reshape(1024, 1024)
        upstream = mm_nt(R.gP[span].reshape(2 * rows, 1024), weight).reshape(2, rows, 1024)
        R.U[pl.ds(h * 2 * per_lat, 2 * per_lat)] = upstream[:, per_media:rows, :].reshape(2 * per_lat, 1024)
        upstream = upstream[:, 0:per_media, :]
        rstd = R.MR[span, 0:per_media, 1:2]
        normed = (R.MED[span].astype(F32) - R.MR[span, 0:per_media, 0:1]) * rstd
        made = norm_back(upstream, normed, rstd, R.VV[0:1, :]).astype(R.MG.dtype)
        pl.when(h >= 1)(lambda: media_copy(h - 1).wait())
        R.MG[...] = made
        media_copy(h).start()
        R.GS[0:1, :] += jnp.sum(flat(upstream * normed), axis=0, keepdims=True)
        R.GS[1:2, :] += jnp.sum(flat(upstream), axis=0, keepdims=True)
        return carry

    for k in range(4):
        getattr(do, "media_%d" % k)(lambda k=k: loop((k, k + 1), media_grads))

    @do.gq_in
    def _():
        for h in range(2):
            R.GQ[halves[h], :] = sums[h].total().astype(BF16)
        latent_low = flat(R.X[:, per_media:rows, :])
        R.gA[:, :, :, :, cols(QU)] = mm_tn(latent_low, R.GQ[...]).astype(BF16).reshape(4, 4, 2, 32, 512)

    def latent_terms():
        rstd = flat(R.MR[:, per_media:rows, 1:2])
        return (flat(R.latents[...]).astype(F32) - flat(R.MR[:, per_media:rows, 0:1])) * rstd, rstd

    @do.norms
    def _():
        R.U[...] += mm_nt(R.GQ[...], R.G[:, :, :, :, cols(QU)].reshape(1024, 512))
        normed, _ = latent_terms()
        R.GS[2:3, :] = jnp.sum(R.U[...] * normed, axis=0, keepdims=True)
        R.GS[3:4, :] = jnp.sum(R.U[...], axis=0, keepdims=True)
        for i in range(8):
            piece = R.GS[:, 128 * i : 128 * i + 128].astype(BF16)
            for p in (2 * (i % 2), 2 * (i % 2) + 1):
                for c in range(2):
                    R.gA[i // 2, p, c, 0:16, cols(GN)] = piece

    results = [
        pltpu.make_async_copy(src, dst, R.local.at[10 + k])
        for k, (src, dst) in enumerate(
            (
                (R.latents_out, R.to_out),
                (R.grad_latents, R.to_latents),
                (R.grad_down, R.to_down),
                (R.grad_up, R.to_up),
                (R.grad_pack, R.to_pack),
            )
        )
    ]

    @do.grad_latents
    def _():
        normed, rstd = latent_terms()
        R.grad_latents[...] = (R.GR[...] + norm_back(R.U[...], normed, rstd, R.VV[2:3, :])).reshape(
            images, per_lat, 1024
        )
        results[1].start()

    do.sum_d(lambda: gd_z.total(R.grad_down), results[2].start)
    post.spare = [m.key for m in up]
    back_up = [
        post.msg(R.SU.at[there], R.AU.at[at.p], dev, R.AU.at[there])
        for there, dev in ((at.px, at.xn), (at.py, at.yn), (at.pd, at.diag))
    ]

    @do.sum_u
    def _():
        gu_z.total(R.SF)
        R.SU[...] = R.SF[...].astype(BF16)
        R.AU[at.p] = R.SU[at.p]
        for m in back_up:
            m.start()

    @do.up_out
    def _():
        for m in back_up:
            m.arrived()
        for p in range(4):
            for zz in range(4):
                for cc in range(2):
                    R.grad_up[:, 128 * (8 * zz + 2 * p + cc) : 128 * (8 * zz + 2 * p + cc) + 128] = R.AU[
                        p, :, 128 * (2 * zz + cc) : 128 * (2 * zz + cc) + 128
                    ].astype(F32)
        results[3].start()

    @do.out_in
    def _():
        R.latents_out[...] = (R.RES[...] + out.total()).astype(BF16).reshape(images, per_lat, 1024)
        results[0].start()

    names = order(Names())
    assert sorted(names) == sorted(do.made), set(names) ^ set(do.made)
    for name in names:
        with jax.named_scope(name):
            for action in do.made[name]:
                action()
    results[4].start()
    media_copy(images // 2 - 1).wait()
    for c in results:
        c.wait()


def loop(bounds, action):
    first, last = bounds if isinstance(bounds, tuple) else (0, bounds)
    lax.fori_loop(first, last, action, 0)


def place_of(name):
    if name == "bucket":
        return pltpu.SMEM
    return pl.ANY if name.startswith(("in_", "to_")) else pltpu.VMEM


class Refs:
    def __init__(self, names, refs):
        for name, ref in zip(names, refs):
            setattr(self, name, ref)


def build(kernel_body, inputs, outputs, scratch, messages, cid, name):
    in_names = [n for n, _ in inputs]
    out_names = [n for n, _, _ in outputs]
    scratch_names = [n for n, _, _ in scratch]

    def kernel(*refs):
        R = Refs(in_names + out_names + scratch_names, refs)
        at = Place()
        R.local = refs[-3]
        post = Post(refs[-2], refs[-1])
        kernel_body(at, post, R)
        with jax.named_scope('drain'):
            post.drain()
        assert (post.most, post.keys) == messages, (post.most, post.keys)

    specs = [
        pl.BlockSpec(memory_space=place_of(n)) for n in in_names
    ]
    return pl.pallas_call(
        kernel,
        out_shape=[jax.ShapeDtypeStruct(s, d) for _, s, d in outputs],
        in_specs=specs,
        out_specs=[
            pl.BlockSpec(memory_space=place_of(n)) for n, _, _ in outputs
        ],
        scratch_shapes=[pltpu.VMEM(s, d) for _, s, d in scratch]
        + [pltpu.SemaphoreType.DMA((15,))] + [pltpu.SemaphoreType.DMA((n,)) for n in messages],
        compiler_params=pltpu.CompilerParams(
            collective_id=cid, has_side_effects=True, vmem_limit_bytes=62 << 20
        ),
        name=name,
    )(*[v for _, v in inputs])


def layer(media, latents, bucket, cotangent, n0, n1, n2, n3, n4, n5, w_query, w_keyvalue, w_output, w_up, w_down):
    images, per_media, _ = media.shape
    per_lat = latents.shape[1]
    rows = per_media + per_lat
    tokens = images * per_lat
    inputs = [
        ("in_media", media),
        ("in_latents", latents),
        ("in_cotangent", cotangent),
        ("bucket", bucket),
        ("n0", n0),
        ("n1", n1),
        ("n2", n2),
        ("n3", n3),
        ("n4", n4),
        ("n5", n5),
        ("in_query", w_query),
        ("in_keyvalue", w_keyvalue),
        ("in_output", w_output),
        ("in_up", w_up),
        ("in_down", w_down),
    ]
    outputs = [
        ("to_out", (images, per_lat, 1024), BF16),
        ("to_media", (images, per_media, 1024), BF16),
        ("to_latents", (images, per_lat, 1024), F32),
        ("to_pack", (32, WIDE), F32),
        ("to_up", (32, 4096), F32),
        ("to_down", (128, 1024), F32),
    ]
    scratch = [
        ("MED", (images, per_media, 1024), BF16),
        ("X", (images, rows, 1024), BF16),
        ("MR", (images, rows, 2), F32),
        ("PR", (images, rows, 1024), BF16),
        ("S", (2 * images, rows, 256), F32),
        ("PB", (2 * images, rows, 256), BF16),
        ("QA", (4, tokens, 512), BF16),
        ("MX", (tokens, 512), BF16),
        ("RES", (tokens, 1024), F32),
        ("MA", (4, tokens, 1024), BF16),
        ("CA", (4, tokens, 1024), BF16),
        ("UD", (4, 2, 128, 1024), BF16),
        ("UU", (4, 4, 2, 32, 1024), BF16),
        ("G", (4, 4, 2, 32, WIDE), BF16),
        ("VV", (16, 1024), F32),
        ("WS", (4, 32, 1024), BF16),
        ("LS", (4, 2 * images, 256), F32),
        ("LG", (2 * images, 256), F32),
        ("OP", (4, tokens, 512), BF16),
        ("O1", (2, tokens, 512), BF16),
        ("O2", (tokens, 512), BF16),
        ("MG", (2, per_media, 1024), BF16),
        ("RN", (tokens, 2), F32),
        ("latents", (images, per_lat, 1024), BF16),
        ("cotangent", (images, per_lat, 1024), BF16),
        ("w_up", (32, 4096), BF16),
        ("latents_out", (images, per_lat, 1024), BF16),
        ("grad_latents", (images, per_lat, 1024), F32),
        ("grad_pack", (32, WIDE), F32),
        ("grad_up", (32, 4096), F32),
        ("grad_down", (128, 1024), F32),
        ("ACT", (4, tokens, 1024), BF16),
        ("GG", (4, tokens, 1024), BF16),
        ("PT", (4, tokens, 1024), BF16),
        ("PY", (2, tokens // 2, 1024), BF16),
        ("PX", (2, tokens // 2, 1024), BF16),
        ("P2", (2, tokens // 2, 1024), BF16),
        ("OX", (2, tokens, 1024), BF16),
        ("OY", (tokens, 1024), BF16),
        ("gD", (4, 2, 128, 1024), BF16),
        ("gU", (4, 4, 2, 32, 1024), BF16),
        ("RD", (4, 128, 1024), BF16),
        ("RU", (4, 4, 32, 1024), BF16),
        ("ZD", (4, 128, 1024), BF16),
        ("ZU", (4, 4, 32, 1024), BF16),
        ("U", (tokens, 1024), F32),
        ("GR", (tokens, 1024), F32),
        ("GS", (16, 1024), F32),
        ("GM", (4, tokens, 512), BF16),
        ("gP", (images, rows, 1024), BF16),
        ("DL", (4, 2 * images, 256), F32),
        ("QP", (4, tokens, 512), BF16),
        ("Q1", (2, tokens, 512), BF16),
        ("Q2", (tokens, 512), BF16),
        ("GQ", (tokens, 512), BF16),
        ("gA", (4, 4, 2, 32, NARROW), BF16),
        ("RA", (4, 4, 32, NARROW), BF16),
        ("RK", (4, 4, 32, 1024), BF16),
        ("WY", (2, 4, 16, WIDE), BF16),
        ("WX", (2, 4, 16, WIDE), BF16),
        ("W2", (2, 4, 16, WIDE), BF16),
        ("ZW", (3, 32, WIDE), BF16),
        ("SF", (4, 32, 1024), F32),
        ("SU", (4, 32, 1024), BF16),
        ("AU", (4, 32, 1024), BF16),
    ]
    return build(kernel_body, inputs, outputs, scratch, MESSAGES, 1, "resampler")


def finish_body(
    out_in, media_in, latents_in, pack, up_in, down_in, out, media, latents, n0, n1, n2, n3, n4, n5, wq, wkv, wo, wu, wd
):
    rows = wo.shape[0]
    media[...] = media_in[...].astype(F32)

    @pl.when(pl.program_id(0) == 0)
    def _():
        out[...] = out_in[...]
        latents[...] = latents_in[...]
        wu[...] = up_in[...]
        wd[...] = down_in[...]
        wq[...] = pack[:, cols(QU)]
        wkv[...] = pack[:, cols(KV)]
        wo[:, 0:512] = pack[0:rows, cols(OUT)]
        wo[:, 512:1024] = pack[rows : 2 * rows, cols(OUT)]
        mine = pltpu.roll(pack[0:8, cols(GN)], lax.rem(128 - 32 * lax.axis_index("lat"), 128), 1)
        for k, ref in enumerate((n0, n1, n2, n3, n4, n5)):
            ref[...] = mine[k, 0:32]


def finish(latents_out, grad_media, grad_latents, grad_pack, grad_up, grad_down):
    images, per_media, width = grad_media.shape
    block = pl.BlockSpec((images // 2, per_media, width), lambda g: (g, 0, 0))

    def whole(shape):
        return pl.BlockSpec(shape, lambda g: (0,) * len(shape))

    shapes = [
        jax.ShapeDtypeStruct(latents_out.shape, BF16),
        jax.ShapeDtypeStruct(grad_media.shape, F32),
        jax.ShapeDtypeStruct(grad_latents.shape, F32),
    ] + [
        jax.ShapeDtypeStruct(shape, F32)
        for shape in ((32,),) * 6 + ((32, 512), (32, 1024), (16, 1024), grad_up.shape, grad_down.shape)
    ]
    values = (latents_out, grad_media, grad_latents, grad_pack, grad_up, grad_down)
    return pl.pallas_call(
        finish_body,
        grid=(2,),
        out_shape=shapes,
        in_specs=[block if k == 1 else whole(v.shape) for k, v in enumerate(values)],
        out_specs=[block if k == 1 else whole(v.shape) for k, v in enumerate(shapes)],
        compiler_params=pltpu.CompilerParams(vmem_limit_bytes=60 << 20),
        name="finish",
    )(*values)


def solution(mesh):
    sizes = dict(mesh.shape)
    blocks = sizes["img"] // BLOCK
    names = ("img", "lat")

    def block_shard(weight):
        if blocks == 1:
            return weight
        whole = lax.all_gather(weight, names, axis=0, tiled=True)
        each = whole.shape[0] // (BLOCK * sizes["lat"])
        mine = lax.rem(lax.axis_index("img"), BLOCK) * sizes["lat"] + lax.axis_index("lat")
        return lax.dynamic_slice_in_dim(whole, mine * each, each, 0)

    def own_shard(gradient):
        if blocks == 1:
            return gradient
        each = gradient.shape[0]
        mine = lax.rem(lax.axis_index("img"), BLOCK) * sizes["lat"] + lax.axis_index("lat")
        whole = jnp.zeros((each * BLOCK * sizes["lat"],) + gradient.shape[1:], gradient.dtype)
        whole = lax.dynamic_update_slice_in_dim(whole, gradient, mine * each, 0)
        return lax.psum_scatter(whole, names, scatter_dimension=0, tiled=True)

    def on_device(
        media,
        latents,
        bucket,
        gain_media,
        shift_media,
        gain_latent,
        shift_latent,
        gain_mlp,
        shift_mlp,
        w_query,
        w_keyvalue,
        w_output,
        w_up,
        w_down,
        cotangent,
    ):
        norms = (gain_media, shift_media, gain_latent, shift_latent, gain_mlp, shift_mlp)
        weights = (w_query, w_keyvalue, w_output, w_up, w_down)
        made = layer(media, latents, bucket, cotangent, *[block_shard(v) for v in norms + weights])
        made = finish(*made)
        return (*made[:3], *[own_shard(v) for v in made[3:]])

    rows = P("img", "lat", None)
    shard = P(names)
    wide = P(names, None)
    return jax.shard_map(
        on_device,
        mesh=mesh,
        in_specs=(rows, rows, P("img")) + (shard,) * 6 + (wide,) * 5 + (rows,),
        out_specs=(rows, rows, rows) + (shard,) * 6 + (wide,) * 5,
        check_vma=False,
    )
```

time: 134 us -> 127 us (0.948)
  Pallas kernels: 133 us -> 126 us
    pallas_call x1, Pallas kernels: 128 us -> 121 us  [build(): pl.pallas_call(kernel, out_shape=[jax.ShapeDtypeStruct(s, d) for _, s, d...]
where the time goes in v4:
time: 127 us; the launch traced here: 126 us
  Pallas kernels  126 us (99%)
    pallas_call x1, Pallas kernels, build(): pl.pallas_call(kernel, out_shape=[jax.ShapeDtypeStruct(s, d) for _, s, d...  121 us
    pallas_call x1, Pallas kernels, finish(): pl.pallas_call(finish_body, grid=(2,), out_shape=shapes, in_specs=[block...  5.14 us

profile of v4, /device:TPU:0, one launch (start us, length us, event | category | flops | bytes accessed | tf_op | source)
XLA Modules:
  0.0 126.5 jit_solution(18199460240931390884)
XLA Ops:
  0.7 120.5 %resampler.1 = (bf16[8,16,1024]{2,1,0:T(8,128)(2,1)}, bf16[8,144,1024]{2,1,0:T(8,128)(2,1)}, f32[8,16,1024]{2,1,0:T(8,128)}, f32[32,2176]{1,0:T(8,128)}, f32[32,4096]{1,0:T(8,128)}, /*index=5*/f32[128,1024]{1,0:T(8,128)}) custom-call(bf16[8,144,1024]{2,1,0:T(8,128)(2,1)} %refs_0_.1, bf16[8,16,1024]{2,1,0:T(8,128)(2,1)} %refs_1_.1, ...), custom_call_target="tpu_custom_call" | custom-call | tf_op jit(solution)/shard_map/resampler/pallas_call | solution.py:1318
  121.2 5.1 %finish.1 = (bf16[8,16,1024]{2,1,0:T(8,128)(2,1)}, f32[8,144,1024]{2,1,0:T(8,128)}, f32[8,16,1024]{2,1,0:T(8,128)}, f32[32]{0:T(128)}, f32[32]{0:T(128)}, /*inde...) custom-call(bf16[8,16,1024]{2,1,0:T(8,128)(2,1)} %get-tuple-element., ...), custom_call_target="tpu_custom_call" | custom-call | tf_op jit(solution)/shard_map/finish/pallas_call | solution.py:1471

commit v5 on v4

--- a/solution.py
+++ b/solution.py
@@ -692,24 +692,24 @@
 
 def order(s):
     return (
-        s.load, s.greet, s.staged, s.first_z, s.first_0, s.keys_0, s.cot_a, s.up_a, s.stats, s.keys_z, s.first_1,
-        s.first_2, s.first_3, s.second_z, s.first_r0, s.first_r1, s.first_r2, s.first_r3, s.keys_1, s.keys_2,
-        s.keys_3, s.third_z, s.first_c0, s.first_c1, s.first_c2, s.first_c3, s.down_a, s.up_in, s.up_z, s.keys_r0,
-        s.keys_r1, s.keys_r2, s.keys_r3, s.first_in, s.query, s.q_a, s.second_in, s.second_a, s.keys_c0, s.keys_c1,
+        s.load, s.greet, s.staged, s.first_z, s.first_0, s.keys_0, s.up_a, s.stats, s.keys_z, s.first_1, s.first_2,
+        s.first_3, s.second_z, s.first_r0, s.first_r1, s.first_r2, s.first_r3, s.keys_1, s.keys_2, s.keys_3,
+        s.third_z, s.first_c0, s.first_c1, s.first_c2, s.first_c3, s.down_a, s.up_in, s.up_z, s.keys_r0, s.keys_r1,
+        s.keys_r2, s.keys_r3, s.cot_a, s.first_in, s.query, s.q_a, s.second_in, s.second_a, s.keys_c0, s.keys_c1,
         s.keys_c2, s.keys_c3, s.low, s.second_b, s.keys_in, s.pairs_k, s.q_b, s.second_r, s.q_in, s.down_far,
-        s.up_far, s.third_in, s.third_a, s.third_b, s.cot_b, s.score_0, s.ls_0, s.cot_r, s.score_1, s.ls_1,
-        s.second_c, s.third_r, s.second_done, s.pairs_v, s.ls_in0, s.mix_0, s.mixed_a0, s.ls_in1, s.mix_1,
-        s.mixed_a1, s.mixed_b0, s.mixed_b1, s.third_c, s.third_done, s.mixed_in0, s.mixed_in1, s.resid, s.mlp_a,
-        s.mlp_b, s.mlp_r0, s.mlp_r1, s.cot_in, s.down_early, s.up_early, s.down_last, s.up_mid, s.down_done,
-        s.cot_back, s.up_end, s.up_done, s.mlp_in0, s.gates_0, s.parts_0, s.recycle, s.back_a0, s.mlp_in1, s.gates_1,
+        s.up_far, s.third_in, s.score_0, s.ls_0, s.cot_r, s.score_1, s.ls_1, s.second_c, s.third_a, s.third_b,
+        s.second_done, s.pairs_v, s.ls_in0, s.cot_b, s.mix_0, s.third_r, s.mixed_a0, s.ls_in1, s.mix_1, s.mixed_a1,
+        s.mixed_b0, s.mixed_b1, s.third_c, s.third_done, s.mixed_in0, s.mixed_in1, s.resid, s.mlp_a, s.mlp_b,
+        s.mlp_r0, s.mlp_r1, s.cot_in, s.down_early, s.up_early, s.down_last, s.up_mid, s.up_end, s.down_done,
+        s.cot_back, s.up_done, s.mlp_in0, s.mlp_in1, s.gates_0, s.gates_1, s.parts_0, s.recycle, s.back_a0,
         s.parts_1, s.back_a1, s.grad_d3, s.grad_u3, s.grad_d2, s.add_d3, s.grad_u2, s.add_u3, s.back_r0, s.grad_d1,
         s.grad_d0, s.back_r1, s.add_d2, s.add_u2, s.grad_u1, s.grad_u0, s.add_d1, s.add_d0, s.out_parts, s.add_u1,
         s.add_u0, s.back_in0, s.norm_0, s.gm_a0, s.back_in1, s.norm_1, s.gm_a1, s.out_a, s.w_out, s.out_core,
         s.gm_b0, s.gm_in0, s.gm_b1, s.probs_0, s.dl_0, s.gm_in1, s.probs_1, s.dl_1, s.value_0, s.dl_in0, s.out_plane,
         s.scores_0, s.gq_a0, s.dl_in1, s.scores_1, s.gq_a1, s.value_1, s.value_core, s.far_d, s.far_u, s.gq_b0,
-        s.gq_b1, s.key_0, s.value_plane, s.out_relay, s.key_1, s.key_core, s.key_plane, s.media_0, s.media_1,
-        s.value_relay, s.media_2, s.out_r, s.media_3, s.gq_in, s.query_core, s.norms, s.norms_core, s.key_relay,
-        s.out_z, s.value_z, s.grad_latents, s.norms_plane, s.query_plane, s.key_z, s.query_relay, s.out_b, s.sum_d,
+        s.gq_b1, s.key_0, s.value_plane, s.out_relay, s.key_1, s.key_core, s.key_plane, s.media_0, s.value_relay,
+        s.media_1, s.key_relay, s.media_2, s.out_r, s.gq_in, s.query_core, s.media_3, s.norms, s.norms_core,
+        s.query_plane, s.out_z, s.value_z, s.grad_latents, s.norms_plane, s.key_z, s.query_relay, s.out_b, s.sum_d,
         s.sum_u, s.norms_z, s.query_z, s.out_sum, s.value_sum, s.key_sum, s.norms_sum, s.up_out, s.out_in,
         s.query_sum,
     )
@@ -981,12 +981,12 @@
 
         def gates(f, carry):
             weight = R.UU[:, :, :, :, span256(f)].reshape(1024, 256)
-            gate = mm(R.MA[:, part, :].reshape(4 * half_rows, 1024), weight)
-            back = R.S[pl.ds(4 * f, 4), part, :].reshape(4 * half_rows, 256)
+            gate = mm(R.MA[...].reshape(4 * tokens, 1024), weight)
+            back = R.S[pl.ds(4 * f, 4), 0:tokens, :].reshape(4 * tokens, 256)
             phi = 0.5 * (1.0 + lax.erf(gate * 0.7071067811865476))
-            R.ACT[:, part, span256(f)] = (gate * phi).astype(BF16).reshape(4, half_rows, 256)
+            R.ACT[:, :, span256(f)] = (gate * phi).astype(BF16).reshape(4, tokens, 256)
             slope = phi + gate * jnp.exp(-0.5 * gate * gate) * 0.3989422804014327
-            R.GG[:, part, span256(f)] = (back * slope).astype(BF16).reshape(4, half_rows, 256)
+            R.GG[:, :, span256(f)] = (back * slope).astype(BF16).reshape(4, tokens, 256)
             return carry
 
         loop(4, gates)
@@ -1003,7 +1003,7 @@
 
     post.spare = [m.key for w in (second, third) for m in (w.one, w.two, w.on)]
     for h in range(2):
-        getattr(do, "gates_%d" % h)(lambda h=h: gates(h))
+        getattr(do, "gates_%d" % h)(*([lambda h=h: gates(h)] if h == 0 else []))
         getattr(do, "parts_%d" % h)(lambda h=h: norm_parts(h))
         back = HalfReduce(
             post, at, h, lambda x, y, h=h: R.PT.at[x * 2 + y, halves[h]], R.PY.at[h], R.PX.at[h], R.P2.at[h]

time: 127 us -> 123 us (0.969)
  Pallas kernels: 126 us -> 122 us
    pallas_call x1, Pallas kernels: 121 us -> 117 us  [build(): pl.pallas_call(kernel, out_shape=[jax.ShapeDtypeStruct(s, d) for _, s, d...]
where the time goes in v5:
time: 123 us
  Pallas kernels  122 us (99%)
    pallas_call x1, Pallas kernels, build(): pl.pallas_call(kernel, out_shape=[jax.ShapeDtypeStruct(s, d) for _, s, d...  117 us
    pallas_call x1, Pallas kernels, finish(): pl.pallas_call(finish_body, grid=(2,), out_shape=shapes, in_specs=[block...  5.14 us

profile of v5, /device:TPU:0, one launch (start us, length us, event | category | flops | bytes accessed | tf_op | source)
XLA Modules:
  0.0 122.7 jit_solution(4928635475426872184)
XLA Ops:
  0.7 116.8 %resampler.1 = (bf16[8,16,1024]{2,1,0:T(8,128)(2,1)}, bf16[8,144,1024]{2,1,0:T(8,128)(2,1)}, f32[8,16,1024]{2,1,0:T(8,128)}, f32[32,2176]{1,0:T(8,128)}, f32[32,4096]{1,0:T(8,128)}, /*index=5*/f32[128,1024]{1,0:T(8,128)}) custom-call(bf16[8,144,1024]{2,1,0:T(8,128)(2,1)} %refs_0_.1, bf16[8,16,1024]{2,1,0:T(8,128)(2,1)} %refs_1_.1, ...), custom_call_target="tpu_custom_call" | custom-call | tf_op jit(solution)/shard_map/resampler/pallas_call | solution.py:1318
  117.4 5.1 %finish.1 = (bf16[8,16,1024]{2,1,0:T(8,128)(2,1)}, f32[8,144,1024]{2,1,0:T(8,128)}, f32[8,16,1024]{2,1,0:T(8,128)}, f32[32]{0:T(128)}, f32[32]{0:T(128)}, /*inde...) custom-call(bf16[8,16,1024]{2,1,0:T(8,128)(2,1)} %get-tuple-element., ...), custom_call_target="tpu_custom_call" | custom-call | tf_op jit(solution)/shard_map/finish/pallas_call | solution.py:1471

commit v6 on v5

--- a/solution.py
+++ b/solution.py
@@ -693,11 +693,11 @@
 def order(s):
     return (
         s.load, s.greet, s.staged, s.first_z, s.first_0, s.keys_0, s.up_a, s.stats, s.keys_z, s.first_1, s.first_2,
-        s.first_3, s.second_z, s.first_r0, s.first_r1, s.first_r2, s.first_r3, s.keys_1, s.keys_2, s.keys_3,
-        s.third_z, s.first_c0, s.first_c1, s.first_c2, s.first_c3, s.down_a, s.up_in, s.up_z, s.keys_r0, s.keys_r1,
+        s.first_3, s.second_z, s.first_r0, s.first_r1, s.first_r2, s.first_r3, s.keys_1, s.keys_2, s.third_z,
+        s.keys_3, s.first_c0, s.first_c1, s.first_c2, s.first_c3, s.down_a, s.up_in, s.up_z, s.keys_r0, s.keys_r1,
         s.keys_r2, s.keys_r3, s.cot_a, s.first_in, s.query, s.q_a, s.second_in, s.second_a, s.keys_c0, s.keys_c1,
         s.keys_c2, s.keys_c3, s.low, s.second_b, s.keys_in, s.pairs_k, s.q_b, s.second_r, s.q_in, s.down_far,
-        s.up_far, s.third_in, s.score_0, s.ls_0, s.cot_r, s.score_1, s.ls_1, s.second_c, s.third_a, s.third_b,
+        s.up_far, s.score_0, s.ls_0, s.cot_r, s.score_1, s.ls_1, s.second_c, s.third_in, s.third_a, s.third_b,
         s.second_done, s.pairs_v, s.ls_in0, s.cot_b, s.mix_0, s.third_r, s.mixed_a0, s.ls_in1, s.mix_1, s.mixed_a1,
         s.mixed_b0, s.mixed_b1, s.third_c, s.third_done, s.mixed_in0, s.mixed_in1, s.resid, s.mlp_a, s.mlp_b,
         s.mlp_r0, s.mlp_r1, s.cot_in, s.down_early, s.up_early, s.down_last, s.up_mid, s.up_end, s.down_done,
@@ -708,7 +708,7 @@
         s.gm_b0, s.gm_in0, s.gm_b1, s.probs_0, s.dl_0, s.gm_in1, s.probs_1, s.dl_1, s.value_0, s.dl_in0, s.out_plane,
         s.scores_0, s.gq_a0, s.dl_in1, s.scores_1, s.gq_a1, s.value_1, s.value_core, s.far_d, s.far_u, s.gq_b0,
         s.gq_b1, s.key_0, s.value_plane, s.out_relay, s.key_1, s.key_core, s.key_plane, s.media_0, s.value_relay,
-        s.media_1, s.key_relay, s.media_2, s.out_r, s.gq_in, s.query_core, s.media_3, s.norms, s.norms_core,
+        s.media_1, s.media_2, s.key_relay, s.out_r, s.gq_in, s.query_core, s.media_3, s.norms, s.norms_core,
         s.query_plane, s.out_z, s.value_z, s.grad_latents, s.norms_plane, s.key_z, s.query_relay, s.out_b, s.sum_d,
         s.sum_u, s.norms_z, s.query_z, s.out_sum, s.value_sum, s.key_sum, s.norms_sum, s.up_out, s.out_in,
         s.query_sum,

time: 123 us -> 122 us (level)
  no operation moved by 1% of the time
where the time goes in v6:
time: 122 us
  Pallas kernels  121 us (99%)
    pallas_call x1, Pallas kernels, build(): pl.pallas_call(kernel, out_shape=[jax.ShapeDtypeStruct(s, d) for _, s, d...  116 us
    pallas_call x1, Pallas kernels, finish(): pl.pallas_call(finish_body, grid=(2,), out_shape=shapes, in_specs=[block...  5.14 us

profile of v6, /device:TPU:0, one launch (start us, length us, event | category | flops | bytes accessed | tf_op | source)
XLA Modules:
  0.0 121.8 jit_solution(12723170669313857326)
XLA Ops:
  0.7 115.8 %resampler.1 = (bf16[8,16,1024]{2,1,0:T(8,128)(2,1)}, bf16[8,144,1024]{2,1,0:T(8,128)(2,1)}, f32[8,16,1024]{2,1,0:T(8,128)}, f32[32,2176]{1,0:T(8,128)}, f32[32,4096]{1,0:T(8,128)}, /*index=5*/f32[128,1024]{1,0:T(8,128)}) custom-call(bf16[8,144,1024]{2,1,0:T(8,128)(2,1)} %refs_0_.1, bf16[8,16,1024]{2,1,0:T(8,128)(2,1)} %refs_1_.1, ...), custom_call_target="tpu_custom_call" | custom-call | tf_op jit(solution)/shard_map/resampler/pallas_call | solution.py:1318
  116.5 5.1 %finish.1 = (bf16[8,16,1024]{2,1,0:T(8,128)(2,1)}, f32[8,144,1024]{2,1,0:T(8,128)}, f32[8,16,1024]{2,1,0:T(8,128)}, f32[32]{0:T(128)}, f32[32]{0:T(128)}, /*inde...) custom-call(bf16[8,16,1024]{2,1,0:T(8,128)(2,1)} %get-tuple-element., ...), custom_call_target="tpu_custom_call" | custom-call | tf_op jit(solution)/shard_map/finish/pallas_call | solution.py:1471
